TPU v7x, 32 devices: a whole 2x2x4 slice. The times are simulated.
32 devices in a mesh: slot: 2 (over x), tile: 16 (over z, y, core).
Axes of the slice: x: 2, y: 2, z: 4, core: 2. Of those that a mesh axis runs over, the one named last changes fastest.
Arguments:
- control: float32 [2, 4, 2, 256, 512], P('slot', None, None, 'tile'), may hold values from -28 to 28
- background: bfloat16 [4, 2, 256, 512], P(None, None, 'tile'), may hold values from -6 to 6
- self_weight: bfloat16 [512, 512], replicated, may hold values from -0.25 to 0.25
- neighbour_weight: bfloat16 [512, 512], replicated, may hold values from -0.25 to 0.25
- output_weight: bfloat16 [512, 512], replicated, may hold values from -0.25 to 0.25
- norm_gain: float32 [512], replicated, may hold values from 0.1 to 1.9
- readout: bfloat16 [512, 128], replicated, may hold values from -0.25 to 0.25
- error_weight: float32 [512], replicated, may hold values from 0.3 to 3
- report_owner: int32 [2, 2, 512, 1], P('slot', None, 'tile'), may hold values from 0 to 15, as said below
- report_stencil: int32 [2, 2, 512, 4], P('slot', None, 'tile'), may hold values from 0 to 31
- report_weights: bfloat16 [2, 2, 512, 4], P('slot', None, 'tile'), may hold values from 0.049804688 to 1
- report_values: bfloat16 [2, 2, 512, 128], P('slot', None, 'tile'), may hold values from -6 to 6
- report_precision: bfloat16 [2, 2, 512], P('slot', None, 'tile'), may hold values from 0.049804688 to 0.5
Outputs:
- gradient: float32 [2, 4, 2, 256, 512], P('slot', None, None, 'tile')
Inputs may be any that keep to these rules, and one draw needn't show every extreme that they name: `report_owner`: within the rows of one device for one slot and step (aligned blocks of 32 rows) no owner tile is named more than 5 times; in every slot and step one owner tile is named exactly 5 times by every device of the slot. `report_stencil`: A cell of the owner tile, numbered latitude row * 16 + column within the tile.
All inputs are finite; a program needn't handle non-finite values.
Results may differ from a plain program's by a relative error of at most 0.006.
Values may be sent and summed in bfloat16 or wider, within the bound.
No kernel may reach another device: no remote copies, remote signals or barrier semaphores. Data moves between devices by JAX's collectives and lax.ppermute only.
A program may use at most 64 MiB of HBM per device.

v0:
```python
import functools
import jax
import jax.numpy as jnp
from jax import lax
from jax.experimental import pallas as pl
from jax.experimental.pallas import tpu as pltpu
from jax.sharding import PartitionSpec as P

EPSILON = 1e-06
F32 = jnp.float32
BF16 = jnp.bfloat16
LANES = 128
CAP = 5
SLOTS = 4 * CAP
CHUNK = 32
META = 16
SENDERS = LANES // SLOTS
WIDE = 40
SLIM = 24
VMEM_LIMIT = 28 * 1024 * 1024


def dot(a, b):
    return jnp.dot(a, b, preferred_element_type=F32)


def dot_t(a, b):
    return lax.dot_general(a, b, (((1,), (1,)), ((), ())), preferred_element_type=F32)


def sublane(shape):
    return lax.broadcasted_iota(jnp.int32, shape, 0)


def inverse_rms(x):
    return lax.rsqrt(jnp.mean(x * x, axis=-1, keepdims=True) + EPSILON)


def sigmoid(p):
    return 0.5 * jnp.tanh(0.5 * p) + 0.5


def neighbours(rows):
    width = rows[0].shape[0]
    return [
        0.25 * (rows[1 - i] + pltpu.roll(rows[i], 1, 0) + pltpu.roll(rows[i], width - 1, 0))
        for i in range(2)
    ]


def forward_step(u, n, mean, act, pre, d, gain, ws, wn, wo, width, members, out, copies=()):
    both = 2 * width
    for m in range(members):
        base = m * both
        rows = []
        for lat in range(2):
            x = u[base + lat * width : base + (lat + 1) * width]
            rows.append((x * inverse_rms(x) * gain).astype(BF16).astype(F32))
        n[base : base + both] = jnp.concatenate(rows, axis=0).astype(BF16)
        mean[base : base + both] = jnp.concatenate(neighbours(rows), axis=0).astype(BF16)
    for copy in copies[:2]:
        copy.wait()
    pre[...] = dot(n[...], ws[...]) + dot(mean[...], wn[...])
    for m in range(members):
        base = m * both
        p = pre[base : base + both]
        sig = sigmoid(p)
        act[base : base + both] = (p * sig).astype(BF16)
        if d is not None:
            pre[base : base + both] = sig * (1.0 + p * (1.0 - sig))
    if d is not None:
        for m in range(members):
            slim_copy(d, pre, m)
    for copy in copies[2:]:
        copy.wait()
    pre[...] = dot(act[...], wo[...])
    for r in range(2 * members):
        out(r, u[r * width : (r + 1) * width] + pre[r * width : (r + 1) * width])


def slim_edge(wide, r):
    low = wide[r * WIDE + 16 : r * WIDE + 24]
    high = wide[r * WIDE + 32 : r * WIDE + 40]
    return jnp.where(sublane(low.shape) < 4, low, high)


def slim_copy(to, wide, m):
    parts = []
    for r in (2 * m, 2 * m + 1):
        parts += [wide[r * WIDE : r * WIDE + 16], slim_edge(wide, r)]
    both = jnp.concatenate(parts, axis=0)
    to[m * 2 * SLIM : (m + 1) * 2 * SLIM] = both.astype(to.dtype)


def reports(arrays, out_hbm, key, meta, picked, out, sem):
    pack(*arrays, out, key, meta, picked)
    store = pltpu.make_async_copy(out, out_hbm, sem)
    store.start()
    store.wait()


def early():
    return lax.axis_index("tile") < lax.axis_size("tile") // 2


def first_kernel(control_hbm, *refs):
    sources, (held, out_hbm), arrays, (key, meta, picked, out, sems) = refs[:5], refs[5:7], refs[7:12], refs[12:]
    copies = [
        pltpu.make_async_copy(source, to, sems.at[i]) for i, (source, to) in enumerate(zip(sources, arrays))
    ]
    copies.append(pltpu.make_async_copy(control_hbm, held, sems.at[5]))
    for copy in copies:
        copy.start()
    for copy in copies[:5]:
        copy.wait()

    @pl.when(early())
    def _():
        reports(arrays, out_hbm, key, meta, picked, out, sems.at[6])

    copies[5].wait()


def later_kernel(packed_hbm, *refs):
    arrays, out_hbm, (key, meta, picked, out, sem) = refs[:5], refs[6], refs[7:]

    @pl.when(jnp.logical_not(early()))
    def _():
        reports(arrays, out_hbm, key, meta, picked, out, sem)


def pack(owner, stencil, weights, precision, values, out, key, meta, picked):
    steps, _, rows = owner.shape
    tiles = out.shape[0] // CHUNK
    total = steps * rows
    place = lax.axis_index("tile") % SENDERS * SLOTS
    earlier = lax.broadcasted_iota(jnp.int32, (rows, rows), 0) < lax.broadcasted_iota(jnp.int32, (rows, rows), 1)
    earlier = earlier.astype(F32).astype(BF16)
    meta[...] = jnp.zeros_like(meta)
    for k in range(steps):
        at = slice(k * rows, (k + 1) * rows)
        named = lax.broadcasted_iota(jnp.int32, (tiles, rows), 0) == owner[k]
        hits = named.astype(F32)
        before = dot(hits.astype(BF16), earlier)
        rank = jnp.sum(hits * before, axis=0, keepdims=True).astype(jnp.int32)
        key[0:1, at] = owner[k] * (2 * CAP) + k * CAP + rank
        meta[4:8, at] = stencil[k].astype(F32)
        meta[8:12, at] = weights[k].astype(F32)
        meta[12:13, at] = precision[k : k + 1].astype(F32)
    row = lax.broadcasted_iota(jnp.int32, (tiles * CHUNK, total), 0)
    tile = row // CHUNK
    slot = row % CHUNK
    other = jnp.where(tile % 2 == 0, (tile + tiles - 1) % tiles, (tile + 1) % tiles)
    mine = slot < 2 * CAP
    wanted = jnp.where(mine, tile * (2 * CAP) + slot, other * (2 * CAP) + slot - 2 * CAP)
    wanted = jnp.where(slot < SLOTS, wanted, -1)
    placement = (wanted == key[...]).astype(F32).astype(BF16)
    picked[...] = dot(placement, values[...])
    entries = dot_t(meta[...].astype(BF16), placement)
    lane = lax.broadcasted_iota(jnp.int32, (META, LANES), 1)
    used = jnp.logical_and(lane >= place, lane < place + SLOTS)
    per_tile = LANES // CHUNK
    for t in range(tiles):
        block = entries[:, t // per_tile * LANES : (t // per_tile + 1) * LANES]
        shift = (place + LANES - t % per_tile * CHUNK) % LANES
        block = jnp.where(used, pltpu.roll(block, shift, 1), 0.0)
        low = picked[t * CHUNK + 16 : (t + 1) * CHUNK]
        picked[t * CHUNK + 16 : (t + 1) * CHUNK] = jnp.where(sublane((META, 1)) < 4, low, block)
    out[...] = picked[...].astype(BF16)


def tile_kernel(control, mate, out, held):
    even = lax.rem(lax.axis_index("tile"), 2) == 0
    size = control.shape[0]
    out[0:size] = control[...].astype(BF16)
    for r in range(size // 16):
        held[r * 2 : (r + 1) * 2] = jnp.where(
            even, mate[r * 16 : r * 16 + 2], mate[r * 16 + 14 : (r + 1) * 16]
        )
    out[size:] = held[...].astype(BF16)


def relay_kernel(control, mate, oth, tile, out, near4, wide):
    even = lax.rem(lax.axis_index("tile"), 2) == 0
    size = mate.shape[0]
    tile[...] = control[...]
    wide[...] = oth[0:size].astype(F32)
    for r in range(size // 16):
        a, b = r * 16, (r + 1) * 16
        out[r * 2 : (r + 1) * 2] = jnp.where(even, wide[b - 2 : b], wide[a : a + 2])
        near4[r * 4 : (r + 1) * 4] = jnp.where(even, mate[a : a + 4], mate[b - 4 : b])
        start = size // 8 + r * 2
        out[start : start + 2] = jnp.where(even, mate[a : a + 2], mate[b - 2 : b])


def forward_kernel(
    gain_hbm, ws_hbm, wn_hbm, wo_hbm, readout_hbm, control, mate, oth,
    edge0, u1x, d0x, d1x, f2x, field, final, wo, readout,
    ua, ub, n, mean, act, pre, edge, states, gain, ws, wn, sems,
):
    pairs = ((gain_hbm, gain), (ws_hbm, ws), (wn_hbm, wn), (wo_hbm, wo), (readout_hbm, readout))
    copies = [pltpu.make_async_copy(source, to, sems.at[i]) for i, (source, to) in enumerate(pairs)]
    for copy in copies:
        copy.start()
    members = final.shape[0] // 32
    even = lax.rem(lax.axis_index("tile"), 2) == 0
    tile_at = jnp.where(even, 24, 16)
    edge_at = jnp.where(even, 16, 32)
    far = oth[members * 32 :].astype(F32)
    for r in range(2 * members):
        ua[r * WIDE : r * WIDE + 16] = control[r * 16 : (r + 1) * 16]
        ua[pl.ds(pl.multiple_of(r * WIDE + tile_at, 8), 16)] = oth[r * 16 : (r + 1) * 16].astype(F32)
        near4 = mate[r * 4 : (r + 1) * 4]
        far2 = far[r * 2 : (r + 1) * 2]
        edge[...] = jnp.zeros_like(edge)
        edge[0:4] = near4
        edge[6:8] = far2
        edge[8:10] = far2
        edge[12:16] = near4
        ua[pl.ds(pl.multiple_of(r * WIDE + edge_at, 8), 8)] = jnp.where(even, edge[0:8], edge[8:16])
    for r in range(2 * members):
        edge0[r * 8 : (r + 1) * 8] = slim_edge(ua, r)
    copies[0].wait()
    g = gain[...]

    def keep(ref):
        def store(r, value):
            ref[r * WIDE : (r + 1) * WIDE] = value

        return store

    def keep_states(ref, k):
        own = k * members * 32
        away = (2 + k) * members * 32
        for r in range(2 * members):
            states[own + r * 16 : own + (r + 1) * 16] = ref[r * WIDE : r * WIDE + 16].astype(BF16)
            taken = ref[pl.ds(pl.multiple_of(r * WIDE + tile_at, 8), 16)]
            states[away + r * 16 : away + (r + 1) * 16] = taken.astype(BF16)

    forward_step(ua, n, mean, act, pre, d0x, g, ws, wn, wo, WIDE, members, keep(ub), copies[1:])
    for m in range(members):
        slim_copy(u1x, ub, m)
    keep_states(ub, 0)
    forward_step(ub, n, mean, act, pre, d1x, g, ws, wn, wo, WIDE, members, keep(ua))
    for m in range(members):
        slim_copy(f2x, ua, m)
    keep_states(ua, 1)
    final[...] = states[members * 32 : 2 * members * 32]
    read = dot(states[...], readout[...])
    for q in range(4):
        for m in range(members):
            start = (q * members + m) * 32
            field[q * 32 : (q + 1) * 32, m * LANES : (m + 1) * LANES] = read[start : start + 32]


def split(x):
    high = x.astype(BF16)
    return high, (x - high.astype(F32)).astype(BF16)


def observe_kernel(
    tiles,
    error_hbm, control_hbm, background_hbm, arrived, field,
    spread, message, error, control, background,
    th, tl, ph, plo, vals, wide, sems,
):
    pairs = ((error_hbm, error), (control_hbm, control), (background_hbm, background))
    copies = [pltpu.make_async_copy(source, to, sems.at[i]) for i, (source, to) in enumerate(pairs)]
    for copy in copies:
        copy.start()
    steps = 2
    members = field.shape[1] // LANES
    even = lax.rem(lax.axis_index("tile"), 2) == 0
    cells = sublane((32, LANES)).astype(F32)
    lane = lax.broadcasted_iota(jnp.int32, (1, LANES), 1)
    table_of = jnp.where(lane < SENDERS * SLOTS, lane % SLOTS // CAP, -1)
    wide[...] = arrived[...].astype(F32)
    vals[...] = jnp.zeros_like(vals)
    for p in range(th.shape[1] // LANES):
        meta = jnp.zeros((META, LANES), F32)
        for d in range(p * SENDERS, min((p + 1) * SENDERS, tiles)):
            meta += wide[d * CHUNK + 16 : (d + 1) * CHUNK]
            start = p * LANES + d % SENDERS * SLOTS
            vals[start : start + SLOTS] = wide[d * CHUNK : d * CHUNK + SLOTS]
        weight = jnp.zeros((32, LANES), F32)
        for i in range(4):
            weight += jnp.where(cells == meta[4 + i : 5 + i], meta[8 + i : 9 + i], 0.0)
        scaled = weight * meta[12:13]
        wh, wl = split(weight)
        sh, sl = split(scaled)
        parts = ((th, wh.astype(F32)), (tl, wl.astype(F32)), (ph, sh.astype(F32)), (plo, sl.astype(F32)))
        for q in range(2 * steps):
            hit = table_of == q
            for ref, value in parts:
                kept = jnp.where(hit, value, 0.0).astype(BF16)
                ref[q * 32 : (q + 1) * 32, p * LANES : (p + 1) * LANES] = kept
    cross = dot_t(ph[...], th[...]) + dot_t(plo[...], th[...]) + dot_t(ph[...], tl[...])
    taken = vals[...].astype(BF16)
    target = dot(ph[...], taken) + dot(plo[...], taken)
    ch, cl = split(cross)
    fh, fl = split(field[...])
    mixed = dot(ch, fh) + dot(cl, fh) + dot(ch, fl)
    for q in range(2 * steps):
        for m in range(members):
            start = (q * members + m) * 32
            value = mixed[q * 32 : (q + 1) * 32, m * LANES : (m + 1) * LANES] - target[q * 32 : (q + 1) * 32]
            spread[start : start + 32] = value.astype(BF16)
    size = members * 32
    for k in range(steps):
        for m in range(members):
            start = k * size + m * 32
            pair = spread[start : start + 32].astype(F32)
            near = [jnp.where(even, pair[i + 8 : i + 16], pair[i : i + 8]) for i in (0, 16)]
            start = k * size // 2 + m * 16
            message[start : start + 16] = jnp.concatenate(near, axis=0).astype(BF16)
    for copy in copies:
        copy.wait()


def adjoint_step(u, cot, gb, gm, flat, d, add, out, gain, ws, wn, wo, members):
    both = 2 * SLIM
    gb[...] = cot[...].astype(BF16)
    flat[...] = dot_t(gb[...], wo[...])
    gb[...] = (flat[...] * d[...]).astype(BF16)
    gm[...] = dot_t(gb[...], wn[...])
    flat[...] = dot_t(gb[...], ws[...])
    for m in range(members):
        base = m * both
        rows = []
        for lat in range(2):
            start = base + lat * SLIM
            rows.append(gm[start : start + SLIM].astype(BF16).astype(F32))
        around = neighbours(rows)
        for lat in range(2):
            start = base + lat * SLIM
            x = u[start : start + SLIM]
            s = inverse_rms(x)
            scaled = gain * (flat[start : start + SLIM] + around[lat])
            inner = jnp.mean(x * scaled, axis=-1, keepdims=True)
            value = cot[start : start + SLIM] + s * scaled - x * (s * s * s * inner)
            if add is not None:
                value = value + add[start : start + SLIM]
            out[start : start + SLIM] = value


def edges(nxt, edge, r):
    even = lax.rem(lax.axis_index("tile"), 2) == 0
    far = nxt[r * 2 : (r + 1) * 2]
    start = nxt.shape[0] // 2 + r * 2
    near = nxt[start : start + 2]
    edge[...] = jnp.zeros_like(edge)
    edge[0:2] = near
    edge[6:8] = far
    edge[8:10] = far
    edge[14:16] = near
    return jnp.where(even, edge[0:8], edge[8:16])


def pull_kernel(
    wn_hbm, ws_hbm, gain_hbm, spread, readout,
    last, first, wn, ws, gain,
    pulled, sems,
):
    pairs = ((wn_hbm, wn), (ws_hbm, ws), (gain_hbm, gain))
    copies = [pltpu.make_async_copy(source, to, sems.at[i]) for i, (source, to) in enumerate(pairs)]
    for copy in copies:
        copy.start()
    size = pulled.shape[0] // 4
    even = lax.rem(lax.axis_index("tile"), 2) == 0
    row8 = sublane((8, 1))
    pulled[...] = dot_t(spread[...], readout[...])
    for k, out in enumerate((first, last)):
        for r in range(size // 16):
            start = k * size + r * 16
            out[r * SLIM : r * SLIM + 16] = pulled[start : start + 16]
            start += 2 * size
            low = jnp.where(row8 < 4, pulled[start : start + 8], 0.0)
            high = jnp.where(row8 >= 4, pulled[start + 8 : start + 16], 0.0)
            out[r * SLIM + 16 : (r + 1) * SLIM] = jnp.where(even, high, low)
    for copy in copies:
        copy.wait()


def backward_kernel(
    last, early_pull, wn, ws, gain, control, background, edge0, nxt, nxt_edges, f2x, wo, readout, error, message,
    u1x, d0x, d1x, before,
    result,
    cot2, cot1, add, gb, gm, flat, mate_pull, edge, u0x, final,
):
    size = result.shape[0]
    members = size // 32
    even = lax.rem(lax.axis_index("tile"), 2) == 0
    slot = lax.axis_index("slot")
    first = slot == 0
    weight = jnp.where(slot == lax.axis_size("slot") - 1, 0.0, 1.0) * error[...]
    row8 = sublane((8, 1))
    mate_side = jnp.where(even, 1, 0) == jnp.where(row8 < 4, 1, 0)
    mate_pull[...] = dot_t(message[...], readout[...])
    final[...] = f2x[...].astype(F32)
    add[...] = early_pull[...]
    for r in range(2 * members):
        a, b = r * SLIM, r * SLIM + 16
        cot2[a:b] = last[a:b] - weight * (nxt[r * 16 : (r + 1) * 16] - final[a:b])
        u0x[a:b] = control[r * 16 : (r + 1) * 16]
        a, b = b, b + 8
        start = size // 2 + r * 8
        pulled = last[a:b] + jnp.where(mate_side, mate_pull[start : start + 8], 0.0)
        cot2[a:b] = pulled - weight * (edges(nxt_edges, edge, r) - final[a:b])
        add[a:b] = early_pull[a:b] + jnp.where(mate_side, mate_pull[r * 8 : (r + 1) * 8], 0.0)
        u0x[a:b] = edge0[r * 8 : (r + 1) * 8]
    adjoint_step(u1x, cot2, gb, gm, flat, d1x, add, cot1, gain[...], ws, wn, wo, members)
    adjoint_step(u0x, cot1, gb, gm, flat, d0x, None, cot2, gain[...], ws, wn, wo, members)
    taken = jnp.where(first, background[...].astype(F32), before[...].astype(F32))
    for r in range(2 * members):
        a, b, start = r * 16, (r + 1) * 16, r * SLIM
        result[a:b] = cot2[start : start + 16] + error[...] * (u0x[start : start + 16] - taken[a:b])


def kernel_call(body, outs, scratch, flops, moved, hbm=0, out_places=None, aliases={}):
    def call(*operands):
        fixed = [i in range(hbm) and i not in aliases for i in range(len(operands))]
        operands = [
            pltpu.with_memory_space_constraint(x, pltpu.HBM) if fix else x for x, fix in zip(operands, fixed)
        ]
        places = [pltpu.HBM] * hbm + [pltpu.VMEM] * (len(operands) - hbm)
        given = {} if out_places is None else {"out_specs": [pl.BlockSpec(memory_space=p) for p in out_places]}
        return pl.pallas_call(
            body,
            out_shape=outs,
            in_specs=[pl.BlockSpec(memory_space=place) for place in places],
            **given,
            scratch_shapes=scratch,
            input_output_aliases=aliases,
            compiler_params=pltpu.CompilerParams(vmem_limit_bytes=VMEM_LIMIT),
            cost_estimate=pl.CostEstimate(flops=flops, bytes_accessed=moved, transcendentals=0),
        )(*operands)

    return call


def per_device(
    control,
    background,
    self_weight,
    neighbour_weight,
    output_weight,
    norm_gain,
    readout,
    error_weight,
    report_owner,
    report_stencil,
    report_weights,
    report_values,
    report_precision,
):
    tiles = lax.axis_size("tile")
    slots = lax.axis_size("slot")
    members, lats, cols, channels = control.shape[1:]
    groups = members * lats
    size = groups * cols
    steps = report_owner.shape[1]
    rows = report_owner.shape[2]
    gain = norm_gain.reshape(1, channels)
    error = error_weight.reshape(1, channels)
    flat = control.reshape(size, channels)

    def spec(count, dtype=F32, width=channels):
        return jax.ShapeDtypeStruct((count, width), dtype)

    def scratch(count, dtype=F32, width=channels):
        return pltpu.VMEM((count, width), dtype)

    mate_of = [(i, i ^ 1) for i in range(tiles)]
    other_of = [(i, (i - 1) % tiles if i % 2 == 0 else (i + 1) % tiles) for i in range(tiles)]

    def across(block, shift, route):
        pairs = [
            (((s + shift) % slots) * tiles + i, s * tiles + j)
            for s in range(slots)
            for i, j in route
        ]
        return lax.ppermute(block, ("slot", "tile"), pairs)

    straight = [(i, i) for i in range(tiles)]
    mate = lax.ppermute(flat, "tile", mate_of)
    listed = (
        jnp.transpose(report_owner[0], (0, 2, 1)),
        jnp.transpose(report_stencil[0], (0, 2, 1)),
        jnp.transpose(report_weights[0], (0, 2, 1)),
        report_precision[0],
        report_values[0].reshape(steps * rows, LANES),
    )
    work = [
        pltpu.VMEM((1, steps * rows), jnp.int32),
        scratch(META, F32, steps * rows),
        scratch(tiles * CHUNK, F32, LANES),
        scratch(tiles * CHUNK, BF16, LANES),
    ]
    held, packed, *listed = kernel_call(
        first_kernel,
        [spec(size), spec(tiles * CHUNK, BF16, LANES)]
        + [jax.ShapeDtypeStruct(block.shape, block.dtype) for block in listed],
        work + [pltpu.SemaphoreType.DMA((7,))],
        10**7,
        200000,
        hbm=6,
        out_places=[pltpu.VMEM, pltpu.HBM] + [pltpu.VMEM] * 5,
    )(flat, *listed)
    sent = kernel_call(
        tile_kernel, spec(groups * (cols + 2), BF16), [scratch(groups * 2)], 1000, 400000
    )(held, mate)
    oth = lax.ppermute(sent, "tile", other_of)
    (packed,) = kernel_call(
        later_kernel,
        [spec(tiles * CHUNK, BF16, LANES)],
        work + [pltpu.SemaphoreType.DMA],
        10**7,
        200000,
        hbm=1,
        out_places=[pltpu.HBM],
        aliases={0: 0},
    )(packed, *listed, sent)
    arrived = lax.all_to_all(packed, "tile", split_axis=0, concat_axis=0, tiled=True)

    tile, near2, near4 = kernel_call(
        relay_kernel, [spec(size), spec(4 * groups), spec(4 * groups)], [scratch(size)], 1000, 700000
    )(held, mate, oth)
    nxt = across(tile, 1, straight)
    nxt_edges = across(near2, 1, straight)
    wide = groups * WIDE
    slim = groups * SLIM
    edge0, u1x, d0x, d1x, f2x, field, final, wo, readout_held = kernel_call(
        forward_kernel,
        [spec(groups * 8), spec(slim)] + [spec(slim, BF16)] * 3
        + [spec(4 * lats * cols, F32, members * LANES), spec(size, BF16)]
        + [spec(channels, BF16), spec(channels, BF16, LANES)],
        [scratch(wide), scratch(wide), scratch(wide, BF16), scratch(wide, BF16), scratch(wide, BF16)]
        + [scratch(wide), scratch(16), scratch(4 * size, BF16)]
        + [scratch(1), scratch(channels, BF16), scratch(channels, BF16), pltpu.SemaphoreType.DMA((5,))],
        10**11,
        4000000,
        hbm=5,
    )(gain, self_weight, neighbour_weight, output_weight, readout, held, near4, oth)
    before = across(final, -1, straight)
    total = -(-tiles // SENDERS) * LANES
    spread, near_spread, error, held, background = kernel_call(
        functools.partial(observe_kernel, tiles),
        [spec(4 * size, BF16, LANES), spec(size, BF16, LANES), spec(1), spec(size), spec(size, BF16)],
        [scratch(128, BF16, total)] * 4
        + [scratch(total, F32, LANES), scratch(tiles * CHUNK, F32, LANES), pltpu.SemaphoreType.DMA((3,))],
        10**9,
        2000000,
        hbm=3,
    )(error, flat, background.reshape(size, channels), arrived, field)
    from_mate = lax.ppermute(near_spread, "tile", mate_of)
    handed = kernel_call(
        pull_kernel,
        [spec(slim), spec(slim), spec(channels, BF16), spec(channels, BF16), spec(1)],
        [scratch(4 * size), pltpu.SemaphoreType.DMA((3,))],
        10**9,
        3000000,
        hbm=3,
    )(neighbour_weight, self_weight, gain, spread, readout_held)
    result = kernel_call(
        backward_kernel,
        spec(size),
        [scratch(slim), scratch(slim), scratch(slim), scratch(slim, BF16), scratch(slim), scratch(slim)]
        + [scratch(size), scratch(16), scratch(slim), scratch(slim)],
        12 * slim * channels * channels,
        6000000,
    )(
        *handed, held, background, edge0, nxt, nxt_edges, f2x, wo, readout_held, error, from_mate,
        u1x, d0x, d1x, before,
    )
    return result.reshape(control.shape)


def solution(mesh):
    in_specs = (
        P("slot", None, None, "tile", None),
        P(None, None, "tile", None),
        P(),
        P(),
        P(),
        P(),
        P(),
        P(),
        P("slot", None, "tile", None),
        P("slot", None, "tile", None),
        P("slot", None, "tile", None),
        P("slot", None, "tile", None),
        P("slot", None, "tile"),
    )
    out_specs = P("slot", None, None, "tile", None)
    return jax.shard_map(
        per_device, mesh=mesh, in_specs=in_specs, out_specs=out_specs, check_vma=False
    )
```

profile of v0, /device:TPU:0, one launch (start us, length us, event | category | flops | bytes accessed | tf_op | source)
XLA Modules:
  0.0 26.5 jit_solution(509766693197582963)
XLA Ops:
  0.0 0.5 %collective-permute-start = (f32[128,512]{1,0:T(8,128)}, f32[128,512]{1,0:T(8,128)S(1)}, u32[]{:S(2)}, u32[]{:S(2)}) collective-permute-start(f32[128,512]{1,0:T(8,128)} %bitcast.19), channel_id=1, source_target_pairs={{0,1},{1,0},{2,3},{3,2},{4,5},{5,4},{6,7},{7,6},{8,9},{9,8},{10,11... | collective-permute-start | bytes 786440 | tf_op jit(solution)/shard_map/ppermute | solution.py:485
  0.5 2.0 %shard_map.127 = (f32[128,512]{1,0:T(8,128)S(1)}, bf16[512,128]{1,0:T(8,128)(2,1)}, s32[2,1,32]{2,1,0:T(1,128)S(1)}, s32[2,4,32]{2,1,0:T(4,128)S(1)}, bf16[2,4,3...) custom-call(f32[128,512]{1,0:T(8,128)} %bitcast.20, s32[2,1,32]{2,1,0:T(1,128)} %bitcast.25, ...), custom_call_target="tpu_custom_call" | custom-call | flops 10000000 | bytes 200000 | tf_op jit(solution)/shard_map/pallas_call | solution.py:427
  2.4 0.0 collective-permute-done.mate
  2.5 5.1 %collective-permute-start.1 = (bf16[144,512]{1,0:T(8,128)(2,1)S(1)}, bf16[144,512]{1,0:T(8,128)(2,1)S(1)}, u32[]{:S(2)}, u32[]{:S(2)}) collective-permute-start(bf16[144,512]{1,0:T(8,128)(2,1)S(1)} %shard_map.128.refs_5_), channel_id=1, source_target_pairs={{0,15},{1,2},{2,1},{3,4},{4,3},{5,6},{6,5},{7,8},{8,7},{9,10},{10,... | collective-permute-start | bytes 442376 | tf_op jit(solution)/shard_map/ppermute | solution.py:512
  7.6 3.5 %all-to-all-start = ((bf16[16,32,128]{2,1,0:T(8,128)(2,1)}), bf16[16,32,128]{2,1,0:T(8,128)(2,1)S(1)}, u32[]{:S(2)}, u32[]{:S(2)}) async-start(bf16[16,32,128]{2,1,0:T(8,128)(2,1)} %bitcast.12), calls=%async_computation | async-start | bytes 262144 | tf_op jit(solution)/shard_map/all_to_all | solution.py:523
  11.2 0.0 collective-permute-done.1.oth
  11.2 0.1 shard_map.130
  11.3 1.6 %collective-permute-start.3 = (f32[32,512]{1,0:T(8,128)S(1)}, f32[32,512]{1,0:T(8,128)S(1)}, u32[]{:S(2)}, u32[]{:S(2)}) collective-permute-start(f32[32,512]{1,0:T(8,128)S(1)} %get-tuple-element.54), channel_id=1, source_target_pairs={{16,0},{17,1},{18,2},{19,3},{20,4},{21,5},{22,6},{23,7},{24,8},{25... | collective-permute-start | bytes 196616 | tf_op jit(solution)/shard_map/ppermute | solution.py:482
  12.8 0.5 %collective-permute-start.2 = (f32[128,512]{1,0:T(8,128)S(1)}, f32[128,512]{1,0:T(8,128)S(1)}, u32[]{:S(2)}, u32[]{:S(2)}) collective-permute-start(f32[128,512]{1,0:T(8,128)S(1)} %get-tuple-element.53), channel_id=1, source_target_pairs={{16,0},{17,1},{18,2},{19,3},{20,4},{21,5},{22,6},{23,7},{24,8},{25... | collective-permute-start | bytes 786440 | tf_op jit(solution)/shard_map/ppermute | solution.py:482
  13.4 3.4 %shard_map.131 = (f32[64,512]{1,0:T(8,128)S(1)}, f32[192,512]{1,0:T(8,128)S(1)}, bf16[192,512]{1,0:T(8,128)(2,1)S(1)}, bf16[192,512]{1,0:T(8,128)(2,1)S(1)}, bf1...) custom-call(f32[1,512]{1,0:T(1,128)} %bitcast.29, ...), custom_call_target="tpu_custom_call" | custom-call | flops 99999997952 | bytes 4000000 | tf_op jit(solution)/shard_map/pallas_call | solution.py:427
  16.8 1.6 %collective-permute-start.5 = (bf16[128,512]{1,0:T(8,128)(2,1)S(1)}, bf16[128,512]{1,0:T(8,128)(2,1)S(1)}, u32[]{:S(2)}, u32[]{:S(2)}) collective-permute-start(bf16[128,512]{1,0:T(8,128)(2,1)S(1)} %get-tuple-element.62), channel_id=1, source_target_pairs={{16,0},{17,1},{18,2},{19,3},{20,4},{21,5},{22,6},{23,7},{24,8},{25... | collective-permute-start | bytes 393224 | tf_op jit(solution)/shard_map/ppermute | solution.py:482
  18.4 0.7 %all-to-all-done = bf16[16,32,128]{2,1,0:T(8,128)(2,1)S(1)} async-done(((bf16[16,32,128]{2,1,0:T(8,128)(2,1)}), bf16[16,32,128]{2,1,0:T(8,128)(2,1)S(1)}, u32[]{:S(2)}, u32[]{:S(2)}) %all-to-all-start) | async-done | bytes 131104 | tf_op jit(solution)/shard_map/all_to_all | solution.py:523
  19.1 1.0 %shard_map.132 = (bf16[512,128]{1,0:T(8,128)(2,1)S(1)}, bf16[128,128]{1,0:T(8,128)(2,1)S(1)}, f32[1,512]{1,0:T(1,128)S(1)}, f32[128,512]{1,0:T(8,128)S(1)}, bf16[128,512]{1,0:T(8,128)(2,1)S(1)}) custom-call(f32[1,512]{1,0:T(1,128)} %bitcast.28, f32[128,512]{1,0:T(8,128)} %bitcast.21, bf16[128,512]{1,0:T(8,128)(2,1)} %bitcast.27, ...), custom_call_target="tpu_custom_call" | custom-call | flops 1000000000 | bytes 2000000 | tf_op jit(solution)/shard_map/pallas_call | solution.py:427
  20.1 0.1 collective-permute-start.4
  20.2 1.2 %shard_map.133 = (f32[192,512]{1,0:T(8,128)S(1)}, f32[192,512]{1,0:T(8,128)S(1)}, bf16[512,512]{1,0:T(8,128)(2,1)S(1)}, bf16[512,512]{1,0:T(8,128)(2,1)S(1)}, f32[1,512]{1,0:T(1,128)S(1)}) custom-call(bf16[512,512]{1,0:T(8,128)(2,1)} %wn_hbm.3, bf16[512,512]{1,0:T(8,128)(2,1)} %ws_hbm.3, f32[1,512]{1,0:T(1,128)} %bitcast.30, ...), custom_call_target="tpu_custom_call" | custom-call | flops 1000000000 | bytes 3000000 | tf_op jit(solution)/shard_map/pallas_call | solution.py:427
  21.4 0.0 collective-permute-done.3.nxt_edges
  21.4 2.6 %collective-permute-done.5.before = bf16[128,512]{1,0:T(8,128)(2,1)S(1)} collective-permute-done((bf16[128,512]{1,0:T(8,128)(2,1)S(1)}, bf16[128,512]{1,0:T(8,128)(2,1)S(1)}, u32[]{:S(2)}, u32[]{:S(2)}) %collective-permute-start.5) | collective-permute-done | bytes 131104 | tf_op jit(solution)/shard_map/ppermute | solution.py:482
  24.0 0.0 collective-permute-done.4.message
  24.0 0.0 collective-permute-done.2.nxt
  24.1 2.4 %shard_map.134 = f32[128,512]{1,0:T(8,128)} custom-call(f32[192,512]{1,0:T(8,128)S(1)} %get-tuple-element.45.last, f32[192,512]{1,0:T(8,128)S(1)} %get-tuple-element.46.early_pull, bf16[512,512]{1,0:T(8,128)(2,1)S(1)} %get-tuple-element.47.wn, bf16[512,512]{1,0:T(8,128)(2,1)S(1)} %get-tuple-element.48.ws, f32[1,512]{1,0:T(1,128)S(1)} %get-tuple-element.49.gain, ...), custom_call_target="tpu_custom_call" | custom-call | flops 603979776 | bytes 6000000 | tf_op jit(solution)/shard_map/pallas_call | solution.py:427
  (2 shorter events, 0.1 us)
Async XLA Ops:
  0.0 2.4 %collective-permute-start = (f32[128,512]{1,0:T(8,128)}, f32[128,512]{1,0:T(8,128)S(1)}, u32[]{:S(2)}, u32[]{:S(2)}) collective-permute-start(f32[128,512]{1,0:T(8,128)} %bitcast.19), channel_id=1, source_target_pairs={{0,1},{1,0},{2,3},{3,2},{4,5},{5,4},{6,7},{7,6},{8,9},{9,8},{10,11... | collective-permute-start | bytes 786440 | tf_op jit(solution)/shard_map/ppermute | solution.py:485
  2.5 8.7 %collective-permute-start.1 = (bf16[144,512]{1,0:T(8,128)(2,1)S(1)}, bf16[144,512]{1,0:T(8,128)(2,1)S(1)}, u32[]{:S(2)}, u32[]{:S(2)}) collective-permute-start(bf16[144,512]{1,0:T(8,128)(2,1)S(1)} %shard_map.128.refs_5_), channel_id=1, source_target_pairs={{0,15},{1,2},{2,1},{3,4},{4,3},{5,6},{6,5},{7,8},{8,7},{9,10},{10,... | collective-permute-start | bytes 442376 | tf_op jit(solution)/shard_map/ppermute | solution.py:512
  7.6 11.4 %all-to-all-start = ((bf16[16,32,128]{2,1,0:T(8,128)(2,1)}), bf16[16,32,128]{2,1,0:T(8,128)(2,1)S(1)}, u32[]{:S(2)}, u32[]{:S(2)}) async-start(bf16[16,32,128]{2,1,0:T(8,128)(2,1)} %bitcast.12), calls=%async_computation | async-start | bytes 262144 | tf_op jit(solution)/shard_map/all_to_all | solution.py:523
  11.3 10.1 %collective-permute-start.3 = (f32[32,512]{1,0:T(8,128)S(1)}, f32[32,512]{1,0:T(8,128)S(1)}, u32[]{:S(2)}, u32[]{:S(2)}) collective-permute-start(f32[32,512]{1,0:T(8,128)S(1)} %get-tuple-element.54), channel_id=1, source_target_pairs={{16,0},{17,1},{18,2},{19,3},{20,4},{21,5},{22,6},{23,7},{24,8},{25... | collective-permute-start | bytes 196616 | tf_op jit(solution)/shard_map/ppermute | solution.py:482
  12.8 11.2 %collective-permute-start.2 = (f32[128,512]{1,0:T(8,128)S(1)}, f32[128,512]{1,0:T(8,128)S(1)}, u32[]{:S(2)}, u32[]{:S(2)}) collective-permute-start(f32[128,512]{1,0:T(8,128)S(1)} %get-tuple-element.53), channel_id=1, source_target_pairs={{16,0},{17,1},{18,2},{19,3},{20,4},{21,5},{22,6},{23,7},{24,8},{25... | collective-permute-start | bytes 786440 | tf_op jit(solution)/shard_map/ppermute | solution.py:482
  16.8 7.2 %collective-permute-start.5 = (bf16[128,512]{1,0:T(8,128)(2,1)S(1)}, bf16[128,512]{1,0:T(8,128)(2,1)S(1)}, u32[]{:S(2)}, u32[]{:S(2)}) collective-permute-start(bf16[128,512]{1,0:T(8,128)(2,1)S(1)} %get-tuple-element.62), channel_id=1, source_target_pairs={{16,0},{17,1},{18,2},{19,3},{20,4},{21,5},{22,6},{23,7},{24,8},{25... | collective-permute-start | bytes 393224 | tf_op jit(solution)/shard_map/ppermute | solution.py:482
  20.1 4.0 %collective-permute-start.4 = (bf16[128,128]{1,0:T(8,128)(2,1)S(1)}, bf16[128,128]{1,0:T(8,128)(2,1)S(1)}, u32[]{:S(2)}, u32[]{:S(2)}) collective-permute-start(bf16[128,128]{1,0:T(8,128)(2,1)S(1)} %get-tuple-element.58), channel_id=1, source_target_pairs={{0,1},{1,0},{2,3},{3,2},{4,5},{5,4},{6,7},{7,6},{8,9},{9,8},{10,11... | collective-permute-start | bytes 98312 | tf_op jit(solution)/shard_map/ppermute | solution.py:555
where the time goes:
time: 26.7 us; the launch traced here: 26.5 us
  starting transfers between devices  12.8 us (48%)
  Pallas kernels  10.2 us (38%)
  waiting for transfers between devices  3.32 us (12%)
    pallas_call x8, Pallas kernels, call(): pl.pallas_call(body, out_shape=outs, in_specs=[pl.BlockSpec(memory_space=...  10.2 us
    ppermute x1, starting transfers between devices, per_device(): oth = lax.ppermute(sent, 'tile', other_of)  5.11 us
    ppermute x3, starting transfers between devices, across(): return lax.ppermute(block, ('slot', 'tile'), pairs)  3.65 us
    all_to_all x1, starting transfers between devices, per_device(): lax.all_to_all(packed, 'tile', split_axis=0, concat_axis=0, tiled=True)  3.52 us
    ppermute x3, waiting for transfers between devices, across(): return lax.ppermute(block, ('slot', 'tile'), pairs)  2.63 us
    all_to_all x1, waiting for transfers between devices, per_device(): lax.all_to_all(packed, 'tile', split_axis=0, concat_axis=0, tiled=True)  0.68 us
  transfers between devices with their start and end apart: 7, of which 2 were waited for; matrix products, arithmetic and copies ran while one was open for 0% of the time, Pallas kernels for 29%

commit v1 on v0

--- a/solution.py
+++ b/solution.py
@@ -180,16 +180,16 @@
     out[size:] = held[...].astype(BF16)
 
 
-def relay_kernel(control, mate, oth, tile, out, near4, wide):
+def relay_kernel(control, mate, oth, out, near4, wide):
     even = lax.rem(lax.axis_index("tile"), 2) == 0
     size = mate.shape[0]
-    tile[...] = control[...]
+    out[0:size] = control[...]
     wide[...] = oth[0:size].astype(F32)
     for r in range(size // 16):
         a, b = r * 16, (r + 1) * 16
-        out[r * 2 : (r + 1) * 2] = jnp.where(even, wide[b - 2 : b], wide[a : a + 2])
+        out[size + r * 2 : size + (r + 1) * 2] = jnp.where(even, wide[b - 2 : b], wide[a : a + 2])
         near4[r * 4 : (r + 1) * 4] = jnp.where(even, mate[a : a + 4], mate[b - 4 : b])
-        start = size // 8 + r * 2
+        start = size + size // 8 + r * 2
         out[start : start + 2] = jnp.where(even, mate[a : a + 2], mate[b - 2 : b])
 
 
@@ -285,16 +285,16 @@
         weight = jnp.zeros((32, LANES), F32)
         for i in range(4):
             weight += jnp.where(cells == meta[4 + i : 5 + i], meta[8 + i : 9 + i], 0.0)
+        at = slice(p * LANES, (p + 1) * LANES)
+        th[:, at], tl[:, at] = split(weight)
         scaled = weight * meta[12:13]
-        wh, wl = split(weight)
-        sh, sl = split(scaled)
-        parts = ((th, wh.astype(F32)), (tl, wl.astype(F32)), (ph, sh.astype(F32)), (plo, sl.astype(F32)))
         for q in range(2 * steps):
-            hit = table_of == q
-            for ref, value in parts:
-                kept = jnp.where(hit, value, 0.0).astype(BF16)
-                ref[q * 32 : (q + 1) * 32, p * LANES : (p + 1) * LANES] = kept
+            kept = jnp.where(table_of == q, scaled, 0.0)
+            ph[q * 32 : (q + 1) * 32, at], plo[q * 32 : (q + 1) * 32, at] = split(kept)
     cross = dot_t(ph[...], th[...]) + dot_t(plo[...], th[...]) + dot_t(ph[...], tl[...])
+    block = jnp.concatenate([cross] * (2 * steps), axis=1)
+    on_block = sublane(block.shape) // 32 == lax.broadcasted_iota(jnp.int32, block.shape, 1) // 32
+    cross = jnp.where(on_block, block, 0.0)
     taken = vals[...].astype(BF16)
     target = dot(ph[...], taken) + dot(plo[...], taken)
     ch, cl = split(cross)
@@ -317,7 +317,7 @@
         copy.wait()
 
 
-def adjoint_step(u, cot, gb, gm, flat, d, add, out, gain, ws, wn, wo, members):
+def adjoint_step(u, cot, gb, gm, flat, d, out, gain, ws, wn, wo, members):
     both = 2 * SLIM
     gb[...] = cot[...].astype(BF16)
     flat[...] = dot_t(gb[...], wo[...])
@@ -337,16 +337,14 @@
             s = inverse_rms(x)
             scaled = gain * (flat[start : start + SLIM] + around[lat])
             inner = jnp.mean(x * scaled, axis=-1, keepdims=True)
-            value = cot[start : start + SLIM] + s * scaled - x * (s * s * s * inner)
-            if add is not None:
-                value = value + add[start : start + SLIM]
-            out[start : start + SLIM] = value
-
-
-def edges(nxt, edge, r):
+            out(2 * m + lat, cot[start : start + SLIM] + s * scaled - x * (s * s * s * inner))
+
+
+def edges(nxt, size, edge, r):
     even = lax.rem(lax.axis_index("tile"), 2) == 0
-    far = nxt[r * 2 : (r + 1) * 2]
-    start = nxt.shape[0] // 2 + r * 2
+    start = size + r * 2
+    far = nxt[start : start + 2]
+    start = size + size // 8 + r * 2
     near = nxt[start : start + 2]
     edge[...] = jnp.zeros_like(edge)
     edge[0:2] = near
@@ -382,12 +380,12 @@
 
 
 def backward_kernel(
-    last, early_pull, wn, ws, gain, control, background, edge0, nxt, nxt_edges, f2x, wo, readout, error, message,
+    last, early_pull, wn, ws, gain, control, background, edge0, nxt, f2x, wo, readout, error, message,
     u1x, d0x, d1x, before,
     result,
-    cot2, cot1, add, gb, gm, flat, mate_pull, edge, u0x, final,
+    cot2, cot1, add, gb, gm, flat, mate_pull, edge, u0x, final, held, sems,
 ):
-    size = result.shape[0]
+    size = held.shape[0]
     members = size // 32
     even = lax.rem(lax.axis_index("tile"), 2) == 0
     slot = lax.axis_index("slot")
@@ -405,15 +403,27 @@
         a, b = b, b + 8
         start = size // 2 + r * 8
         pulled = last[a:b] + jnp.where(mate_side, mate_pull[start : start + 8], 0.0)
-        cot2[a:b] = pulled - weight * (edges(nxt_edges, edge, r) - final[a:b])
+        cot2[a:b] = pulled - weight * (edges(nxt, size, edge, r) - final[a:b])
         add[a:b] = early_pull[a:b] + jnp.where(mate_side, mate_pull[r * 8 : (r + 1) * 8], 0.0)
         u0x[a:b] = edge0[r * 8 : (r + 1) * 8]
-    adjoint_step(u1x, cot2, gb, gm, flat, d1x, add, cot1, gain[...], ws, wn, wo, members)
-    adjoint_step(u0x, cot1, gb, gm, flat, d0x, None, cot2, gain[...], ws, wn, wo, members)
-    taken = jnp.where(first, background[...].astype(F32), before[...].astype(F32))
-    for r in range(2 * members):
+    def keep(r, value):
+        cot1[r * SLIM : (r + 1) * SLIM] = value + add[r * SLIM : (r + 1) * SLIM]
+
+    copies = []
+
+    def finish(r, value):
         a, b, start = r * 16, (r + 1) * 16, r * SLIM
-        result[a:b] = cot2[start : start + 16] + error[...] * (u0x[start : start + 16] - taken[a:b])
+        taken = jnp.where(first, background[a:b].astype(F32), before[a:b].astype(F32))
+        held[a:b] = value[0:16] + error[...] * (u0x[start : start + 16] - taken)
+        if r % 2 == 1:
+            rows = pl.ds(b - 32, 32)
+            copies.append(pltpu.make_async_copy(held.at[rows], result.at[rows], sems.at[r // 2]))
+            copies[-1].start()
+
+    adjoint_step(u1x, cot2, gb, gm, flat, d1x, keep, gain[...], ws, wn, wo, members)
+    adjoint_step(u0x, cot1, gb, gm, flat, d0x, finish, gain[...], ws, wn, wo, members)
+    for copy in copies:
+        copy.wait()
 
 
 def kernel_call(body, outs, scratch, flops, moved, hbm=0, out_places=None, aliases={}):
@@ -473,15 +483,15 @@
     mate_of = [(i, i ^ 1) for i in range(tiles)]
     other_of = [(i, (i - 1) % tiles if i % 2 == 0 else (i + 1) % tiles) for i in range(tiles)]
 
-    def across(block, shift, route):
+    def across(block, shift):
         pairs = [
-            (((s + shift) % slots) * tiles + i, s * tiles + j)
+            ((s + shift) * tiles + i, s * tiles + i)
             for s in range(slots)
-            for i, j in route
+            for i in range(tiles)
+            if 0 <= s + shift < slots
         ]
         return lax.ppermute(block, ("slot", "tile"), pairs)
 
-    straight = [(i, i) for i in range(tiles)]
     mate = lax.ppermute(flat, "tile", mate_of)
     listed = (
         jnp.transpose(report_owner[0], (0, 2, 1)),
@@ -522,11 +532,10 @@
     )(packed, *listed, sent)
     arrived = lax.all_to_all(packed, "tile", split_axis=0, concat_axis=0, tiled=True)
 
-    tile, near2, near4 = kernel_call(
-        relay_kernel, [spec(size), spec(4 * groups), spec(4 * groups)], [scratch(size)], 1000, 700000
+    message, near4 = kernel_call(
+        relay_kernel, [spec(size + 4 * groups), spec(4 * groups)], [scratch(size)], 1000, 700000
     )(held, mate, oth)
-    nxt = across(tile, 1, straight)
-    nxt_edges = across(near2, 1, straight)
+    nxt = across(message, 1)
     wide = groups * WIDE
     slim = groups * SLIM
     edge0, u1x, d0x, d1x, f2x, field, final, wo, readout_held = kernel_call(
@@ -541,12 +550,12 @@
         4000000,
         hbm=5,
     )(gain, self_weight, neighbour_weight, output_weight, readout, held, near4, oth)
-    before = across(final, -1, straight)
+    before = across(final, -1)
     total = -(-tiles // SENDERS) * LANES
     spread, near_spread, error, held, background = kernel_call(
         functools.partial(observe_kernel, tiles),
         [spec(4 * size, BF16, LANES), spec(size, BF16, LANES), spec(1), spec(size), spec(size, BF16)],
-        [scratch(128, BF16, total)] * 4
+        [scratch(32, BF16, total)] * 2 + [scratch(128, BF16, total)] * 2
         + [scratch(total, F32, LANES), scratch(tiles * CHUNK, F32, LANES), pltpu.SemaphoreType.DMA((3,))],
         10**9,
         2000000,
@@ -561,15 +570,17 @@
         3000000,
         hbm=3,
     )(neighbour_weight, self_weight, gain, spread, readout_held)
-    result = kernel_call(
+    (result,) = kernel_call(
         backward_kernel,
-        spec(size),
+        [spec(size)],
         [scratch(slim), scratch(slim), scratch(slim), scratch(slim, BF16), scratch(slim), scratch(slim)]
-        + [scratch(size), scratch(16), scratch(slim), scratch(slim)],
+        + [scratch(size), scratch(16), scratch(slim), scratch(slim), scratch(size)]
+        + [pltpu.SemaphoreType.DMA((members,))],
         12 * slim * channels * channels,
         6000000,
+        out_places=[pltpu.HBM],
     )(
-        *handed, held, background, edge0, nxt, nxt_edges, f2x, wo, readout_held, error, from_mate,
+        *handed, held, background, edge0, nxt, f2x, wo, readout_held, error, from_mate,
         u1x, d0x, d1x, before,
     )
     return result.reshape(control.shape)

time: 26.7 us -> 26.2 us (0.981)
  waiting for transfers between devices: 3.32 us -> 0.54 us
  starting transfers between devices: 12.8 us -> 15 us
    ppermute x3 -> x2, starting transfers between devices: 3.65 us -> 5.86 us  [across(): return lax.ppermute(block, ('slot', 'tile'), pairs)]
    ppermute x3 -> x2, waiting for transfers between devices: 2.63 us -> 0.53 us  [across(): return lax.ppermute(block, ('slot', 'tile'), pairs)]
    all_to_all x1, waiting for transfers between devices: 0.68 us -> 0.01 us  [per_device(): lax.all_to_all(packed, 'tile', split_axis=0, concat_axis=0, tiled=True)]
  transfers between devices with their start and end apart: 7 -> 6, of which waited for: 2 -> 1; matrix products, arithmetic and copies ran while one was open for 0% -> 0% of each run, Pallas kernels for 29% -> 30%
where the time goes in v1:
time: 26.2 us; the launch traced here: 25.9 us
  starting transfers between devices  15 us (57%)
  Pallas kernels  10.2 us (39%)
  waiting for transfers between devices  0.54 us (2%)
    pallas_call x8, Pallas kernels, call(): pl.pallas_call(body, out_shape=outs, in_specs=[pl.BlockSpec(memory_space=...  10.2 us
    ppermute x2, starting transfers between devices, across(): return lax.ppermute(block, ('slot', 'tile'), pairs)  5.86 us
    ppermute x1, starting transfers between devices, per_device(): oth = lax.ppermute(sent, 'tile', other_of)  5.11 us
    all_to_all x1, starting transfers between devices, per_device(): lax.all_to_all(packed, 'tile', split_axis=0, concat_axis=0, tiled=True)  3.52 us
    ppermute x2, waiting for transfers between devices, across(): return lax.ppermute(block, ('slot', 'tile'), pairs)  0.53 us
  transfers between devices with their start and end apart: 6, of which 1 were waited for; matrix products, arithmetic and copies ran while one was open for 0% of the time, Pallas kernels for 30%

profile of v1, /device:TPU:0, one launch (start us, length us, event | category | flops | bytes accessed | tf_op | source)
XLA Modules:
  0.0 25.9 jit_solution(1761496938631783925)
XLA Ops:
  0.0 0.5 %collective-permute-start = (f32[128,512]{1,0:T(8,128)}, f32[128,512]{1,0:T(8,128)S(1)}, u32[]{:S(2)}, u32[]{:S(2)}) collective-permute-start(f32[128,512]{1,0:T(8,128)} %bitcast.19), channel_id=1, source_target_pairs={{0,1},{1,0},{2,3},{3,2},{4,5},{5,4},{6,7},{7,6},{8,9},{9,8},{10,11... | collective-permute-start | bytes 786440 | tf_op jit(solution)/shard_map/ppermute | solution.py:495
  0.5 2.0 %shard_map.127 = (f32[128,512]{1,0:T(8,128)S(1)}, bf16[512,128]{1,0:T(8,128)(2,1)}, s32[2,1,32]{2,1,0:T(1,128)S(1)}, s32[2,4,32]{2,1,0:T(4,128)S(1)}, bf16[2,4,3...) custom-call(f32[128,512]{1,0:T(8,128)} %bitcast.20, s32[2,1,32]{2,1,0:T(1,128)} %bitcast.25, ...), custom_call_target="tpu_custom_call" | custom-call | flops 10000000 | bytes 200000 | tf_op jit(solution)/shard_map/pallas_call | solution.py:437
  2.4 0.0 collective-permute-done.mate
  2.5 5.1 %collective-permute-start.1 = (bf16[144,512]{1,0:T(8,128)(2,1)S(1)}, bf16[144,512]{1,0:T(8,128)(2,1)S(1)}, u32[]{:S(2)}, u32[]{:S(2)}) collective-permute-start(bf16[144,512]{1,0:T(8,128)(2,1)S(1)} %shard_map.128.refs_5_), channel_id=1, source_target_pairs={{0,15},{1,2},{2,1},{3,4},{4,3},{5,6},{6,5},{7,8},{8,7},{9,10},{10,... | collective-permute-start | bytes 442376 | tf_op jit(solution)/shard_map/ppermute | solution.py:522
  7.6 3.5 %all-to-all-start = ((bf16[16,32,128]{2,1,0:T(8,128)(2,1)}), bf16[16,32,128]{2,1,0:T(8,128)(2,1)S(1)}, u32[]{:S(2)}, u32[]{:S(2)}) async-start(bf16[16,32,128]{2,1,0:T(8,128)(2,1)} %bitcast.12), calls=%async_computation | async-start | bytes 262144 | tf_op jit(solution)/shard_map/all_to_all | solution.py:533
  11.2 0.0 collective-permute-done.1.oth
  11.2 0.1 shard_map.130
  11.3 1.3 %collective-permute-start.2 = (f32[160,512]{1,0:T(8,128)S(1)}, f32[160,512]{1,0:T(8,128)S(1)}, u32[]{:S(2)}, u32[]{:S(2)}) collective-permute-start(f32[160,512]{1,0:T(8,128)S(1)} %get-tuple-element.52), channel_id=1, source_target_pairs={{16,0},{17,1},{18,2},{19,3},{20,4},{21,5},{22,6},{23,7},{24,8},{25... | collective-permute-start | bytes 983048 | tf_op jit(solution)/shard_map/ppermute | solution.py:493
  12.6 3.4 %shard_map.131 = (f32[64,512]{1,0:T(8,128)S(1)}, f32[192,512]{1,0:T(8,128)S(1)}, bf16[192,512]{1,0:T(8,128)(2,1)S(1)}, bf16[192,512]{1,0:T(8,128)(2,1)S(1)}, bf1...) custom-call(f32[1,512]{1,0:T(1,128)} %bitcast.29, ...), custom_call_target="tpu_custom_call" | custom-call | flops 99999997952 | bytes 4000000 | tf_op jit(solution)/shard_map/pallas_call | solution.py:437
  16.0 4.6 %collective-permute-start.4 = (bf16[128,512]{1,0:T(8,128)(2,1)S(1)}, bf16[128,512]{1,0:T(8,128)(2,1)S(1)}, u32[]{:S(2)}, u32[]{:S(2)}) collective-permute-start(bf16[128,512]{1,0:T(8,128)(2,1)S(1)} %get-tuple-element.60), channel_id=1, source_target_pairs={{0,16},{1,17},{2,18},{3,19},{4,20},{5,21},{6,22},{7,23},{8,24},{9,... | collective-permute-start | bytes 393224 | tf_op jit(solution)/shard_map/ppermute | solution.py:493
  20.6 0.0 all-to-all-done
  20.6 1.0 %shard_map.132 = (bf16[512,128]{1,0:T(8,128)(2,1)S(1)}, bf16[128,128]{1,0:T(8,128)(2,1)S(1)}, f32[1,512]{1,0:T(1,128)S(1)}, f32[128,512]{1,0:T(8,128)S(1)}, bf16[128,512]{1,0:T(8,128)(2,1)S(1)}) custom-call(f32[1,512]{1,0:T(1,128)} %bitcast.28, f32[128,512]{1,0:T(8,128)} %bitcast.21, bf16[128,512]{1,0:T(8,128)(2,1)} %bitcast.27, ...), custom_call_target="tpu_custom_call" | custom-call | flops 1000000000 | bytes 2000000 | tf_op jit(solution)/shard_map/pallas_call | solution.py:437
  21.6 0.1 collective-permute-start.3
  21.7 1.2 %shard_map.133 = (f32[192,512]{1,0:T(8,128)S(1)}, f32[192,512]{1,0:T(8,128)S(1)}, bf16[512,512]{1,0:T(8,128)(2,1)S(1)}, bf16[512,512]{1,0:T(8,128)(2,1)S(1)}, f32[1,512]{1,0:T(1,128)S(1)}) custom-call(bf16[512,512]{1,0:T(8,128)(2,1)} %wn_hbm.3, bf16[512,512]{1,0:T(8,128)(2,1)} %ws_hbm.3, f32[1,512]{1,0:T(1,128)} %bitcast.30, ...), custom_call_target="tpu_custom_call" | custom-call | flops 1000000000 | bytes 3000000 | tf_op jit(solution)/shard_map/pallas_call | solution.py:437
  23.0 0.5 %collective-permute-done.4.before = bf16[128,512]{1,0:T(8,128)(2,1)S(1)} collective-permute-done((bf16[128,512]{1,0:T(8,128)(2,1)S(1)}, bf16[128,512]{1,0:T(8,128)(2,1)S(1)}, u32[]{:S(2)}, u32[]{:S(2)}) %collective-permute-start.4) | collective-permute-done | bytes 131104 | tf_op jit(solution)/shard_map/ppermute | solution.py:493
  23.5 0.0 collective-permute-done.3.message
  23.5 0.0 collective-permute-done.2.nxt
  23.5 2.4 %shard_map.134 = f32[128,512]{1,0:T(8,128)} custom-call(f32[192,512]{1,0:T(8,128)S(1)} %get-tuple-element.44.last, f32[192,512]{1,0:T(8,128)S(1)} %get-tuple-element.45.early_pull, bf16[512,512]{1,0:T(8,128)(2,1)S(1)} %get-tuple-element.46.wn, bf16[512,512]{1,0:T(8,128)(2,1)S(1)} %get-tuple-element.47.ws, f32[1,512]{1,0:T(1,128)S(1)} %get-tuple-element.48.gain, ...), custom_call_target="tpu_custom_call" | custom-call | flops 603979776 | bytes 6000000 | tf_op jit(solution)/shard_map/pallas_call | solution.py:437
  (2 shorter events, 0.1 us)
Async XLA Ops:
  0.0 2.4 %collective-permute-start = (f32[128,512]{1,0:T(8,128)}, f32[128,512]{1,0:T(8,128)S(1)}, u32[]{:S(2)}, u32[]{:S(2)}) collective-permute-start(f32[128,512]{1,0:T(8,128)} %bitcast.19), channel_id=1, source_target_pairs={{0,1},{1,0},{2,3},{3,2},{4,5},{5,4},{6,7},{7,6},{8,9},{9,8},{10,11... | collective-permute-start | bytes 786440 | tf_op jit(solution)/shard_map/ppermute | solution.py:495
  2.5 8.7 %collective-permute-start.1 = (bf16[144,512]{1,0:T(8,128)(2,1)S(1)}, bf16[144,512]{1,0:T(8,128)(2,1)S(1)}, u32[]{:S(2)}, u32[]{:S(2)}) collective-permute-start(bf16[144,512]{1,0:T(8,128)(2,1)S(1)} %shard_map.128.refs_5_), channel_id=1, source_target_pairs={{0,15},{1,2},{2,1},{3,4},{4,3},{5,6},{6,5},{7,8},{8,7},{9,10},{10,... | collective-permute-start | bytes 442376 | tf_op jit(solution)/shard_map/ppermute | solution.py:522
  7.6 13.0 %all-to-all-start = ((bf16[16,32,128]{2,1,0:T(8,128)(2,1)}), bf16[16,32,128]{2,1,0:T(8,128)(2,1)S(1)}, u32[]{:S(2)}, u32[]{:S(2)}) async-start(bf16[16,32,128]{2,1,0:T(8,128)(2,1)} %bitcast.12), calls=%async_computation | async-start | bytes 262144 | tf_op jit(solution)/shard_map/all_to_all | solution.py:533
  11.3 12.2 %collective-permute-start.2 = (f32[160,512]{1,0:T(8,128)S(1)}, f32[160,512]{1,0:T(8,128)S(1)}, u32[]{:S(2)}, u32[]{:S(2)}) collective-permute-start(f32[160,512]{1,0:T(8,128)S(1)} %get-tuple-element.52), channel_id=1, source_target_pairs={{16,0},{17,1},{18,2},{19,3},{20,4},{21,5},{22,6},{23,7},{24,8},{25... | collective-permute-start | bytes 983048 | tf_op jit(solution)/shard_map/ppermute | solution.py:493
  16.0 7.5 %collective-permute-start.4 = (bf16[128,512]{1,0:T(8,128)(2,1)S(1)}, bf16[128,512]{1,0:T(8,128)(2,1)S(1)}, u32[]{:S(2)}, u32[]{:S(2)}) collective-permute-start(bf16[128,512]{1,0:T(8,128)(2,1)S(1)} %get-tuple-element.60), channel_id=1, source_target_pairs={{0,16},{1,17},{2,18},{3,19},{4,20},{5,21},{6,22},{7,23},{8,24},{9,... | collective-permute-start | bytes 393224 | tf_op jit(solution)/shard_map/ppermute | solution.py:493
  21.6 1.9 %collective-permute-start.3 = (bf16[128,128]{1,0:T(8,128)(2,1)S(1)}, bf16[128,128]{1,0:T(8,128)(2,1)S(1)}, u32[]{:S(2)}, u32[]{:S(2)}) collective-permute-start(bf16[128,128]{1,0:T(8,128)(2,1)S(1)} %get-tuple-element.56), channel_id=1, source_target_pairs={{0,1},{1,0},{2,3},{3,2},{4,5},{5,4},{6,7},{7,6},{8,9},{9,8},{10,11... | collective-permute-start | bytes 98312 | tf_op jit(solution)/shard_map/ppermute | solution.py:564

commit v2 on v1

--- a/solution.py
+++ b/solution.py
@@ -180,25 +180,29 @@
     out[size:] = held[...].astype(BF16)
 
 
-def relay_kernel(control, mate, oth, out, near4, wide):
+def relay_kernel(control, mate, oth, out, near4, wide, edge):
     even = lax.rem(lax.axis_index("tile"), 2) == 0
     size = mate.shape[0]
-    out[0:size] = control[...]
+    out[0:size] = control[...].astype(BF16)
     wide[...] = oth[0:size].astype(F32)
     for r in range(size // 16):
         a, b = r * 16, (r + 1) * 16
-        out[size + r * 2 : size + (r + 1) * 2] = jnp.where(even, wide[b - 2 : b], wide[a : a + 2])
+        edge[r * 2 : (r + 1) * 2] = jnp.where(even, wide[b - 2 : b], wide[a : a + 2])
         near4[r * 4 : (r + 1) * 4] = jnp.where(even, mate[a : a + 4], mate[b - 4 : b])
-        start = size + size // 8 + r * 2
-        out[start : start + 2] = jnp.where(even, mate[a : a + 2], mate[b - 2 : b])
+        start = size // 8 + r * 2
+        edge[start : start + 2] = jnp.where(even, mate[a : a + 2], mate[b - 2 : b])
+    out[size:] = edge[...].astype(BF16)
 
 
 def forward_kernel(
-    gain_hbm, ws_hbm, wn_hbm, wo_hbm, readout_hbm, control, mate, oth,
-    edge0, u1x, d0x, d1x, f2x, field, final, wo, readout,
-    ua, ub, n, mean, act, pre, edge, states, gain, ws, wn, sems,
+    gain_hbm, ws_hbm, wn_hbm, wo_hbm, readout_hbm, error_hbm, background_hbm, control, mate, oth,
+    edge0, u1x, d0x, d1x, f2x, field, final, wo, readout, gain, error, background,
+    ua, ub, n, mean, act, pre, edge, states, ws, wn, sems,
 ):
-    pairs = ((gain_hbm, gain), (ws_hbm, ws), (wn_hbm, wn), (wo_hbm, wo), (readout_hbm, readout))
+    pairs = (
+        (gain_hbm, gain), (ws_hbm, ws), (wn_hbm, wn), (wo_hbm, wo), (readout_hbm, readout),
+        (error_hbm, error), (background_hbm, background),
+    )
     copies = [pltpu.make_async_copy(source, to, sems.at[i]) for i, (source, to) in enumerate(pairs)]
     for copy in copies:
         copy.start()
@@ -259,15 +263,10 @@
 
 
 def observe_kernel(
-    tiles,
-    error_hbm, control_hbm, background_hbm, arrived, field,
-    spread, message, error, control, background,
-    th, tl, ph, plo, vals, wide, sems,
+    tiles, arrived, field,
+    spread, message,
+    th, tl, ph, plo, vals, wide,
 ):
-    pairs = ((error_hbm, error), (control_hbm, control), (background_hbm, background))
-    copies = [pltpu.make_async_copy(source, to, sems.at[i]) for i, (source, to) in enumerate(pairs)]
-    for copy in copies:
-        copy.start()
     steps = 2
     members = field.shape[1] // LANES
     even = lax.rem(lax.axis_index("tile"), 2) == 0
@@ -313,8 +312,6 @@
             near = [jnp.where(even, pair[i + 8 : i + 16], pair[i : i + 8]) for i in (0, 16)]
             start = k * size // 2 + m * 16
             message[start : start + 16] = jnp.concatenate(near, axis=0).astype(BF16)
-    for copy in copies:
-        copy.wait()
 
 
 def adjoint_step(u, cot, gb, gm, flat, d, out, gain, ws, wn, wo, members):
@@ -355,11 +352,11 @@
 
 
 def pull_kernel(
-    wn_hbm, ws_hbm, gain_hbm, spread, readout,
-    last, first, wn, ws, gain,
+    wn_hbm, ws_hbm, spread, readout,
+    last, first, wn, ws,
     pulled, sems,
 ):
-    pairs = ((wn_hbm, wn), (ws_hbm, ws), (gain_hbm, gain))
+    pairs = ((wn_hbm, wn), (ws_hbm, ws))
     copies = [pltpu.make_async_copy(source, to, sems.at[i]) for i, (source, to) in enumerate(pairs)]
     for copy in copies:
         copy.start()
@@ -380,17 +377,16 @@
 
 
 def backward_kernel(
-    last, early_pull, wn, ws, gain, control, background, edge0, nxt, f2x, wo, readout, error, message,
-    u1x, d0x, d1x, before,
+    last, early_pull, wn, ws, gain, control, edge0, message16, f2x, wo, readout, error, message,
+    u1x, d0x, d1x,
     result,
-    cot2, cot1, add, gb, gm, flat, mate_pull, edge, u0x, final, held, sems,
+    cot2, cot1, add, gb, gm, flat, mate_pull, edge, u0x, final, nxt,
 ):
-    size = held.shape[0]
+    size = result.shape[0]
     members = size // 32
     even = lax.rem(lax.axis_index("tile"), 2) == 0
-    slot = lax.axis_index("slot")
-    first = slot == 0
-    weight = jnp.where(slot == lax.axis_size("slot") - 1, 0.0, 1.0) * error[...]
+    nxt[...] = message16[...].astype(F32)
+    weight = jnp.where(lax.axis_index("slot") == lax.axis_size("slot") - 1, 0.0, 1.0) * error[...]
     row8 = sublane((8, 1))
     mate_side = jnp.where(even, 1, 0) == jnp.where(row8 < 4, 1, 0)
     mate_pull[...] = dot_t(message[...], readout[...])
@@ -409,21 +405,18 @@
     def keep(r, value):
         cot1[r * SLIM : (r + 1) * SLIM] = value + add[r * SLIM : (r + 1) * SLIM]
 
-    copies = []
-
     def finish(r, value):
-        a, b, start = r * 16, (r + 1) * 16, r * SLIM
-        taken = jnp.where(first, background[a:b].astype(F32), before[a:b].astype(F32))
-        held[a:b] = value[0:16] + error[...] * (u0x[start : start + 16] - taken)
-        if r % 2 == 1:
-            rows = pl.ds(b - 32, 32)
-            copies.append(pltpu.make_async_copy(held.at[rows], result.at[rows], sems.at[r // 2]))
-            copies[-1].start()
+        a, b = r * SLIM, r * SLIM + 16
+        result[r * 16 : (r + 1) * 16] = value[0:16] + error[...] * u0x[a:b]
 
     adjoint_step(u1x, cot2, gb, gm, flat, d1x, keep, gain[...], ws, wn, wo, members)
     adjoint_step(u0x, cot1, gb, gm, flat, d0x, finish, gain[...], ws, wn, wo, members)
-    for copy in copies:
-        copy.wait()
+
+
+def last_kernel(base, background, before, error, result):
+    first = lax.axis_index("slot") == 0
+    taken = jnp.where(first, background[...].astype(F32), before[...].astype(F32))
+    result[...] = base[...] - error[...] * taken
 
 
 def kernel_call(body, outs, scratch, flops, moved, hbm=0, out_places=None, aliases={}):
@@ -485,10 +478,7 @@
 
     def across(block, shift):
         pairs = [
-            ((s + shift) * tiles + i, s * tiles + i)
-            for s in range(slots)
-            for i in range(tiles)
-            if 0 <= s + shift < slots
+            ((s + shift) % slots * tiles + i, s * tiles + i) for s in range(slots) for i in range(tiles)
         ]
         return lax.ppermute(block, ("slot", "tile"), pairs)
 
@@ -533,56 +523,63 @@
     arrived = lax.all_to_all(packed, "tile", split_axis=0, concat_axis=0, tiled=True)
 
     message, near4 = kernel_call(
-        relay_kernel, [spec(size + 4 * groups), spec(4 * groups)], [scratch(size)], 1000, 700000
+        relay_kernel,
+        [spec(size + 4 * groups, BF16), spec(4 * groups)],
+        [scratch(size), scratch(4 * groups)],
+        1000,
+        700000,
     )(held, mate, oth)
     nxt = across(message, 1)
     wide = groups * WIDE
     slim = groups * SLIM
-    edge0, u1x, d0x, d1x, f2x, field, final, wo, readout_held = kernel_call(
+    (
+        edge0, u1x, d0x, d1x, f2x, field, final, wo, readout_held, gain_held, error_held, background_held,
+    ) = kernel_call(
         forward_kernel,
         [spec(groups * 8), spec(slim)] + [spec(slim, BF16)] * 3
         + [spec(4 * lats * cols, F32, members * LANES), spec(size, BF16)]
-        + [spec(channels, BF16), spec(channels, BF16, LANES)],
+        + [spec(channels, BF16), spec(channels, BF16, LANES), spec(1), spec(1), spec(size, BF16)],
         [scratch(wide), scratch(wide), scratch(wide, BF16), scratch(wide, BF16), scratch(wide, BF16)]
         + [scratch(wide), scratch(16), scratch(4 * size, BF16)]
-        + [scratch(1), scratch(channels, BF16), scratch(channels, BF16), pltpu.SemaphoreType.DMA((5,))],
+        + [scratch(channels, BF16), scratch(channels, BF16), pltpu.SemaphoreType.DMA((7,))],
         10**11,
         4000000,
-        hbm=5,
-    )(gain, self_weight, neighbour_weight, output_weight, readout, held, near4, oth)
+        hbm=7,
+    )(
+        gain, self_weight, neighbour_weight, output_weight, readout, error, background.reshape(size, channels),
+        held, near4, oth,
+    )
     before = across(final, -1)
     total = -(-tiles // SENDERS) * LANES
-    spread, near_spread, error, held, background = kernel_call(
+    spread, near_spread = kernel_call(
         functools.partial(observe_kernel, tiles),
-        [spec(4 * size, BF16, LANES), spec(size, BF16, LANES), spec(1), spec(size), spec(size, BF16)],
+        [spec(4 * size, BF16, LANES), spec(size, BF16, LANES)],
         [scratch(32, BF16, total)] * 2 + [scratch(128, BF16, total)] * 2
-        + [scratch(total, F32, LANES), scratch(tiles * CHUNK, F32, LANES), pltpu.SemaphoreType.DMA((3,))],
+        + [scratch(total, F32, LANES), scratch(tiles * CHUNK, F32, LANES)],
         10**9,
         2000000,
-        hbm=3,
-    )(error, flat, background.reshape(size, channels), arrived, field)
+    )(arrived, field)
     from_mate = lax.ppermute(near_spread, "tile", mate_of)
     handed = kernel_call(
         pull_kernel,
-        [spec(slim), spec(slim), spec(channels, BF16), spec(channels, BF16), spec(1)],
-        [scratch(4 * size), pltpu.SemaphoreType.DMA((3,))],
+        [spec(slim), spec(slim), spec(channels, BF16), spec(channels, BF16)],
+        [scratch(4 * size), pltpu.SemaphoreType.DMA((2,))],
         10**9,
         3000000,
-        hbm=3,
-    )(neighbour_weight, self_weight, gain, spread, readout_held)
-    (result,) = kernel_call(
+        hbm=2,
+    )(neighbour_weight, self_weight, spread, readout_held)
+    base = kernel_call(
         backward_kernel,
-        [spec(size)],
+        spec(size),
         [scratch(slim), scratch(slim), scratch(slim), scratch(slim, BF16), scratch(slim), scratch(slim)]
-        + [scratch(size), scratch(16), scratch(slim), scratch(slim), scratch(size)]
-        + [pltpu.SemaphoreType.DMA((members,))],
+        + [scratch(size), scratch(16), scratch(slim), scratch(slim), scratch(size + 4 * groups)],
         12 * slim * channels * channels,
         6000000,
-        out_places=[pltpu.HBM],
     )(
-        *handed, held, background, edge0, nxt, f2x, wo, readout_held, error, from_mate,
-        u1x, d0x, d1x, before,
+        *handed, gain_held, held, edge0, nxt, f2x, wo, readout_held, error_held, from_mate,
+        u1x, d0x, d1x,
     )
+    result = kernel_call(last_kernel, spec(size), [], 10**6, 900000)(base, background_held, before, error_held)
     return result.reshape(control.shape)
 
 

time: 26.2 us -> 23.8 us (0.908)
  starting transfers between devices: 15 us -> 11.3 us
  waiting for transfers between devices: 0.54 us -> 2.17 us
    ppermute x2, starting transfers between devices: 5.86 us -> 2.16 us  [across(): return lax.ppermute(block, ('slot', 'tile'), pairs)]
    all_to_all x1, waiting for transfers between devices: 0.01 us -> 2.16 us  [per_device(): lax.all_to_all(packed, 'tile', split_axis=0, concat_axis=0, tiled=True)]
    ppermute x2, waiting for transfers between devices: 0.53 us -> 0.01 us  [across(): return lax.ppermute(block, ('slot', 'tile'), pairs)]
    pallas_call x8 -> x9, Pallas kernels: 10.2 us -> 9.94 us  [call(): pl.pallas_call(body, out_shape=outs, in_specs=[pl.BlockSpec(memory_space=...]
  transfers between devices with their start and end apart: 6 -> 6, of which waited for: 1 -> 1; matrix products, arithmetic and copies ran while one was open for 0% -> 0% of each run, Pallas kernels for 30% -> 39%
where the time goes in v2:
time: 23.8 us; the launch traced here: 23.5 us
  starting transfers between devices  11.3 us (47%)
  Pallas kernels  9.94 us (42%)
  waiting for transfers between devices  2.17 us (9%)
    pallas_call x9, Pallas kernels, call(): pl.pallas_call(body, out_shape=outs, in_specs=[pl.BlockSpec(memory_space=...  9.94 us
    ppermute x1, starting transfers between devices, per_device(): oth = lax.ppermute(sent, 'tile', other_of)  5.11 us
    all_to_all x1, starting transfers between devices, per_device(): lax.all_to_all(packed, 'tile', split_axis=0, concat_axis=0, tiled=True)  3.52 us
    all_to_all x1, waiting for transfers between devices, per_device(): lax.all_to_all(packed, 'tile', split_axis=0, concat_axis=0, tiled=True)  2.16 us
    ppermute x2, starting transfers between devices, across(): return lax.ppermute(block, ('slot', 'tile'), pairs)  2.16 us
  transfers between devices with their start and end apart: 6, of which 1 were waited for; matrix products, arithmetic and copies ran while one was open for 0% of the time, Pallas kernels for 39%

profile of v2, /device:TPU:0, one launch (start us, length us, event | category | flops | bytes accessed | tf_op | source)
XLA Modules:
  0.0 23.5 jit_solution(8443861792482504403)
XLA Ops:
  0.0 0.5 %collective-permute-start = (f32[128,512]{1,0:T(8,128)}, f32[128,512]{1,0:T(8,128)S(1)}, u32[]{:S(2)}, u32[]{:S(2)}) collective-permute-start(f32[128,512]{1,0:T(8,128)} %bitcast.19), channel_id=1, source_target_pairs={{0,1},{1,0},{2,3},{3,2},{4,5},{5,4},{6,7},{7,6},{8,9},{9,8},{10,11... | collective-permute-start | bytes 786440 | tf_op jit(solution)/shard_map/ppermute | solution.py:485
  0.5 2.0 %shard_map.127 = (f32[128,512]{1,0:T(8,128)S(1)}, bf16[512,128]{1,0:T(8,128)(2,1)}, s32[2,1,32]{2,1,0:T(1,128)S(1)}, s32[2,4,32]{2,1,0:T(4,128)S(1)}, bf16[2,4,3...) custom-call(f32[128,512]{1,0:T(8,128)} %bitcast.20, s32[2,1,32]{2,1,0:T(1,128)} %bitcast.24, ...), custom_call_target="tpu_custom_call" | custom-call | flops 10000000 | bytes 200000 | tf_op jit(solution)/shard_map/pallas_call | solution.py:430
  2.4 0.0 collective-permute-done.mate
  2.5 5.1 %collective-permute-start.1 = (bf16[144,512]{1,0:T(8,128)(2,1)S(1)}, bf16[144,512]{1,0:T(8,128)(2,1)S(1)}, u32[]{:S(2)}, u32[]{:S(2)}) collective-permute-start(bf16[144,512]{1,0:T(8,128)(2,1)S(1)} %shard_map.128.refs_5_), channel_id=1, source_target_pairs={{0,15},{1,2},{2,1},{3,4},{4,3},{5,6},{6,5},{7,8},{8,7},{9,10},{10,... | collective-permute-start | bytes 442376 | tf_op jit(solution)/shard_map/ppermute | solution.py:512
  7.6 3.5 %all-to-all-start = ((bf16[16,32,128]{2,1,0:T(8,128)(2,1)}), bf16[16,32,128]{2,1,0:T(8,128)(2,1)S(1)}, u32[]{:S(2)}, u32[]{:S(2)}) async-start(bf16[16,32,128]{2,1,0:T(8,128)(2,1)} %bitcast.9), calls=%async_computation | async-start | bytes 262144 | tf_op jit(solution)/shard_map/all_to_all | solution.py:523
  11.2 0.0 collective-permute-done.1.oth
  11.2 0.1 shard_map.130
  11.3 1.6 %collective-permute-start.2 = (bf16[160,512]{1,0:T(8,128)(2,1)S(1)}, bf16[160,512]{1,0:T(8,128)(2,1)S(1)}, u32[]{:S(2)}, u32[]{:S(2)}) collective-permute-start(bf16[160,512]{1,0:T(8,128)(2,1)S(1)} %get-tuple-element.49), channel_id=1, source_target_pairs={{16,0},{17,1},{18,2},{19,3},{20,4},{21,5},{22,6},{23,7},{24,8},{25... | collective-permute-start | bytes 491528 | tf_op jit(solution)/shard_map/ppermute | solution.py:483
  12.8 3.5 %shard_map.131 = (f32[64,512]{1,0:T(8,128)S(1)}, f32[192,512]{1,0:T(8,128)S(1)}, bf16[192,512]{1,0:T(8,128)(2,1)S(1)}, bf16[192,512]{1,0:T(8,128)(2,1)S(1)}, bf1...) custom-call(f32[1,512]{1,0:T(1,128)} %bitcast.27, ...), custom_call_target="tpu_custom_call" | custom-call | flops 99999997952 | bytes 4000000 | tf_op jit(solution)/shard_map/pallas_call | solution.py:430
  16.3 0.6 %collective-permute-start.4 = (bf16[128,512]{1,0:T(8,128)(2,1)S(1)}, bf16[128,512]{1,0:T(8,128)(2,1)S(1)}, u32[]{:S(2)}, u32[]{:S(2)}) collective-permute-start(bf16[128,512]{1,0:T(8,128)(2,1)S(1)} %get-tuple-element.58), channel_id=1, source_target_pairs={{16,0},{17,1},{18,2},{19,3},{20,4},{21,5},{22,6},{23,7},{24,8},{25... | collective-permute-start | bytes 393224 | tf_op jit(solution)/shard_map/ppermute | solution.py:483
  16.9 2.2 %all-to-all-done = bf16[16,32,128]{2,1,0:T(8,128)(2,1)S(1)} async-done(((bf16[16,32,128]{2,1,0:T(8,128)(2,1)}), bf16[16,32,128]{2,1,0:T(8,128)(2,1)S(1)}, u32[]{:S(2)}, u32[]{:S(2)}) %all-to-all-start) | async-done | bytes 131104 | tf_op jit(solution)/shard_map/all_to_all | solution.py:523
  19.1 0.7 %shard_map.132 = (bf16[512,128]{1,0:T(8,128)(2,1)S(1)}, bf16[128,128]{1,0:T(8,128)(2,1)S(1)}) custom-call(bf16[512,128]{1,0:T(8,128)(2,1)S(1)} %bitcast.18, f32[128,512]{1,0:T(8,128)S(1)} %get-tuple-element.40.field), custom_call_target="tpu_custom_call" | custom-call | flops 1000000000 | bytes 2000000 | tf_op jit(solution)/shard_map/pallas_call | solution.py:430
  19.8 0.1 collective-permute-start.3
  19.8 1.2 %shard_map.133 = (f32[192,512]{1,0:T(8,128)S(1)}, f32[192,512]{1,0:T(8,128)S(1)}, bf16[512,512]{1,0:T(8,128)(2,1)S(1)}, bf16[512,512]{1,0:T(8,128)(2,1)S(1)}) custom-call(bf16[512,512]{1,0:T(8,128)(2,1)} %wn_hbm.3, bf16[512,512]{1,0:T(8,128)(2,1)} %ws_hbm.3, bf16[512,128]{1,0:T(8,128)(2,1)S(1)} %get-tuple-element.41.spread, ...), custom_call_target="tpu_custom_call" | custom-call | flops 1000000000 | bytes 3000000 | tf_op jit(solution)/shard_map/pallas_call | solution.py:430
  21.1 0.0 collective-permute-done.3.message
  21.1 0.0 collective-permute-done.2.message16
  21.1 1.7 %shard_map.134.base = f32[128,512]{1,0:T(8,128)S(1)} custom-call(f32[192,512]{1,0:T(8,128)S(1)} %get-tuple-element.43.last, f32[192,512]{1,0:T(8,128)S(1)} %get-tuple-element.44.early_pull, bf16[512,512]{1,0:T(8,128)(2,1)S(1)} %get-tuple-element.45.wn, bf16[512,512]{1,0:T(8,128)(2,1)S(1)} %get-tuple-element.46.ws, f32[1,512]{1,0:T(1,128)S(1)} %get-tuple-element.47.gain, ...), custom_call_target="tpu_custom_call" | custom-call | flops 603979776 | bytes 6000000 | tf_op jit(solution)/shard_map/pallas_call | solution.py:430
  22.8 0.0 collective-permute-done.4.before
  22.8 0.8 %shard_map.135 = f32[128,512]{1,0:T(8,128)} custom-call(f32[128,512]{1,0:T(8,128)S(1)} %shard_map.134.base, bf16[128,512]{1,0:T(8,128)(2,1)S(1)} %get-tuple-element.57.background, bf16[128,512]{1,0:T(8,128)(2,1)S(1)} %collective-permute-done.4.before, f32[1,512]{1,0:T(1,128)S(1)} %get-tuple-element.52.error), custom_call_target="tpu_custom_call" | custom-call | flops 1000000 | bytes 900000 | tf_op jit(solution)/shard_map/pallas_call | solution.py:430
  (2 shorter events, 0.1 us)
Async XLA Ops:
  0.0 2.4 %collective-permute-start = (f32[128,512]{1,0:T(8,128)}, f32[128,512]{1,0:T(8,128)S(1)}, u32[]{:S(2)}, u32[]{:S(2)}) collective-permute-start(f32[128,512]{1,0:T(8,128)} %bitcast.19), channel_id=1, source_target_pairs={{0,1},{1,0},{2,3},{3,2},{4,5},{5,4},{6,7},{7,6},{8,9},{9,8},{10,11... | collective-permute-start | bytes 786440 | tf_op jit(solution)/shard_map/ppermute | solution.py:485
  2.5 8.7 %collective-permute-start.1 = (bf16[144,512]{1,0:T(8,128)(2,1)S(1)}, bf16[144,512]{1,0:T(8,128)(2,1)S(1)}, u32[]{:S(2)}, u32[]{:S(2)}) collective-permute-start(bf16[144,512]{1,0:T(8,128)(2,1)S(1)} %shard_map.128.refs_5_), channel_id=1, source_target_pairs={{0,15},{1,2},{2,1},{3,4},{4,3},{5,6},{6,5},{7,8},{8,7},{9,10},{10,... | collective-permute-start | bytes 442376 | tf_op jit(solution)/shard_map/ppermute | solution.py:512
  7.6 11.4 %all-to-all-start = ((bf16[16,32,128]{2,1,0:T(8,128)(2,1)}), bf16[16,32,128]{2,1,0:T(8,128)(2,1)S(1)}, u32[]{:S(2)}, u32[]{:S(2)}) async-start(bf16[16,32,128]{2,1,0:T(8,128)(2,1)} %bitcast.9), calls=%async_computation | async-start | bytes 262144 | tf_op jit(solution)/shard_map/all_to_all | solution.py:523
  11.3 9.8 %collective-permute-start.2 = (bf16[160,512]{1,0:T(8,128)(2,1)S(1)}, bf16[160,512]{1,0:T(8,128)(2,1)S(1)}, u32[]{:S(2)}, u32[]{:S(2)}) collective-permute-start(bf16[160,512]{1,0:T(8,128)(2,1)S(1)} %get-tuple-element.49), channel_id=1, source_target_pairs={{16,0},{17,1},{18,2},{19,3},{20,4},{21,5},{22,6},{23,7},{24,8},{25... | collective-permute-start | bytes 491528 | tf_op jit(solution)/shard_map/ppermute | solution.py:483
  16.3 6.5 %collective-permute-start.4 = (bf16[128,512]{1,0:T(8,128)(2,1)S(1)}, bf16[128,512]{1,0:T(8,128)(2,1)S(1)}, u32[]{:S(2)}, u32[]{:S(2)}) collective-permute-start(bf16[128,512]{1,0:T(8,128)(2,1)S(1)} %get-tuple-element.58), channel_id=1, source_target_pairs={{16,0},{17,1},{18,2},{19,3},{20,4},{21,5},{22,6},{23,7},{24,8},{25... | collective-permute-start | bytes 393224 | tf_op jit(solution)/shard_map/ppermute | solution.py:483
  19.8 1.3 %collective-permute-start.3 = (bf16[128,128]{1,0:T(8,128)(2,1)S(1)}, bf16[128,128]{1,0:T(8,128)(2,1)S(1)}, u32[]{:S(2)}, u32[]{:S(2)}) collective-permute-start(bf16[128,128]{1,0:T(8,128)(2,1)S(1)} %get-tuple-element.53), channel_id=1, source_target_pairs={{0,1},{1,0},{2,3},{3,2},{4,5},{5,4},{6,7},{7,6},{8,9},{9,8},{10,11... | collective-permute-start | bytes 98312 | tf_op jit(solution)/shard_map/ppermute | solution.py:562

commit v3 on v2

--- a/solution.py
+++ b/solution.py
@@ -262,17 +262,38 @@
     return high, (x - high.astype(F32)).astype(BF16)
 
 
+def spread_of(first, th, tl, scaled, taken, field, ph, plo, spread):
+    lane = lax.broadcasted_iota(jnp.int32, (1, LANES), 1)
+    table_of = jnp.where(lane < SENDERS * SLOTS, lane % SLOTS // CAP, -1)
+    members = field.shape[1] // LANES
+    for p in range(th.shape[1] // LANES):
+        at = slice(p * LANES, (p + 1) * LANES)
+        for q in range(2):
+            kept = jnp.where(table_of == first + q, scaled[:, at], 0.0)
+            ph[q * 32 : (q + 1) * 32, at], plo[q * 32 : (q + 1) * 32, at] = split(kept)
+    cross = dot_t(ph[...], th[...]) + dot_t(plo[...], th[...]) + dot_t(ph[...], tl[...])
+    block = jnp.concatenate([cross] * 2, axis=1)
+    on_block = sublane(block.shape) // 32 == lax.broadcasted_iota(jnp.int32, block.shape, 1) // 32
+    target = dot(ph[...], taken[...]) + dot(plo[...], taken[...])
+    ch, cl = split(jnp.where(on_block, block, 0.0))
+    fh, fl = split(field[first * 32 : (first + 2) * 32])
+    mixed = dot(ch, fh) + dot(cl, fh) + dot(ch, fl)
+    for q in range(2):
+        for m in range(members):
+            start = (q * members + m) * 32
+            value = mixed[q * 32 : (q + 1) * 32, m * LANES : (m + 1) * LANES] - target[q * 32 : (q + 1) * 32]
+            spread[start : start + 32] = value.astype(BF16)
+
+
 def observe_kernel(
     tiles, arrived, field,
-    spread, message,
-    th, tl, ph, plo, vals, wide,
+    spread, message, th, tl, scaled, taken,
+    ph, plo, vals, wide,
 ):
     steps = 2
     members = field.shape[1] // LANES
     even = lax.rem(lax.axis_index("tile"), 2) == 0
     cells = sublane((32, LANES)).astype(F32)
-    lane = lax.broadcasted_iota(jnp.int32, (1, LANES), 1)
-    table_of = jnp.where(lane < SENDERS * SLOTS, lane % SLOTS // CAP, -1)
     wide[...] = arrived[...].astype(F32)
     vals[...] = jnp.zeros_like(vals)
     for p in range(th.shape[1] // LANES):
@@ -286,24 +307,9 @@
             weight += jnp.where(cells == meta[4 + i : 5 + i], meta[8 + i : 9 + i], 0.0)
         at = slice(p * LANES, (p + 1) * LANES)
         th[:, at], tl[:, at] = split(weight)
-        scaled = weight * meta[12:13]
-        for q in range(2 * steps):
-            kept = jnp.where(table_of == q, scaled, 0.0)
-            ph[q * 32 : (q + 1) * 32, at], plo[q * 32 : (q + 1) * 32, at] = split(kept)
-    cross = dot_t(ph[...], th[...]) + dot_t(plo[...], th[...]) + dot_t(ph[...], tl[...])
-    block = jnp.concatenate([cross] * (2 * steps), axis=1)
-    on_block = sublane(block.shape) // 32 == lax.broadcasted_iota(jnp.int32, block.shape, 1) // 32
-    cross = jnp.where(on_block, block, 0.0)
-    taken = vals[...].astype(BF16)
-    target = dot(ph[...], taken) + dot(plo[...], taken)
-    ch, cl = split(cross)
-    fh, fl = split(field[...])
-    mixed = dot(ch, fh) + dot(cl, fh) + dot(ch, fl)
-    for q in range(2 * steps):
-        for m in range(members):
-            start = (q * members + m) * 32
-            value = mixed[q * 32 : (q + 1) * 32, m * LANES : (m + 1) * LANES] - target[q * 32 : (q + 1) * 32]
-            spread[start : start + 32] = value.astype(BF16)
+        scaled[:, at] = weight * meta[12:13]
+    taken[...] = vals[...].astype(BF16)
+    spread_of(0, th, tl, scaled, taken, field, ph, plo, spread)
     size = members * 32
     for k in range(steps):
         for m in range(members):
@@ -314,9 +320,10 @@
             message[start : start + 16] = jnp.concatenate(near, axis=0).astype(BF16)
 
 
-def adjoint_step(u, cot, gb, gm, flat, d, out, gain, ws, wn, wo, members):
+def adjoint_step(u, s, cot, gb, gm, flat, d, out, gain, ws, wn, wo, members):
     both = 2 * SLIM
-    gb[...] = cot[...].astype(BF16)
+    for m in range(members):
+        gb[m * both : (m + 1) * both] = jnp.concatenate([cot(2 * m), cot(2 * m + 1)], axis=0).astype(BF16)
     flat[...] = dot_t(gb[...], wo[...])
     gb[...] = (flat[...] * d[...]).astype(BF16)
     gm[...] = dot_t(gb[...], wn[...])
@@ -329,12 +336,12 @@
             rows.append(gm[start : start + SLIM].astype(BF16).astype(F32))
         around = neighbours(rows)
         for lat in range(2):
-            start = base + lat * SLIM
-            x = u[start : start + SLIM]
-            s = inverse_rms(x)
-            scaled = gain * (flat[start : start + SLIM] + around[lat])
+            at = slice(base + lat * SLIM, base + (lat + 1) * SLIM)
+            x = u[at]
+            inverse = jnp.concatenate([s[at]] * (x.shape[1] // LANES), axis=1)
+            scaled = gain * (flat[at] + around[lat])
             inner = jnp.mean(x * scaled, axis=-1, keepdims=True)
-            out(2 * m + lat, cot[start : start + SLIM] + s * scaled - x * (s * s * s * inner))
+            out(2 * m + lat, cot(2 * m + lat) + inverse * (scaled - x * (inverse * inverse * inner)))
 
 
 def edges(nxt, size, edge, r):
@@ -352,65 +359,77 @@
 
 
 def pull_kernel(
-    wn_hbm, ws_hbm, spread, readout,
-    last, first, wn, ws,
-    pulled, sems,
+    wn_hbm, ws_hbm, spread_own, readout, th, tl, scaled, taken, field, control, edge0, message, f2x, error, u1x,
+    cot_own, cot_edge, add_own, add_edge, u0x, s0, s1, wn, ws,
+    ph, plo, spread, pulled, away, nxt, final, edge, sems,
 ):
     pairs = ((wn_hbm, wn), (ws_hbm, ws))
     copies = [pltpu.make_async_copy(source, to, sems.at[i]) for i, (source, to) in enumerate(pairs)]
     for copy in copies:
         copy.start()
-    size = pulled.shape[0] // 4
+    size = control.shape[0]
     even = lax.rem(lax.axis_index("tile"), 2) == 0
+    weight = jnp.where(lax.axis_index("slot") == lax.axis_size("slot") - 1, 0.0, 1.0) * error[...]
     row8 = sublane((8, 1))
-    pulled[...] = dot_t(spread[...], readout[...])
-    for k, out in enumerate((first, last)):
-        for r in range(size // 16):
-            start = k * size + r * 16
-            out[r * SLIM : r * SLIM + 16] = pulled[start : start + 16]
-            start += 2 * size
-            low = jnp.where(row8 < 4, pulled[start : start + 8], 0.0)
-            high = jnp.where(row8 >= 4, pulled[start + 8 : start + 16], 0.0)
-            out[r * SLIM + 16 : (r + 1) * SLIM] = jnp.where(even, high, low)
+    spread_of(2, th, tl, scaled, taken, field, ph, plo, spread)
+    pulled[...] = dot_t(spread_own[...], readout[...])
+    away[...] = dot_t(spread[...], readout[...])
+    nxt[...] = message[...].astype(F32)
+    final[...] = f2x[...].astype(F32)
+
+    def other_edge(k, r):
+        start = k * size + r * 16
+        low = jnp.where(row8 < 4, away[start : start + 8], 0.0)
+        high = jnp.where(row8 >= 4, away[start + 8 : start + 16], 0.0)
+        return jnp.where(even, high, low)
+
+    for r in range(size // 16):
+        a, b = r * 16, (r + 1) * 16
+        c, d, e = r * SLIM, r * SLIM + 16, (r + 1) * SLIM
+        cot_own[a:b] = pulled[size + a : size + b] - weight * (nxt[a:b] - final[c:d])
+        cot_edge[r * 8 : (r + 1) * 8] = other_edge(1, r) - weight * (edges(nxt, size, edge, r) - final[d:e])
+        add_own[a:b] = pulled[a:b]
+        add_edge[r * 8 : (r + 1) * 8] = other_edge(0, r)
+        u0x[c:d] = control[a:b]
+        u0x[d:e] = edge0[r * 8 : (r + 1) * 8]
+        for u, s in ((u0x, s0), (u1x, s1)):
+            s[c:e] = jnp.broadcast_to(inverse_rms(u[c:e]), (SLIM, LANES))
     for copy in copies:
         copy.wait()
 
 
 def backward_kernel(
-    last, early_pull, wn, ws, gain, control, edge0, message16, f2x, wo, readout, error, message,
-    u1x, d0x, d1x,
+    cot_own, cot_edge, add_own, add_edge, u0x, s0, s1, wn, ws, wo, gain, readout, error, message, u1x, d0x, d1x,
     result,
-    cot2, cot1, add, gb, gm, flat, mate_pull, edge, u0x, final, nxt,
+    cot1, gb, gm, flat, mate_pull, edge2, edge1,
 ):
     size = result.shape[0]
     members = size // 32
     even = lax.rem(lax.axis_index("tile"), 2) == 0
-    nxt[...] = message16[...].astype(F32)
-    weight = jnp.where(lax.axis_index("slot") == lax.axis_size("slot") - 1, 0.0, 1.0) * error[...]
     row8 = sublane((8, 1))
     mate_side = jnp.where(even, 1, 0) == jnp.where(row8 < 4, 1, 0)
     mate_pull[...] = dot_t(message[...], readout[...])
-    final[...] = f2x[...].astype(F32)
-    add[...] = early_pull[...]
     for r in range(2 * members):
-        a, b = r * SLIM, r * SLIM + 16
-        cot2[a:b] = last[a:b] - weight * (nxt[r * 16 : (r + 1) * 16] - final[a:b])
-        u0x[a:b] = control[r * 16 : (r + 1) * 16]
-        a, b = b, b + 8
-        start = size // 2 + r * 8
-        pulled = last[a:b] + jnp.where(mate_side, mate_pull[start : start + 8], 0.0)
-        cot2[a:b] = pulled - weight * (edges(nxt, size, edge, r) - final[a:b])
-        add[a:b] = early_pull[a:b] + jnp.where(mate_side, mate_pull[r * 8 : (r + 1) * 8], 0.0)
-        u0x[a:b] = edge0[r * 8 : (r + 1) * 8]
+        a, b, start = r * 8, (r + 1) * 8, size // 2 + r * 8
+        edge2[a:b] = cot_edge[a:b] + jnp.where(mate_side, mate_pull[start : start + 8], 0.0)
+        edge1[a:b] = add_edge[a:b] + jnp.where(mate_side, mate_pull[a:b], 0.0)
+
+    def joined(own, edge):
+        return lambda r: jnp.concatenate([own[r * 16 : (r + 1) * 16], edge[r * 8 : (r + 1) * 8]], axis=0)
+
+    added = joined(add_own, edge1)
+
     def keep(r, value):
-        cot1[r * SLIM : (r + 1) * SLIM] = value + add[r * SLIM : (r + 1) * SLIM]
+        cot1[r * SLIM : (r + 1) * SLIM] = value + added(r)
 
     def finish(r, value):
-        a, b = r * SLIM, r * SLIM + 16
-        result[r * 16 : (r + 1) * 16] = value[0:16] + error[...] * u0x[a:b]
-
-    adjoint_step(u1x, cot2, gb, gm, flat, d1x, keep, gain[...], ws, wn, wo, members)
-    adjoint_step(u0x, cot1, gb, gm, flat, d0x, finish, gain[...], ws, wn, wo, members)
+        result[r * 16 : (r + 1) * 16] = value[0:16] + error[...] * u0x[r * SLIM : r * SLIM + 16]
+
+    def kept(r):
+        return cot1[r * SLIM : (r + 1) * SLIM]
+
+    adjoint_step(u1x, s1, joined(cot_own, edge2), gb, gm, flat, d1x, keep, gain[...], ws, wn, wo, members)
+    adjoint_step(u0x, s0, kept, gb, gm, flat, d0x, finish, gain[...], ws, wn, wo, members)
 
 
 def last_kernel(base, background, before, error, result):
@@ -551,34 +570,38 @@
     )
     before = across(final, -1)
     total = -(-tiles // SENDERS) * LANES
-    spread, near_spread = kernel_call(
+    tables = [scratch(64, BF16, total), scratch(64, BF16, total)]
+    spread, near_spread, *reports_held = kernel_call(
         functools.partial(observe_kernel, tiles),
-        [spec(4 * size, BF16, LANES), spec(size, BF16, LANES)],
-        [scratch(32, BF16, total)] * 2 + [scratch(128, BF16, total)] * 2
-        + [scratch(total, F32, LANES), scratch(tiles * CHUNK, F32, LANES)],
+        [spec(2 * size, BF16, LANES), spec(size, BF16, LANES)]
+        + [spec(32, BF16, total), spec(32, BF16, total), spec(32, F32, total), spec(total, BF16, LANES)],
+        tables + [scratch(total, F32, LANES), scratch(tiles * CHUNK, F32, LANES)],
         10**9,
         2000000,
     )(arrived, field)
     from_mate = lax.ppermute(near_spread, "tile", mate_of)
     handed = kernel_call(
         pull_kernel,
-        [spec(slim), spec(slim), spec(channels, BF16), spec(channels, BF16)],
-        [scratch(4 * size), pltpu.SemaphoreType.DMA((2,))],
+        [spec(size), spec(size // 2), spec(size), spec(size // 2), spec(slim), spec(slim, F32, LANES)]
+        + [spec(slim, F32, LANES), spec(channels, BF16), spec(channels, BF16)],
+        tables
+        + [scratch(2 * size, BF16, LANES), scratch(2 * size), scratch(2 * size), scratch(size + 4 * groups)]
+        + [scratch(slim), scratch(16), pltpu.SemaphoreType.DMA((2,))],
         10**9,
         3000000,
         hbm=2,
-    )(neighbour_weight, self_weight, spread, readout_held)
+    )(
+        neighbour_weight, self_weight, spread, readout_held, *reports_held, field, held, edge0, nxt, f2x,
+        error_held, u1x,
+    )
     base = kernel_call(
         backward_kernel,
         spec(size),
-        [scratch(slim), scratch(slim), scratch(slim), scratch(slim, BF16), scratch(slim), scratch(slim)]
-        + [scratch(size), scratch(16), scratch(slim), scratch(slim), scratch(size + 4 * groups)],
+        [scratch(slim), scratch(slim, BF16), scratch(slim), scratch(slim), scratch(size)]
+        + [scratch(size // 2), scratch(size // 2)],
         12 * slim * channels * channels,
         6000000,
-    )(
-        *handed, gain_held, held, edge0, nxt, f2x, wo, readout_held, error_held, from_mate,
-        u1x, d0x, d1x,
-    )
+    )(*handed, wo, gain_held, readout_held, error_held, from_mate, u1x, d0x, d1x)
     result = kernel_call(last_kernel, spec(size), [], 10**6, 900000)(base, background_held, before, error_held)
     return result.reshape(control.shape)
 

time: 23.8 us -> 24 us (level)
  no operation moved by 1% of the time
where the time goes in v3:
time: 24 us; the launch traced here: 23.7 us
  starting transfers between devices  11.3 us (47%)
  Pallas kernels  10.1 us (42%)
  waiting for transfers between devices  2.17 us (9%)
    pallas_call x9, Pallas kernels, call(): pl.pallas_call(body, out_shape=outs, in_specs=[pl.BlockSpec(memory_space=...  10.1 us
    ppermute x1, starting transfers between devices, per_device(): oth = lax.ppermute(sent, 'tile', other_of)  5.11 us
    all_to_all x1, starting transfers between devices, per_device(): lax.all_to_all(packed, 'tile', split_axis=0, concat_axis=0, tiled=True)  3.52 us
    all_to_all x1, waiting for transfers between devices, per_device(): lax.all_to_all(packed, 'tile', split_axis=0, concat_axis=0, tiled=True)  2.16 us
    ppermute x2, starting transfers between devices, across(): return lax.ppermute(block, ('slot', 'tile'), pairs)  2.16 us
  transfers between devices with their start and end apart: 6, of which 1 were waited for; matrix products, arithmetic and copies ran while one was open for 0% of the time, Pallas kernels for 39%

profile of v3, /device:TPU:0, one launch (start us, length us, event | category | flops | bytes accessed | tf_op | source)
XLA Modules:
  0.0 23.7 jit_solution(14055232421192184705)
XLA Ops:
  0.0 0.5 %collective-permute-start = (f32[128,512]{1,0:T(8,128)}, f32[128,512]{1,0:T(8,128)S(1)}, u32[]{:S(2)}, u32[]{:S(2)}) collective-permute-start(f32[128,512]{1,0:T(8,128)} %bitcast.19), channel_id=1, source_target_pairs={{0,1},{1,0},{2,3},{3,2},{4,5},{5,4},{6,7},{7,6},{8,9},{9,8},{10,11... | collective-permute-start | bytes 786440 | tf_op jit(solution)/shard_map/ppermute | solution.py:504
  0.5 2.0 %shard_map.127 = (f32[128,512]{1,0:T(8,128)S(1)}, bf16[512,128]{1,0:T(8,128)(2,1)}, s32[2,1,32]{2,1,0:T(1,128)S(1)}, s32[2,4,32]{2,1,0:T(4,128)S(1)}, bf16[2,4,3...) custom-call(f32[128,512]{1,0:T(8,128)} %bitcast.20, s32[2,1,32]{2,1,0:T(1,128)} %bitcast.24, ...), custom_call_target="tpu_custom_call" | custom-call | flops 10000000 | bytes 200000 | tf_op jit(solution)/shard_map/pallas_call | solution.py:449
  2.4 0.0 collective-permute-done.mate
  2.5 5.1 %collective-permute-start.1 = (bf16[144,512]{1,0:T(8,128)(2,1)S(1)}, bf16[144,512]{1,0:T(8,128)(2,1)S(1)}, u32[]{:S(2)}, u32[]{:S(2)}) collective-permute-start(bf16[144,512]{1,0:T(8,128)(2,1)S(1)} %shard_map.128.refs_5_), channel_id=1, source_target_pairs={{0,15},{1,2},{2,1},{3,4},{4,3},{5,6},{6,5},{7,8},{8,7},{9,10},{10,... | collective-permute-start | bytes 442376 | tf_op jit(solution)/shard_map/ppermute | solution.py:531
  7.6 3.5 %all-to-all-start = ((bf16[16,32,128]{2,1,0:T(8,128)(2,1)}), bf16[16,32,128]{2,1,0:T(8,128)(2,1)S(1)}, u32[]{:S(2)}, u32[]{:S(2)}) async-start(bf16[16,32,128]{2,1,0:T(8,128)(2,1)} %bitcast.9), calls=%async_computation | async-start | bytes 262144 | tf_op jit(solution)/shard_map/all_to_all | solution.py:542
  11.2 0.0 collective-permute-done.1.oth
  11.2 0.1 shard_map.130
  11.3 1.6 %collective-permute-start.2 = (bf16[160,512]{1,0:T(8,128)(2,1)S(1)}, bf16[160,512]{1,0:T(8,128)(2,1)S(1)}, u32[]{:S(2)}, u32[]{:S(2)}) collective-permute-start(bf16[160,512]{1,0:T(8,128)(2,1)S(1)} %get-tuple-element.57), channel_id=1, source_target_pairs={{16,0},{17,1},{18,2},{19,3},{20,4},{21,5},{22,6},{23,7},{24,8},{25... | collective-permute-start | bytes 491528 | tf_op jit(solution)/shard_map/ppermute | solution.py:502
  12.8 3.5 %shard_map.131 = (f32[64,512]{1,0:T(8,128)S(1)}, f32[192,512]{1,0:T(8,128)S(1)}, bf16[192,512]{1,0:T(8,128)(2,1)S(1)}, bf16[192,512]{1,0:T(8,128)(2,1)S(1)}, bf1...) custom-call(f32[1,512]{1,0:T(1,128)} %bitcast.27, ...), custom_call_target="tpu_custom_call" | custom-call | flops 99999997952 | bytes 4000000 | tf_op jit(solution)/shard_map/pallas_call | solution.py:449
  16.3 0.6 %collective-permute-start.4 = (bf16[128,512]{1,0:T(8,128)(2,1)S(1)}, bf16[128,512]{1,0:T(8,128)(2,1)S(1)}, u32[]{:S(2)}, u32[]{:S(2)}) collective-permute-start(bf16[128,512]{1,0:T(8,128)(2,1)S(1)} %get-tuple-element.76), channel_id=1, source_target_pairs={{16,0},{17,1},{18,2},{19,3},{20,4},{21,5},{22,6},{23,7},{24,8},{25... | collective-permute-start | bytes 393224 | tf_op jit(solution)/shard_map/ppermute | solution.py:502
  16.9 2.2 %all-to-all-done = bf16[16,32,128]{2,1,0:T(8,128)(2,1)S(1)} async-done(((bf16[16,32,128]{2,1,0:T(8,128)(2,1)}), bf16[16,32,128]{2,1,0:T(8,128)(2,1)S(1)}, u32[]{:S(2)}, u32[]{:S(2)}) %all-to-all-start) | async-done | bytes 131104 | tf_op jit(solution)/shard_map/all_to_all | solution.py:542
  19.1 0.5 %shard_map.132 = (bf16[256,128]{1,0:T(8,128)(2,1)S(1)}, bf16[128,128]{1,0:T(8,128)(2,1)S(1)}, bf16[32,384]{1,0:T(8,128)(2,1)S(1)}, bf16[32,384]{1,0:T(8,128)(2,1...) custom-call(bf16[512,128]{1,0:T(8,128)(2,1)S(1)} %bitcast.18, f32[128,512]{1,0:T(8,128)S(1)} %get-tuple-element.49.field), custom_call_target="tpu_custom_call" | custom-call | flops 1000000000 | bytes 2000000 | tf_op jit(solution)/shard_map/pallas_call | solution.py:449
  19.6 0.1 collective-permute-start.3
  19.6 0.0 collective-permute-done.2.message
  19.7 1.6 %shard_map.133 = (f32[128,512]{1,0:T(8,128)S(1)}, f32[64,512]{1,0:T(8,128)S(1)}, f32[128,512]{1,0:T(8,128)S(1)}, f32[64,512]{1,0:T(8,128)S(1)}, f32[192,512]{1,0...) custom-call(bf16[512,512]{1,0:T(8,128)(2,1)} %wn_hbm.3, ...), custom_call_target="tpu_custom_call" | custom-call | flops 1000000000 | bytes 3000000 | tf_op jit(solution)/shard_map/pallas_call | solution.py:449
  21.3 0.0 collective-permute-done.3.message
  21.3 1.7 %shard_map.134.base = f32[128,512]{1,0:T(8,128)S(1)} custom-call(f32[128,512]{1,0:T(8,128)S(1)} %get-tuple-element.61.cot_own, f32[64,512]{1,0:T(8,128)S(1)} %get-tuple-element.62.cot_edge, f32[128,512]{1,0:T(8,128)S(1)} %get-tuple-element.63.add_own, f32[64,512]{1,0:T(8,128)S(1)} %get-tuple-element.64.add_edge, f32[192,512]{1,0:T(8,128)S(1)} %get-tuple-element.65.u0x, ...), custom_call_target="tpu_custom_call" | custom-call | flops 603979776 | bytes 6000000 | tf_op jit(solution)/shard_map/pallas_call | solution.py:449
  23.0 0.0 collective-permute-done.4.before
  23.0 0.8 %shard_map.135 = f32[128,512]{1,0:T(8,128)} custom-call(f32[128,512]{1,0:T(8,128)S(1)} %shard_map.134.base, bf16[128,512]{1,0:T(8,128)(2,1)S(1)} %get-tuple-element.75.background, bf16[128,512]{1,0:T(8,128)(2,1)S(1)} %collective-permute-done.4.before, f32[1,512]{1,0:T(1,128)S(1)} %get-tuple-element.59.error), custom_call_target="tpu_custom_call" | custom-call | flops 1000000 | bytes 900000 | tf_op jit(solution)/shard_map/pallas_call | solution.py:449
  (2 shorter events, 0.1 us)
Async XLA Ops:
  0.0 2.4 %collective-permute-start = (f32[128,512]{1,0:T(8,128)}, f32[128,512]{1,0:T(8,128)S(1)}, u32[]{:S(2)}, u32[]{:S(2)}) collective-permute-start(f32[128,512]{1,0:T(8,128)} %bitcast.19), channel_id=1, source_target_pairs={{0,1},{1,0},{2,3},{3,2},{4,5},{5,4},{6,7},{7,6},{8,9},{9,8},{10,11... | collective-permute-start | bytes 786440 | tf_op jit(solution)/shard_map/ppermute | solution.py:504
  2.5 8.7 %collective-permute-start.1 = (bf16[144,512]{1,0:T(8,128)(2,1)S(1)}, bf16[144,512]{1,0:T(8,128)(2,1)S(1)}, u32[]{:S(2)}, u32[]{:S(2)}) collective-permute-start(bf16[144,512]{1,0:T(8,128)(2,1)S(1)} %shard_map.128.refs_5_), channel_id=1, source_target_pairs={{0,15},{1,2},{2,1},{3,4},{4,3},{5,6},{6,5},{7,8},{8,7},{9,10},{10,... | collective-permute-start | bytes 442376 | tf_op jit(solution)/shard_map/ppermute | solution.py:531
  7.6 11.4 %all-to-all-start = ((bf16[16,32,128]{2,1,0:T(8,128)(2,1)}), bf16[16,32,128]{2,1,0:T(8,128)(2,1)S(1)}, u32[]{:S(2)}, u32[]{:S(2)}) async-start(bf16[16,32,128]{2,1,0:T(8,128)(2,1)} %bitcast.9), calls=%async_computation | async-start | bytes 262144 | tf_op jit(solution)/shard_map/all_to_all | solution.py:542
  11.3 8.4 %collective-permute-start.2 = (bf16[160,512]{1,0:T(8,128)(2,1)S(1)}, bf16[160,512]{1,0:T(8,128)(2,1)S(1)}, u32[]{:S(2)}, u32[]{:S(2)}) collective-permute-start(bf16[160,512]{1,0:T(8,128)(2,1)S(1)} %get-tuple-element.57), channel_id=1, source_target_pairs={{16,0},{17,1},{18,2},{19,3},{20,4},{21,5},{22,6},{23,7},{24,8},{25... | collective-permute-start | bytes 491528 | tf_op jit(solution)/shard_map/ppermute | solution.py:502
  16.3 6.7 %collective-permute-start.4 = (bf16[128,512]{1,0:T(8,128)(2,1)S(1)}, bf16[128,512]{1,0:T(8,128)(2,1)S(1)}, u32[]{:S(2)}, u32[]{:S(2)}) collective-permute-start(bf16[128,512]{1,0:T(8,128)(2,1)S(1)} %get-tuple-element.76), channel_id=1, source_target_pairs={{16,0},{17,1},{18,2},{19,3},{20,4},{21,5},{22,6},{23,7},{24,8},{25... | collective-permute-start | bytes 393224 | tf_op jit(solution)/shard_map/ppermute | solution.py:502
  19.6 1.7 %collective-permute-start.3 = (bf16[128,128]{1,0:T(8,128)(2,1)S(1)}, bf16[128,128]{1,0:T(8,128)(2,1)S(1)}, u32[]{:S(2)}, u32[]{:S(2)}) collective-permute-start(bf16[128,128]{1,0:T(8,128)(2,1)S(1)} %get-tuple-element.72), channel_id=1, source_target_pairs={{0,1},{1,0},{2,3},{3,2},{4,5},{5,4},{6,7},{7,6},{8,9},{9,8},{10,11... | collective-permute-start | bytes 98312 | tf_op jit(solution)/shard_map/ppermute | solution.py:582

commit v4 on v2

--- a/solution.py
+++ b/solution.py
@@ -12,8 +12,8 @@
 LANES = 128
 CAP = 5
 SLOTS = 4 * CAP
-CHUNK = 32
-META = 16
+CHUNK = 24
+STRIDE = 32
 SENDERS = LANES // SLOTS
 WIDE = 40
 SLIM = 24
@@ -129,11 +129,18 @@
         reports(arrays, out_hbm, key, meta, picked, out, sem)
 
 
+def fan(x, shift):
+    if shift % LANES:
+        x = pltpu.roll(x, shift % LANES, 1)
+    for _ in range(2):
+        x = pltpu.roll(x, 0, 1, stride=SLOTS // 2, stride_axis=0)
+    return x
+
+
 def pack(owner, stencil, weights, precision, values, out, key, meta, picked):
     steps, _, rows = owner.shape
     tiles = out.shape[0] // CHUNK
     total = steps * rows
-    place = lax.axis_index("tile") % SENDERS * SLOTS
     earlier = lax.broadcasted_iota(jnp.int32, (rows, rows), 0) < lax.broadcasted_iota(jnp.int32, (rows, rows), 1)
     earlier = earlier.astype(F32).astype(BF16)
     meta[...] = jnp.zeros_like(meta)
@@ -144,28 +151,31 @@
         before = dot(hits.astype(BF16), earlier)
         rank = jnp.sum(hits * before, axis=0, keepdims=True).astype(jnp.int32)
         key[0:1, at] = owner[k] * (2 * CAP) + k * CAP + rank
-        meta[4:8, at] = stencil[k].astype(F32)
-        meta[8:12, at] = weights[k].astype(F32)
-        meta[12:13, at] = precision[k : k + 1].astype(F32)
-    row = lax.broadcasted_iota(jnp.int32, (tiles * CHUNK, total), 0)
-    tile = row // CHUNK
-    slot = row % CHUNK
+        meta[0:4, at] = stencil[k].astype(F32)
+        meta[4:6, at] = weights[k, 0:2].astype(F32)
+        meta[8:10, at] = weights[k, 2:4].astype(F32)
+        meta[10:11, at] = precision[k : k + 1].astype(F32)
+    row = lax.broadcasted_iota(jnp.int32, (tiles * STRIDE, total), 0)
+    tile = row // STRIDE
+    slot = row % STRIDE
     other = jnp.where(tile % 2 == 0, (tile + tiles - 1) % tiles, (tile + 1) % tiles)
     mine = slot < 2 * CAP
     wanted = jnp.where(mine, tile * (2 * CAP) + slot, other * (2 * CAP) + slot - 2 * CAP)
     wanted = jnp.where(slot < SLOTS, wanted, -1)
     placement = (wanted == key[...]).astype(F32).astype(BF16)
-    picked[...] = dot(placement, values[...])
+    placed = dot(placement, values[...])
     entries = dot_t(meta[...].astype(BF16), placement)
-    lane = lax.broadcasted_iota(jnp.int32, (META, LANES), 1)
-    used = jnp.logical_and(lane >= place, lane < place + SLOTS)
-    per_tile = LANES // CHUNK
+    lane = lax.broadcasted_iota(jnp.int32, (16, LANES), 1)
+    per_tile = LANES // STRIDE
     for t in range(tiles):
-        block = entries[:, t // per_tile * LANES : (t // per_tile + 1) * LANES]
-        shift = (place + LANES - t % per_tile * CHUNK) % LANES
-        block = jnp.where(used, pltpu.roll(block, shift, 1), 0.0)
-        low = picked[t * CHUNK + 16 : (t + 1) * CHUNK]
-        picked[t * CHUNK + 16 : (t + 1) * CHUNK] = jnp.where(sublane((META, 1)) < 4, low, block)
+        picked[t * CHUNK : (t + 1) * CHUNK] = placed[t * STRIDE : t * STRIDE + CHUNK]
+        start = t % per_tile * STRIDE
+        used = jnp.logical_and(lane >= start, lane < start + SLOTS)
+        block = jnp.where(used, entries[:, t // per_tile * LANES : (t // per_tile + 1) * LANES], 0.0)
+        for j in range(2):
+            spread = fan(block[j * 8 : (j + 1) * 8], LANES - start)
+            row = t * CHUNK + SLOTS + j
+            picked[row : row + 1] = jnp.sum(spread, axis=0, keepdims=True)
     out[...] = picked[...].astype(BF16)
 
 
@@ -262,48 +272,62 @@
     return high, (x - high.astype(F32)).astype(BF16)
 
 
+def spread_of(first, th, tl, scaled, taken, field, ph, plo, spread):
+    lane = lax.broadcasted_iota(jnp.int32, (1, LANES), 1)
+    table_of = jnp.where(lane < SENDERS * SLOTS, lane % SLOTS // CAP, -1)
+    members = field.shape[1] // LANES
+    for p in range(th.shape[1] // LANES):
+        at = slice(p * LANES, (p + 1) * LANES)
+        for q in range(2):
+            kept = jnp.where(table_of == first + q, scaled[:, at], 0.0)
+            ph[q * 32 : (q + 1) * 32, at], plo[q * 32 : (q + 1) * 32, at] = split(kept)
+    cross = dot_t(ph[...], th[...]) + dot_t(plo[...], th[...]) + dot_t(ph[...], tl[...])
+    block = jnp.concatenate([cross] * 2, axis=1)
+    on_block = sublane(block.shape) // 32 == lax.broadcasted_iota(jnp.int32, block.shape, 1) // 32
+    target = dot(ph[...], taken[...]) + dot(plo[...], taken[...])
+    ch, cl = split(jnp.where(on_block, block, 0.0))
+    fh, fl = split(field[first * 32 : (first + 2) * 32])
+    mixed = dot(ch, fh) + dot(cl, fh) + dot(ch, fl)
+    for q in range(2):
+        for m in range(members):
+            start = (q * members + m) * 32
+            value = mixed[q * 32 : (q + 1) * 32, m * LANES : (m + 1) * LANES] - target[q * 32 : (q + 1) * 32]
+            spread[start : start + 32] = value.astype(BF16)
+
+
 def observe_kernel(
     tiles, arrived, field,
-    spread, message,
-    th, tl, ph, plo, vals, wide,
+    spread, message, th, tl, scaled, taken,
+    ph, plo, vals, wide,
 ):
     steps = 2
     members = field.shape[1] // LANES
     even = lax.rem(lax.axis_index("tile"), 2) == 0
     cells = sublane((32, LANES)).astype(F32)
-    lane = lax.broadcasted_iota(jnp.int32, (1, LANES), 1)
-    table_of = jnp.where(lane < SENDERS * SLOTS, lane % SLOTS // CAP, -1)
+    lane = lax.broadcasted_iota(jnp.int32, (8, LANES), 1)
     wide[...] = arrived[...].astype(F32)
     vals[...] = jnp.zeros_like(vals)
     for p in range(th.shape[1] // LANES):
-        meta = jnp.zeros((META, LANES), F32)
+        meta = [jnp.zeros((8, LANES), F32)] * 2
         for d in range(p * SENDERS, min((p + 1) * SENDERS, tiles)):
-            meta += wide[d * CHUNK + 16 : (d + 1) * CHUNK]
-            start = p * LANES + d % SENDERS * SLOTS
+            start = d % SENDERS * SLOTS
+            used = jnp.logical_and(lane >= start, lane < start + SLOTS)
+            for j in range(2):
+                row = d * CHUNK + SLOTS + j
+                rows = jnp.broadcast_to(wide[row : row + 1], (8, LANES))
+                turned = fan(rows, start + LANES - 5 * SLOTS)
+                meta[j] = meta[j] + jnp.where(used, turned, 0.0)
+            start += p * LANES
             vals[start : start + SLOTS] = wide[d * CHUNK : d * CHUNK + SLOTS]
+        entry = [meta[i // 6][5 - i % 6 : 6 - i % 6] for i in range(9)]
         weight = jnp.zeros((32, LANES), F32)
         for i in range(4):
-            weight += jnp.where(cells == meta[4 + i : 5 + i], meta[8 + i : 9 + i], 0.0)
+            weight += jnp.where(cells == entry[i], entry[4 + i], 0.0)
         at = slice(p * LANES, (p + 1) * LANES)
         th[:, at], tl[:, at] = split(weight)
-        scaled = weight * meta[12:13]
-        for q in range(2 * steps):
-            kept = jnp.where(table_of == q, scaled, 0.0)
-            ph[q * 32 : (q + 1) * 32, at], plo[q * 32 : (q + 1) * 32, at] = split(kept)
-    cross = dot_t(ph[...], th[...]) + dot_t(plo[...], th[...]) + dot_t(ph[...], tl[...])
-    block = jnp.concatenate([cross] * (2 * steps), axis=1)
-    on_block = sublane(block.shape) // 32 == lax.broadcasted_iota(jnp.int32, block.shape, 1) // 32
-    cross = jnp.where(on_block, block, 0.0)
-    taken = vals[...].astype(BF16)
-    target = dot(ph[...], taken) + dot(plo[...], taken)
-    ch, cl = split(cross)
-    fh, fl = split(field[...])
-    mixed = dot(ch, fh) + dot(cl, fh) + dot(ch, fl)
-    for q in range(2 * steps):
-        for m in range(members):
-            start = (q * members + m) * 32
-            value = mixed[q * 32 : (q + 1) * 32, m * LANES : (m + 1) * LANES] - target[q * 32 : (q + 1) * 32]
-            spread[start : start + 32] = value.astype(BF16)
+        scaled[:, at] = weight * entry[8]
+    taken[...] = vals[...].astype(BF16)
+    spread_of(0, th, tl, scaled, taken, field, ph, plo, spread)
     size = members * 32
     for k in range(steps):
         for m in range(members):
@@ -352,25 +376,26 @@
 
 
 def pull_kernel(
-    wn_hbm, ws_hbm, spread, readout,
+    wn_hbm, ws_hbm, spread_own, readout, th, tl, scaled, taken, field,
     last, first, wn, ws,
-    pulled, sems,
+    ph, plo, spread, pulled, away, sems,
 ):
     pairs = ((wn_hbm, wn), (ws_hbm, ws))
     copies = [pltpu.make_async_copy(source, to, sems.at[i]) for i, (source, to) in enumerate(pairs)]
     for copy in copies:
         copy.start()
-    size = pulled.shape[0] // 4
+    size = pulled.shape[0] // 2
     even = lax.rem(lax.axis_index("tile"), 2) == 0
     row8 = sublane((8, 1))
-    pulled[...] = dot_t(spread[...], readout[...])
+    spread_of(2, th, tl, scaled, taken, field, ph, plo, spread)
+    pulled[...] = dot_t(spread_own[...], readout[...])
+    away[...] = dot_t(spread[...], readout[...])
     for k, out in enumerate((first, last)):
         for r in range(size // 16):
             start = k * size + r * 16
             out[r * SLIM : r * SLIM + 16] = pulled[start : start + 16]
-            start += 2 * size
-            low = jnp.where(row8 < 4, pulled[start : start + 8], 0.0)
-            high = jnp.where(row8 >= 4, pulled[start + 8 : start + 16], 0.0)
+            low = jnp.where(row8 < 4, away[start : start + 8], 0.0)
+            high = jnp.where(row8 >= 4, away[start + 8 : start + 16], 0.0)
             out[r * SLIM + 16 : (r + 1) * SLIM] = jnp.where(even, high, low)
     for copy in copies:
         copy.wait()
@@ -492,7 +517,7 @@
     )
     work = [
         pltpu.VMEM((1, steps * rows), jnp.int32),
-        scratch(META, F32, steps * rows),
+        scratch(16, F32, steps * rows),
         scratch(tiles * CHUNK, F32, LANES),
         scratch(tiles * CHUNK, BF16, LANES),
     ]
@@ -551,11 +576,12 @@
     )
     before = across(final, -1)
     total = -(-tiles // SENDERS) * LANES
-    spread, near_spread = kernel_call(
+    tables = [scratch(64, BF16, total), scratch(64, BF16, total)]
+    spread, near_spread, *reports_held = kernel_call(
         functools.partial(observe_kernel, tiles),
-        [spec(4 * size, BF16, LANES), spec(size, BF16, LANES)],
-        [scratch(32, BF16, total)] * 2 + [scratch(128, BF16, total)] * 2
-        + [scratch(total, F32, LANES), scratch(tiles * CHUNK, F32, LANES)],
+        [spec(2 * size, BF16, LANES), spec(size, BF16, LANES)]
+        + [spec(32, BF16, total), spec(32, BF16, total), spec(32, F32, total), spec(total, BF16, LANES)],
+        tables + [scratch(total, F32, LANES), scratch(tiles * CHUNK, F32, LANES)],
         10**9,
         2000000,
     )(arrived, field)
@@ -563,11 +589,12 @@
     handed = kernel_call(
         pull_kernel,
         [spec(slim), spec(slim), spec(channels, BF16), spec(channels, BF16)],
-        [scratch(4 * size), pltpu.SemaphoreType.DMA((2,))],
+        tables
+        + [scratch(2 * size, BF16, LANES), scratch(2 * size), scratch(2 * size), pltpu.SemaphoreType.DMA((2,))],
         10**9,
         3000000,
         hbm=2,
-    )(neighbour_weight, self_weight, spread, readout_held)
+    )(neighbour_weight, self_weight, spread, readout_held, *reports_held, field)
     base = kernel_call(
         backward_kernel,
         spec(size),

time: 23.8 us -> 23.5 us (0.987)
  waiting for transfers between devices: 2.17 us -> 1.65 us
  Pallas kernels: 9.94 us -> 10.3 us
    all_to_all x1, waiting for transfers between devices: 2.16 us -> 1.64 us  [per_device(): lax.all_to_all(packed, 'tile', split_axis=0, concat_axis=0, tiled=True)]
    pallas_call x9, Pallas kernels: 9.94 us -> 10.3 us  [call(): pl.pallas_call(body, out_shape=outs, in_specs=[pl.BlockSpec(memory_space=...]
  transfers between devices with their start and end apart: 6 -> 6, of which waited for: 1 -> 1; matrix products, arithmetic and copies ran while one was open for 0% -> 0% of each run, Pallas kernels for 39% -> 41%
where the time goes in v4:
time: 23.5 us; the launch traced here: 23.2 us
  starting transfers between devices  11.2 us (48%)
  Pallas kernels  10.3 us (44%)
  waiting for transfers between devices  1.65 us (7%)
    pallas_call x9, Pallas kernels, call(): pl.pallas_call(body, out_shape=outs, in_specs=[pl.BlockSpec(memory_space=...  10.3 us
    ppermute x1, starting transfers between devices, per_device(): oth = lax.ppermute(sent, 'tile', other_of)  4.97 us
    all_to_all x1, starting transfers between devices, per_device(): lax.all_to_all(packed, 'tile', split_axis=0, concat_axis=0, tiled=True)  3.52 us
    ppermute x2, starting transfers between devices, across(): return lax.ppermute(block, ('slot', 'tile'), pairs)  2.15 us
    all_to_all x1, waiting for transfers between devices, per_device(): lax.all_to_all(packed, 'tile', split_axis=0, concat_axis=0, tiled=True)  1.64 us
  transfers between devices with their start and end apart: 6, of which 1 were waited for; matrix products, arithmetic and copies ran while one was open for 0% of the time, Pallas kernels for 41%

profile of v4, /device:TPU:0, one launch (start us, length us, event | category | flops | bytes accessed | tf_op | source)
XLA Modules:
  0.0 23.2 jit_solution(16993681277606621467)
XLA Ops:
  0.0 0.5 %collective-permute-start = (f32[128,512]{1,0:T(8,128)}, f32[128,512]{1,0:T(8,128)S(1)}, u32[]{:S(2)}, u32[]{:S(2)}) collective-permute-start(f32[128,512]{1,0:T(8,128)} %bitcast.19), channel_id=1, source_target_pairs={{0,1},{1,0},{2,3},{3,2},{4,5},{5,4},{6,7},{7,6},{8,9},{9,8},{10,11... | collective-permute-start | bytes 786440 | tf_op jit(solution)/shard_map/ppermute | solution.py:510
  0.5 2.1 %shard_map.127 = (f32[128,512]{1,0:T(8,128)S(1)}, bf16[384,128]{1,0:T(8,128)(2,1)}, s32[2,1,32]{2,1,0:T(1,128)S(1)}, s32[2,4,32]{2,1,0:T(4,128)S(1)}, bf16[2,4,3...) custom-call(f32[128,512]{1,0:T(8,128)} %bitcast.20, s32[2,1,32]{2,1,0:T(1,128)} %bitcast.24, ...), custom_call_target="tpu_custom_call" | custom-call | flops 10000000 | bytes 200000 | tf_op jit(solution)/shard_map/pallas_call | solution.py:455
  2.6 0.0 collective-permute-done.mate
  2.6 5.0 %collective-permute-start.1 = (bf16[144,512]{1,0:T(8,128)(2,1)S(1)}, bf16[144,512]{1,0:T(8,128)(2,1)S(1)}, u32[]{:S(2)}, u32[]{:S(2)}) collective-permute-start(bf16[144,512]{1,0:T(8,128)(2,1)S(1)} %shard_map.128.refs_5_), channel_id=1, source_target_pairs={{0,15},{1,2},{2,1},{3,4},{4,3},{5,6},{6,5},{7,8},{8,7},{9,10},{10,... | collective-permute-start | bytes 442376 | tf_op jit(solution)/shard_map/ppermute | solution.py:537
  7.6 3.5 %all-to-all-start = ((bf16[16,24,128]{2,1,0:T(8,128)(2,1)}), bf16[16,24,128]{2,1,0:T(8,128)(2,1)S(1)}, u32[]{:S(2)}, u32[]{:S(2)}) async-start(bf16[16,24,128]{2,1,0:T(8,128)(2,1)} %bitcast.9), calls=%async_computation | async-start | bytes 196608 | tf_op jit(solution)/shard_map/all_to_all | solution.py:548
  11.1 0.0 collective-permute-done.1.oth
  11.2 0.1 shard_map.130
  11.3 1.6 %collective-permute-start.2 = (bf16[160,512]{1,0:T(8,128)(2,1)S(1)}, bf16[160,512]{1,0:T(8,128)(2,1)S(1)}, u32[]{:S(2)}, u32[]{:S(2)}) collective-permute-start(bf16[160,512]{1,0:T(8,128)(2,1)S(1)} %get-tuple-element.57), channel_id=1, source_target_pairs={{16,0},{17,1},{18,2},{19,3},{20,4},{21,5},{22,6},{23,7},{24,8},{25... | collective-permute-start | bytes 491528 | tf_op jit(solution)/shard_map/ppermute | solution.py:508
  12.8 3.5 %shard_map.131 = (f32[64,512]{1,0:T(8,128)S(1)}, f32[192,512]{1,0:T(8,128)S(1)}, bf16[192,512]{1,0:T(8,128)(2,1)S(1)}, bf16[192,512]{1,0:T(8,128)(2,1)S(1)}, bf1...) custom-call(f32[1,512]{1,0:T(1,128)} %bitcast.27, ...), custom_call_target="tpu_custom_call" | custom-call | flops 99999997952 | bytes 4000000 | tf_op jit(solution)/shard_map/pallas_call | solution.py:455
  16.3 0.6 %collective-permute-start.4 = (bf16[128,512]{1,0:T(8,128)(2,1)S(1)}, bf16[128,512]{1,0:T(8,128)(2,1)S(1)}, u32[]{:S(2)}, u32[]{:S(2)}) collective-permute-start(bf16[128,512]{1,0:T(8,128)(2,1)S(1)} %get-tuple-element.66), channel_id=1, source_target_pairs={{16,0},{17,1},{18,2},{19,3},{20,4},{21,5},{22,6},{23,7},{24,8},{25... | collective-permute-start | bytes 393224 | tf_op jit(solution)/shard_map/ppermute | solution.py:508
  16.9 1.6 %all-to-all-done = bf16[16,24,128]{2,1,0:T(8,128)(2,1)S(1)} async-done(((bf16[16,24,128]{2,1,0:T(8,128)(2,1)}), bf16[16,24,128]{2,1,0:T(8,128)(2,1)S(1)}, u32[]{:S(2)}, u32[]{:S(2)}) %all-to-all-start) | async-done | bytes 98336 | tf_op jit(solution)/shard_map/all_to_all | solution.py:548
  18.5 0.7 %shard_map.132 = (bf16[256,128]{1,0:T(8,128)(2,1)S(1)}, bf16[128,128]{1,0:T(8,128)(2,1)S(1)}, bf16[32,384]{1,0:T(8,128)(2,1)S(1)}, bf16[32,384]{1,0:T(8,128)(2,1...) custom-call(bf16[384,128]{1,0:T(8,128)(2,1)S(1)} %bitcast.18, f32[128,512]{1,0:T(8,128)S(1)} %get-tuple-element.44.field), custom_call_target="tpu_custom_call" | custom-call | flops 1000000000 | bytes 2000000 | tf_op jit(solution)/shard_map/pallas_call | solution.py:455
  19.2 0.1 collective-permute-start.3
  19.3 1.5 %shard_map.133 = (f32[192,512]{1,0:T(8,128)S(1)}, f32[192,512]{1,0:T(8,128)S(1)}, bf16[512,512]{1,0:T(8,128)(2,1)S(1)}, bf16[512,512]{1,0:T(8,128)(2,1)S(1)}) custom-call(bf16[512,512]{1,0:T(8,128)(2,1)} %wn_hbm.3, bf16[512,512]{1,0:T(8,128)(2,1)} %ws_hbm.3, bf16[256,128]{1,0:T(8,128)(2,1)S(1)} %get-tuple-element.45.spread_own, ...), custom_call_target="tpu_custom_call" | custom-call | flops 1000000000 | bytes 3000000 | tf_op jit(solution)/shard_map/pallas_call | solution.py:455
  20.8 0.0 collective-permute-done.3.message
  20.8 0.0 collective-permute-done.2.message16
  20.8 1.7 %shard_map.134.base = f32[128,512]{1,0:T(8,128)S(1)} custom-call(f32[192,512]{1,0:T(8,128)S(1)} %get-tuple-element.51.last, f32[192,512]{1,0:T(8,128)S(1)} %get-tuple-element.52.early_pull, bf16[512,512]{1,0:T(8,128)(2,1)S(1)} %get-tuple-element.53.wn, bf16[512,512]{1,0:T(8,128)(2,1)S(1)} %get-tuple-element.54.ws, f32[1,512]{1,0:T(1,128)S(1)} %get-tuple-element.55.gain, ...), custom_call_target="tpu_custom_call" | custom-call | flops 603979776 | bytes 6000000 | tf_op jit(solution)/shard_map/pallas_call | solution.py:455
  22.5 0.0 collective-permute-done.4.before
  22.5 0.8 %shard_map.135 = f32[128,512]{1,0:T(8,128)} custom-call(f32[128,512]{1,0:T(8,128)S(1)} %shard_map.134.base, bf16[128,512]{1,0:T(8,128)(2,1)S(1)} %get-tuple-element.65.background, bf16[128,512]{1,0:T(8,128)(2,1)S(1)} %collective-permute-done.4.before, f32[1,512]{1,0:T(1,128)S(1)} %get-tuple-element.60.error), custom_call_target="tpu_custom_call" | custom-call | flops 1000000 | bytes 900000 | tf_op jit(solution)/shard_map/pallas_call | solution.py:455
  (2 shorter events, 0.1 us)
Async XLA Ops:
  0.0 2.6 %collective-permute-start = (f32[128,512]{1,0:T(8,128)}, f32[128,512]{1,0:T(8,128)S(1)}, u32[]{:S(2)}, u32[]{:S(2)}) collective-permute-start(f32[128,512]{1,0:T(8,128)} %bitcast.19), channel_id=1, source_target_pairs={{0,1},{1,0},{2,3},{3,2},{4,5},{5,4},{6,7},{7,6},{8,9},{9,8},{10,11... | collective-permute-start | bytes 786440 | tf_op jit(solution)/shard_map/ppermute | solution.py:510
  2.6 8.5 %collective-permute-start.1 = (bf16[144,512]{1,0:T(8,128)(2,1)S(1)}, bf16[144,512]{1,0:T(8,128)(2,1)S(1)}, u32[]{:S(2)}, u32[]{:S(2)}) collective-permute-start(bf16[144,512]{1,0:T(8,128)(2,1)S(1)} %shard_map.128.refs_5_), channel_id=1, source_target_pairs={{0,15},{1,2},{2,1},{3,4},{4,3},{5,6},{6,5},{7,8},{8,7},{9,10},{10,... | collective-permute-start | bytes 442376 | tf_op jit(solution)/shard_map/ppermute | solution.py:537
  7.6 10.9 %all-to-all-start = ((bf16[16,24,128]{2,1,0:T(8,128)(2,1)}), bf16[16,24,128]{2,1,0:T(8,128)(2,1)S(1)}, u32[]{:S(2)}, u32[]{:S(2)}) async-start(bf16[16,24,128]{2,1,0:T(8,128)(2,1)} %bitcast.9), calls=%async_computation | async-start | bytes 196608 | tf_op jit(solution)/shard_map/all_to_all | solution.py:548
  11.3 9.5 %collective-permute-start.2 = (bf16[160,512]{1,0:T(8,128)(2,1)S(1)}, bf16[160,512]{1,0:T(8,128)(2,1)S(1)}, u32[]{:S(2)}, u32[]{:S(2)}) collective-permute-start(bf16[160,512]{1,0:T(8,128)(2,1)S(1)} %get-tuple-element.57), channel_id=1, source_target_pairs={{16,0},{17,1},{18,2},{19,3},{20,4},{21,5},{22,6},{23,7},{24,8},{25... | collective-permute-start | bytes 491528 | tf_op jit(solution)/shard_map/ppermute | solution.py:508
  16.3 6.2 %collective-permute-start.4 = (bf16[128,512]{1,0:T(8,128)(2,1)S(1)}, bf16[128,512]{1,0:T(8,128)(2,1)S(1)}, u32[]{:S(2)}, u32[]{:S(2)}) collective-permute-start(bf16[128,512]{1,0:T(8,128)(2,1)S(1)} %get-tuple-element.66), channel_id=1, source_target_pairs={{16,0},{17,1},{18,2},{19,3},{20,4},{21,5},{22,6},{23,7},{24,8},{25... | collective-permute-start | bytes 393224 | tf_op jit(solution)/shard_map/ppermute | solution.py:508
  19.2 1.6 %collective-permute-start.3 = (bf16[128,128]{1,0:T(8,128)(2,1)S(1)}, bf16[128,128]{1,0:T(8,128)(2,1)S(1)}, u32[]{:S(2)}, u32[]{:S(2)}) collective-permute-start(bf16[128,128]{1,0:T(8,128)(2,1)S(1)} %get-tuple-element.61), channel_id=1, source_target_pairs={{0,1},{1,0},{2,3},{3,2},{4,5},{5,4},{6,7},{7,6},{8,9},{9,8},{10,11... | collective-permute-start | bytes 98312 | tf_op jit(solution)/shard_map/ppermute | solution.py:588

commit v5 on v4

--- a/solution.py
+++ b/solution.py
@@ -14,7 +14,6 @@
 SLOTS = 4 * CAP
 CHUNK = 24
 STRIDE = 32
-SENDERS = LANES // SLOTS
 WIDE = 40
 SLIM = 24
 VMEM_LIMIT = 28 * 1024 * 1024
@@ -274,10 +273,11 @@
 
 def spread_of(first, th, tl, scaled, taken, field, ph, plo, spread):
     lane = lax.broadcasted_iota(jnp.int32, (1, LANES), 1)
-    table_of = jnp.where(lane < SENDERS * SLOTS, lane % SLOTS // CAP, -1)
     members = field.shape[1] // LANES
     for p in range(th.shape[1] // LANES):
         at = slice(p * LANES, (p + 1) * LANES)
+        slot = (lane + p * LANES) % CHUNK
+        table_of = jnp.where(slot < SLOTS, slot // CAP, -1)
         for q in range(2):
             kept = jnp.where(table_of == first + q, scaled[:, at], 0.0)
             ph[q * 32 : (q + 1) * 32, at], plo[q * 32 : (q + 1) * 32, at] = split(kept)
@@ -297,8 +297,8 @@
 
 def observe_kernel(
     tiles, arrived, field,
-    spread, message, th, tl, scaled, taken,
-    ph, plo, vals, wide,
+    spread, message, th, tl, scaled,
+    ph, plo, wide,
 ):
     steps = 2
     members = field.shape[1] // LANES
@@ -306,28 +306,27 @@
     cells = sublane((32, LANES)).astype(F32)
     lane = lax.broadcasted_iota(jnp.int32, (8, LANES), 1)
     wide[...] = arrived[...].astype(F32)
-    vals[...] = jnp.zeros_like(vals)
-    for p in range(th.shape[1] // LANES):
-        meta = [jnp.zeros((8, LANES), F32)] * 2
-        for d in range(p * SENDERS, min((p + 1) * SENDERS, tiles)):
-            start = d % SENDERS * SLOTS
-            used = jnp.logical_and(lane >= start, lane < start + SLOTS)
-            for j in range(2):
-                row = d * CHUNK + SLOTS + j
-                rows = jnp.broadcast_to(wide[row : row + 1], (8, LANES))
-                turned = fan(rows, start + LANES - 5 * SLOTS)
-                meta[j] = meta[j] + jnp.where(used, turned, 0.0)
-            start += p * LANES
-            vals[start : start + SLOTS] = wide[d * CHUNK : d * CHUNK + SLOTS]
-        entry = [meta[i // 6][5 - i % 6 : 6 - i % 6] for i in range(9)]
+    packs = th.shape[1] // LANES
+    meta = [[jnp.zeros((8, LANES), F32)] * 2 for _ in range(packs)]
+    for d in range(tiles):
+        p, start = divmod(d * CHUNK, LANES)
+        ends = start + SLOTS - LANES
+        here = jnp.logical_and(lane >= start, lane < start + SLOTS)
+        for j in range(2):
+            row = d * CHUNK + SLOTS + j
+            turned = fan(jnp.broadcast_to(wide[row : row + 1], (8, LANES)), start + LANES - 5 * SLOTS)
+            meta[p][j] = meta[p][j] + jnp.where(here, turned, 0.0)
+            if ends > 0:
+                meta[p + 1][j] = meta[p + 1][j] + jnp.where(lane < ends, turned, 0.0)
+    for p in range(packs):
+        entry = [meta[p][i // 6][5 - i % 6 : 6 - i % 6] for i in range(9)]
         weight = jnp.zeros((32, LANES), F32)
         for i in range(4):
             weight += jnp.where(cells == entry[i], entry[4 + i], 0.0)
         at = slice(p * LANES, (p + 1) * LANES)
         th[:, at], tl[:, at] = split(weight)
         scaled[:, at] = weight * entry[8]
-    taken[...] = vals[...].astype(BF16)
-    spread_of(0, th, tl, scaled, taken, field, ph, plo, spread)
+    spread_of(0, th, tl, scaled, arrived, field, ph, plo, spread)
     size = members * 32
     for k in range(steps):
         for m in range(members):
@@ -376,36 +375,31 @@
 
 
 def pull_kernel(
-    wn_hbm, ws_hbm, spread_own, readout, th, tl, scaled, taken, field,
-    last, first, wn, ws,
-    ph, plo, spread, pulled, away, sems,
+    wn_hbm, ws_hbm, spread_own, readout, th, tl, scaled, arrived, field,
+    pulled, away, wn, ws,
+    ph, plo, spread, near, sems,
 ):
     pairs = ((wn_hbm, wn), (ws_hbm, ws))
     copies = [pltpu.make_async_copy(source, to, sems.at[i]) for i, (source, to) in enumerate(pairs)]
     for copy in copies:
         copy.start()
-    size = pulled.shape[0] // 2
     even = lax.rem(lax.axis_index("tile"), 2) == 0
-    row8 = sublane((8, 1))
-    spread_of(2, th, tl, scaled, taken, field, ph, plo, spread)
     pulled[...] = dot_t(spread_own[...], readout[...])
-    away[...] = dot_t(spread[...], readout[...])
-    for k, out in enumerate((first, last)):
-        for r in range(size // 16):
-            start = k * size + r * 16
-            out[r * SLIM : r * SLIM + 16] = pulled[start : start + 16]
-            low = jnp.where(row8 < 4, away[start : start + 8], 0.0)
-            high = jnp.where(row8 >= 4, away[start + 8 : start + 16], 0.0)
-            out[r * SLIM + 16 : (r + 1) * SLIM] = jnp.where(even, high, low)
+    spread_of(2, th, tl, scaled, arrived, field, ph, plo, spread)
+    for start in range(0, spread.shape[0], 32):
+        pair = spread[start : start + 32].astype(F32)
+        rows = [jnp.where(even, pair[i + 8 : i + 16], pair[i : i + 8]) for i in (0, 16)]
+        near[start // 2 : start // 2 + 16] = jnp.concatenate(rows, axis=0).astype(BF16)
+    away[...] = dot_t(near[...], readout[...])
     for copy in copies:
         copy.wait()
 
 
 def backward_kernel(
-    last, early_pull, wn, ws, gain, control, edge0, message16, f2x, wo, readout, error, message,
+    pulled, away, wn, ws, gain, control, edge0, message16, f2x, wo, readout, error, message,
     u1x, d0x, d1x,
     result,
-    cot2, cot1, add, gb, gm, flat, mate_pull, edge, u0x, final, nxt,
+    cot2, cot1, gb, gm, flat, mate_pull, edge, u0x, final, nxt,
 ):
     size = result.shape[0]
     members = size // 32
@@ -416,19 +410,24 @@
     mate_side = jnp.where(even, 1, 0) == jnp.where(row8 < 4, 1, 0)
     mate_pull[...] = dot_t(message[...], readout[...])
     final[...] = f2x[...].astype(F32)
-    add[...] = early_pull[...]
+
+    def pulls(k, r):
+        own = k * size + r * 16
+        near = k * size // 2 + r * 8
+        group = jnp.where(mate_side, mate_pull[near : near + 8], away[near : near + 8])
+        return pulled[own : own + 16], group
+
     for r in range(2 * members):
+        own, group = pulls(1, r)
         a, b = r * SLIM, r * SLIM + 16
-        cot2[a:b] = last[a:b] - weight * (nxt[r * 16 : (r + 1) * 16] - final[a:b])
+        cot2[a:b] = own - weight * (nxt[r * 16 : (r + 1) * 16] - final[a:b])
         u0x[a:b] = control[r * 16 : (r + 1) * 16]
         a, b = b, b + 8
-        start = size // 2 + r * 8
-        pulled = last[a:b] + jnp.where(mate_side, mate_pull[start : start + 8], 0.0)
-        cot2[a:b] = pulled - weight * (edges(nxt, size, edge, r) - final[a:b])
-        add[a:b] = early_pull[a:b] + jnp.where(mate_side, mate_pull[r * 8 : (r + 1) * 8], 0.0)
+        cot2[a:b] = group - weight * (edges(nxt, size, edge, r) - final[a:b])
         u0x[a:b] = edge0[r * 8 : (r + 1) * 8]
+
     def keep(r, value):
-        cot1[r * SLIM : (r + 1) * SLIM] = value + add[r * SLIM : (r + 1) * SLIM]
+        cot1[r * SLIM : (r + 1) * SLIM] = value + jnp.concatenate(pulls(0, r), axis=0)
 
     def finish(r, value):
         a, b = r * SLIM, r * SLIM + 16
@@ -575,30 +574,29 @@
         held, near4, oth,
     )
     before = across(final, -1)
-    total = -(-tiles // SENDERS) * LANES
+    total = tiles * CHUNK
     tables = [scratch(64, BF16, total), scratch(64, BF16, total)]
     spread, near_spread, *reports_held = kernel_call(
         functools.partial(observe_kernel, tiles),
         [spec(2 * size, BF16, LANES), spec(size, BF16, LANES)]
-        + [spec(32, BF16, total), spec(32, BF16, total), spec(32, F32, total), spec(total, BF16, LANES)],
-        tables + [scratch(total, F32, LANES), scratch(tiles * CHUNK, F32, LANES)],
+        + [spec(32, BF16, total), spec(32, BF16, total), spec(32, F32, total)],
+        tables + [scratch(total, F32, LANES)],
         10**9,
         2000000,
     )(arrived, field)
     from_mate = lax.ppermute(near_spread, "tile", mate_of)
     handed = kernel_call(
         pull_kernel,
-        [spec(slim), spec(slim), spec(channels, BF16), spec(channels, BF16)],
-        tables
-        + [scratch(2 * size, BF16, LANES), scratch(2 * size), scratch(2 * size), pltpu.SemaphoreType.DMA((2,))],
+        [spec(2 * size), spec(size), spec(channels, BF16), spec(channels, BF16)],
+        tables + [scratch(2 * size, BF16, LANES), scratch(size, BF16, LANES), pltpu.SemaphoreType.DMA((2,))],
         10**9,
         3000000,
         hbm=2,
-    )(neighbour_weight, self_weight, spread, readout_held, *reports_held, field)
+    )(neighbour_weight, self_weight, spread, readout_held, *reports_held, arrived, field)
     base = kernel_call(
         backward_kernel,
         spec(size),
-        [scratch(slim), scratch(slim), scratch(slim), scratch(slim, BF16), scratch(slim), scratch(slim)]
+        [scratch(slim), scratch(slim), scratch(slim, BF16), scratch(slim), scratch(slim)]
         + [scratch(size), scratch(16), scratch(slim), scratch(slim), scratch(size + 4 * groups)],
         12 * slim * channels * channels,
         6000000,

time: 23.5 us -> 23.3 us (level)
    pallas_call x9, Pallas kernels: 10.3 us -> 10.1 us  [call(): pl.pallas_call(body, out_shape=outs, in_specs=[pl.BlockSpec(memory_space=...]
  transfers between devices with their start and end apart: 6 -> 6, of which waited for: 1 -> 1; matrix products, arithmetic and copies ran while one was open for 0% -> 0% of each run, Pallas kernels for 41% -> 40%
where the time goes in v5:
time: 23.3 us; the launch traced here: 23 us
  starting transfers between devices  11.2 us (48%)
  Pallas kernels  10.1 us (43%)
  waiting for transfers between devices  1.65 us (7%)
    pallas_call x9, Pallas kernels, call(): pl.pallas_call(body, out_shape=outs, in_specs=[pl.BlockSpec(memory_space=...  10.1 us
    ppermute x1, starting transfers between devices, per_device(): oth = lax.ppermute(sent, 'tile', other_of)  4.97 us
    all_to_all x1, starting transfers between devices, per_device(): lax.all_to_all(packed, 'tile', split_axis=0, concat_axis=0, tiled=True)  3.52 us
    ppermute x2, starting transfers between devices, across(): return lax.ppermute(block, ('slot', 'tile'), pairs)  2.15 us
    all_to_all x1, waiting for transfers between devices, per_device(): lax.all_to_all(packed, 'tile', split_axis=0, concat_axis=0, tiled=True)  1.64 us
  transfers between devices with their start and end apart: 6, of which 1 were waited for; matrix products, arithmetic and copies ran while one was open for 0% of the time, Pallas kernels for 40%

profile of v5, /device:TPU:0, one launch (start us, length us, event | category | flops | bytes accessed | tf_op | source)
XLA Modules:
  0.0 23.0 jit_solution(4470230303673831464)
XLA Ops:
  0.0 0.5 %collective-permute-start = (f32[128,512]{1,0:T(8,128)}, f32[128,512]{1,0:T(8,128)S(1)}, u32[]{:S(2)}, u32[]{:S(2)}) collective-permute-start(f32[128,512]{1,0:T(8,128)} %bitcast.20), channel_id=1, source_target_pairs={{0,1},{1,0},{2,3},{3,2},{4,5},{5,4},{6,7},{7,6},{8,9},{9,8},{10,11... | collective-permute-start | bytes 786440 | tf_op jit(solution)/shard_map/ppermute | solution.py:509
  0.5 2.1 %shard_map.127 = (f32[128,512]{1,0:T(8,128)S(1)}, bf16[384,128]{1,0:T(8,128)(2,1)}, s32[2,1,32]{2,1,0:T(1,128)S(1)}, s32[2,4,32]{2,1,0:T(4,128)S(1)}, bf16[2,4,3...) custom-call(f32[128,512]{1,0:T(8,128)} %bitcast.21, s32[2,1,32]{2,1,0:T(1,128)} %bitcast.25, ...), custom_call_target="tpu_custom_call" | custom-call | flops 10000000 | bytes 200000 | tf_op jit(solution)/shard_map/pallas_call | solution.py:454
  2.6 0.0 collective-permute-done.mate
  2.6 5.0 %collective-permute-start.1 = (bf16[144,512]{1,0:T(8,128)(2,1)S(1)}, bf16[144,512]{1,0:T(8,128)(2,1)S(1)}, u32[]{:S(2)}, u32[]{:S(2)}) collective-permute-start(bf16[144,512]{1,0:T(8,128)(2,1)S(1)} %shard_map.128.refs_5_), channel_id=1, source_target_pairs={{0,15},{1,2},{2,1},{3,4},{4,3},{5,6},{6,5},{7,8},{8,7},{9,10},{10,... | collective-permute-start | bytes 442376 | tf_op jit(solution)/shard_map/ppermute | solution.py:536
  7.6 3.5 %all-to-all-start = ((bf16[16,24,128]{2,1,0:T(8,128)(2,1)}), bf16[16,24,128]{2,1,0:T(8,128)(2,1)S(1)}, u32[]{:S(2)}, u32[]{:S(2)}) async-start(bf16[16,24,128]{2,1,0:T(8,128)(2,1)} %bitcast.9), calls=%async_computation | async-start | bytes 196608 | tf_op jit(solution)/shard_map/all_to_all | solution.py:547
  11.1 0.0 collective-permute-done.1.oth
  11.2 0.1 shard_map.130
  11.3 1.6 %collective-permute-start.2 = (bf16[160,512]{1,0:T(8,128)(2,1)S(1)}, bf16[160,512]{1,0:T(8,128)(2,1)S(1)}, u32[]{:S(2)}, u32[]{:S(2)}) collective-permute-start(bf16[160,512]{1,0:T(8,128)(2,1)S(1)} %get-tuple-element.55), channel_id=1, source_target_pairs={{16,0},{17,1},{18,2},{19,3},{20,4},{21,5},{22,6},{23,7},{24,8},{25... | collective-permute-start | bytes 491528 | tf_op jit(solution)/shard_map/ppermute | solution.py:507
  12.8 3.5 %shard_map.131 = (f32[64,512]{1,0:T(8,128)S(1)}, f32[192,512]{1,0:T(8,128)S(1)}, bf16[192,512]{1,0:T(8,128)(2,1)S(1)}, bf16[192,512]{1,0:T(8,128)(2,1)S(1)}, bf1...) custom-call(f32[1,512]{1,0:T(1,128)} %bitcast.28, ...), custom_call_target="tpu_custom_call" | custom-call | flops 99999997952 | bytes 4000000 | tf_op jit(solution)/shard_map/pallas_call | solution.py:454
  16.3 0.6 %collective-permute-start.4 = (bf16[128,512]{1,0:T(8,128)(2,1)S(1)}, bf16[128,512]{1,0:T(8,128)(2,1)S(1)}, u32[]{:S(2)}, u32[]{:S(2)}) collective-permute-start(bf16[128,512]{1,0:T(8,128)(2,1)S(1)} %get-tuple-element.64), channel_id=1, source_target_pairs={{16,0},{17,1},{18,2},{19,3},{20,4},{21,5},{22,6},{23,7},{24,8},{25... | collective-permute-start | bytes 393224 | tf_op jit(solution)/shard_map/ppermute | solution.py:507
  16.9 1.6 %all-to-all-done = bf16[16,24,128]{2,1,0:T(8,128)(2,1)S(1)} async-done(((bf16[16,24,128]{2,1,0:T(8,128)(2,1)}), bf16[16,24,128]{2,1,0:T(8,128)(2,1)S(1)}, u32[]{:S(2)}, u32[]{:S(2)}) %all-to-all-start) | async-done | bytes 98336 | tf_op jit(solution)/shard_map/all_to_all | solution.py:547
  18.5 0.7 %shard_map.132 = (bf16[256,128]{1,0:T(8,128)(2,1)S(1)}, bf16[128,128]{1,0:T(8,128)(2,1)S(1)}, bf16[32,384]{1,0:T(8,128)(2,1)S(1)}, bf16[32,384]{1,0:T(8,128)(2,1)S(1)}, f32[32,384]{1,0:T(8,128)S(1)}) custom-call(bf16[384,128]{1,0:T(8,128)(2,1)S(1)} %bitcast.18, f32[128,512]{1,0:T(8,128)S(1)} %get-tuple-element.43.field), custom_call_target="tpu_custom_call" | custom-call | flops 1000000000 | bytes 2000000 | tf_op jit(solution)/shard_map/pallas_call | solution.py:454
  19.2 0.1 collective-permute-start.3
  19.3 1.2 %shard_map.133 = (f32[256,512]{1,0:T(8,128)S(1)}, f32[128,512]{1,0:T(8,128)S(1)}, bf16[512,512]{1,0:T(8,128)(2,1)S(1)}, bf16[512,512]{1,0:T(8,128)(2,1)S(1)}) custom-call(bf16[512,512]{1,0:T(8,128)(2,1)} %wn_hbm.3, bf16[512,512]{1,0:T(8,128)(2,1)} %ws_hbm.3, bf16[256,128]{1,0:T(8,128)(2,1)S(1)} %get-tuple-element.44.spread_own, ...), custom_call_target="tpu_custom_call" | custom-call | flops 1000000000 | bytes 3000000 | tf_op jit(solution)/shard_map/pallas_call | solution.py:454
  20.5 0.0 collective-permute-done.3.message
  20.5 0.0 collective-permute-done.2.message16
  20.6 1.7 %shard_map.134.base = f32[128,512]{1,0:T(8,128)S(1)} custom-call(f32[256,512]{1,0:T(8,128)S(1)} %get-tuple-element.49.pulled, f32[128,512]{1,0:T(8,128)S(1)} %get-tuple-element.50.away, bf16[512,512]{1,0:T(8,128)(2,1)S(1)} %get-tuple-element.51.wn, bf16[512,512]{1,0:T(8,128)(2,1)S(1)} %get-tuple-element.52.ws, f32[1,512]{1,0:T(1,128)S(1)} %get-tuple-element.53.gain, ...), custom_call_target="tpu_custom_call" | custom-call | flops 603979776 | bytes 6000000 | tf_op jit(solution)/shard_map/pallas_call | solution.py:454
  22.2 0.0 collective-permute-done.4.before
  22.2 0.8 %shard_map.135 = f32[128,512]{1,0:T(8,128)} custom-call(f32[128,512]{1,0:T(8,128)S(1)} %shard_map.134.base, bf16[128,512]{1,0:T(8,128)(2,1)S(1)} %get-tuple-element.63.background, bf16[128,512]{1,0:T(8,128)(2,1)S(1)} %collective-permute-done.4.before, f32[1,512]{1,0:T(1,128)S(1)} %get-tuple-element.58.error), custom_call_target="tpu_custom_call" | custom-call | flops 1000000 | bytes 900000 | tf_op jit(solution)/shard_map/pallas_call | solution.py:454
  (2 shorter events, 0.1 us)
Async XLA Ops:
  0.0 2.6 %collective-permute-start = (f32[128,512]{1,0:T(8,128)}, f32[128,512]{1,0:T(8,128)S(1)}, u32[]{:S(2)}, u32[]{:S(2)}) collective-permute-start(f32[128,512]{1,0:T(8,128)} %bitcast.20), channel_id=1, source_target_pairs={{0,1},{1,0},{2,3},{3,2},{4,5},{5,4},{6,7},{7,6},{8,9},{9,8},{10,11... | collective-permute-start | bytes 786440 | tf_op jit(solution)/shard_map/ppermute | solution.py:509
  2.6 8.5 %collective-permute-start.1 = (bf16[144,512]{1,0:T(8,128)(2,1)S(1)}, bf16[144,512]{1,0:T(8,128)(2,1)S(1)}, u32[]{:S(2)}, u32[]{:S(2)}) collective-permute-start(bf16[144,512]{1,0:T(8,128)(2,1)S(1)} %shard_map.128.refs_5_), channel_id=1, source_target_pairs={{0,15},{1,2},{2,1},{3,4},{4,3},{5,6},{6,5},{7,8},{8,7},{9,10},{10,... | collective-permute-start | bytes 442376 | tf_op jit(solution)/shard_map/ppermute | solution.py:536
  7.6 10.9 %all-to-all-start = ((bf16[16,24,128]{2,1,0:T(8,128)(2,1)}), bf16[16,24,128]{2,1,0:T(8,128)(2,1)S(1)}, u32[]{:S(2)}, u32[]{:S(2)}) async-start(bf16[16,24,128]{2,1,0:T(8,128)(2,1)} %bitcast.9), calls=%async_computation | async-start | bytes 196608 | tf_op jit(solution)/shard_map/all_to_all | solution.py:547
  11.3 9.3 %collective-permute-start.2 = (bf16[160,512]{1,0:T(8,128)(2,1)S(1)}, bf16[160,512]{1,0:T(8,128)(2,1)S(1)}, u32[]{:S(2)}, u32[]{:S(2)}) collective-permute-start(bf16[160,512]{1,0:T(8,128)(2,1)S(1)} %get-tuple-element.55), channel_id=1, source_target_pairs={{16,0},{17,1},{18,2},{19,3},{20,4},{21,5},{22,6},{23,7},{24,8},{25... | collective-permute-start | bytes 491528 | tf_op jit(solution)/shard_map/ppermute | solution.py:507
  16.3 5.9 %collective-permute-start.4 = (bf16[128,512]{1,0:T(8,128)(2,1)S(1)}, bf16[128,512]{1,0:T(8,128)(2,1)S(1)}, u32[]{:S(2)}, u32[]{:S(2)}) collective-permute-start(bf16[128,512]{1,0:T(8,128)(2,1)S(1)} %get-tuple-element.64), channel_id=1, source_target_pairs={{16,0},{17,1},{18,2},{19,3},{20,4},{21,5},{22,6},{23,7},{24,8},{25... | collective-permute-start | bytes 393224 | tf_op jit(solution)/shard_map/ppermute | solution.py:507
  19.2 1.3 %collective-permute-start.3 = (bf16[128,128]{1,0:T(8,128)(2,1)S(1)}, bf16[128,128]{1,0:T(8,128)(2,1)S(1)}, u32[]{:S(2)}, u32[]{:S(2)}) collective-permute-start(bf16[128,128]{1,0:T(8,128)(2,1)S(1)} %get-tuple-element.59), channel_id=1, source_target_pairs={{0,1},{1,0},{2,3},{3,2},{4,5},{5,4},{6,7},{7,6},{8,9},{9,8},{10,11... | collective-permute-start | bytes 98312 | tf_op jit(solution)/shard_map/ppermute | solution.py:587

commit v6 on v5

--- a/solution.py
+++ b/solution.py
@@ -13,6 +13,7 @@
 CAP = 5
 SLOTS = 4 * CAP
 CHUNK = 24
+APART = 36
 STRIDE = 32
 WIDE = 40
 SLIM = 24
@@ -47,7 +48,7 @@
     ]
 
 
-def forward_step(u, n, mean, act, pre, d, gain, ws, wn, wo, width, members, out, copies=()):
+def forward_step(u, n, act, pre, d, gain, weights, wo, width, members, out, copies=()):
     both = 2 * width
     for m in range(members):
         base = m * both
@@ -55,11 +56,12 @@
         for lat in range(2):
             x = u[base + lat * width : base + (lat + 1) * width]
             rows.append((x * inverse_rms(x) * gain).astype(BF16).astype(F32))
-        n[base : base + both] = jnp.concatenate(rows, axis=0).astype(BF16)
-        mean[base : base + both] = jnp.concatenate(neighbours(rows), axis=0).astype(BF16)
+        channels = rows[0].shape[1]
+        n[base : base + both, :channels] = jnp.concatenate(rows, axis=0).astype(BF16)
+        n[base : base + both, channels:] = jnp.concatenate(neighbours(rows), axis=0).astype(BF16)
     for copy in copies[:2]:
         copy.wait()
-    pre[...] = dot(n[...], ws[...]) + dot(mean[...], wn[...])
+    pre[...] = dot(n[...], weights[...])
     for m in range(members):
         base = m * both
         p = pre[base : base + both]
@@ -132,7 +134,7 @@
     if shift % LANES:
         x = pltpu.roll(x, shift % LANES, 1)
     for _ in range(2):
-        x = pltpu.roll(x, 0, 1, stride=SLOTS // 2, stride_axis=0)
+        x = pltpu.roll(x, 0, 1, stride=APART // 2, stride_axis=0)
     return x
 
 
@@ -150,10 +152,11 @@
         before = dot(hits.astype(BF16), earlier)
         rank = jnp.sum(hits * before, axis=0, keepdims=True).astype(jnp.int32)
         key[0:1, at] = owner[k] * (2 * CAP) + k * CAP + rank
-        meta[0:4, at] = stencil[k].astype(F32)
-        meta[4:6, at] = weights[k, 0:2].astype(F32)
-        meta[8:10, at] = weights[k, 2:4].astype(F32)
-        meta[10:11, at] = precision[k : k + 1].astype(F32)
+        for i in range(4):
+            meta[i // 3 * 8 + i % 3 : i // 3 * 8 + i % 3 + 1, at] = stencil[k, i : i + 1].astype(F32)
+            j = 4 + i
+            meta[j // 3 * 8 + j % 3 : j // 3 * 8 + j % 3 + 1, at] = weights[k, i : i + 1].astype(F32)
+        meta[18:19, at] = precision[k : k + 1].astype(F32)
     row = lax.broadcasted_iota(jnp.int32, (tiles * STRIDE, total), 0)
     tile = row // STRIDE
     slot = row % STRIDE
@@ -164,17 +167,20 @@
     placement = (wanted == key[...]).astype(F32).astype(BF16)
     placed = dot(placement, values[...])
     entries = dot_t(meta[...].astype(BF16), placement)
-    lane = lax.broadcasted_iota(jnp.int32, (16, LANES), 1)
+    lane = lax.broadcasted_iota(jnp.int32, (24, LANES), 1)
+    turn = lax.axis_index("tile") * CHUNK % LANES
     per_tile = LANES // STRIDE
     for t in range(tiles):
         picked[t * CHUNK : (t + 1) * CHUNK] = placed[t * STRIDE : t * STRIDE + CHUNK]
         start = t % per_tile * STRIDE
         used = jnp.logical_and(lane >= start, lane < start + SLOTS)
         block = jnp.where(used, entries[:, t // per_tile * LANES : (t // per_tile + 1) * LANES], 0.0)
-        for j in range(2):
-            spread = fan(block[j * 8 : (j + 1) * 8], LANES - start)
+        for j in range(3):
+            laid = fan(block[j * 8 : (j + 1) * 8], LANES - start)
             row = t * CHUNK + SLOTS + j
-            picked[row : row + 1] = jnp.sum(spread, axis=0, keepdims=True)
+            picked[row : row + 1] = jnp.sum(laid, axis=0, keepdims=True)
+        group = picked[t * CHUNK + 16 : (t + 1) * CHUNK]
+        picked[t * CHUNK + 16 : (t + 1) * CHUNK] = jnp.where(sublane((8, 1)) < 4, group, pltpu.roll(group, turn, 1))
     out[...] = picked[...].astype(BF16)
 
 
@@ -206,10 +212,12 @@
 def forward_kernel(
     gain_hbm, ws_hbm, wn_hbm, wo_hbm, readout_hbm, error_hbm, background_hbm, control, mate, oth,
     edge0, u1x, d0x, d1x, f2x, field, final, wo, readout, gain, error, background,
-    ua, ub, n, mean, act, pre, edge, states, ws, wn, sems,
+    ua, ub, n, act, pre, edge, states, weights, sems,
 ):
+    channels = wo.shape[0]
+    halves = weights.at[pl.ds(0, channels)], weights.at[pl.ds(channels, channels)]
     pairs = (
-        (gain_hbm, gain), (ws_hbm, ws), (wn_hbm, wn), (wo_hbm, wo), (readout_hbm, readout),
+        (gain_hbm, gain), (ws_hbm, halves[0]), (wn_hbm, halves[1]), (wo_hbm, wo), (readout_hbm, readout),
         (error_hbm, error), (background_hbm, background),
     )
     copies = [pltpu.make_async_copy(source, to, sems.at[i]) for i, (source, to) in enumerate(pairs)]
@@ -250,11 +258,11 @@
             taken = ref[pl.ds(pl.multiple_of(r * WIDE + tile_at, 8), 16)]
             states[away + r * 16 : away + (r + 1) * 16] = taken.astype(BF16)
 
-    forward_step(ua, n, mean, act, pre, d0x, g, ws, wn, wo, WIDE, members, keep(ub), copies[1:])
+    forward_step(ua, n, act, pre, d0x, g, weights, wo, WIDE, members, keep(ub), copies[1:])
     for m in range(members):
         slim_copy(u1x, ub, m)
     keep_states(ub, 0)
-    forward_step(ub, n, mean, act, pre, d1x, g, ws, wn, wo, WIDE, members, keep(ua))
+    forward_step(ub, n, act, pre, d1x, g, weights, wo, WIDE, members, keep(ua))
     for m in range(members):
         slim_copy(f2x, ua, m)
     keep_states(ua, 1)
@@ -307,19 +315,22 @@
     lane = lax.broadcasted_iota(jnp.int32, (8, LANES), 1)
     wide[...] = arrived[...].astype(F32)
     packs = th.shape[1] // LANES
-    meta = [[jnp.zeros((8, LANES), F32)] * 2 for _ in range(packs)]
+    sums = [[jnp.zeros((8, LANES), F32)] * 3 for _ in range(packs)]
     for d in range(tiles):
         p, start = divmod(d * CHUNK, LANES)
-        ends = start + SLOTS - LANES
-        here = jnp.logical_and(lane >= start, lane < start + SLOTS)
-        for j in range(2):
-            row = d * CHUNK + SLOTS + j
-            turned = fan(jnp.broadcast_to(wide[row : row + 1], (8, LANES)), start + LANES - 5 * SLOTS)
-            meta[p][j] = meta[p][j] + jnp.where(here, turned, 0.0)
-            if ends > 0:
-                meta[p + 1][j] = meta[p + 1][j] + jnp.where(lane < ends, turned, 0.0)
+        group = wide[d * CHUNK + 16 : (d + 1) * CHUNK]
+        for b in range(3):
+            first = start + b * APART
+            place = lane - first % LANES
+            place = jnp.where(place < 0, place + LANES, place)
+            ends = min(LANES - start, SLOTS)
+            sums[p][b] = sums[p][b] + jnp.where(place < ends, group, 0.0)
+            if ends < SLOTS:
+                rest = jnp.logical_and(place >= ends, place < SLOTS)
+                sums[p + 1][b] = sums[p + 1][b] + jnp.where(rest, group, 0.0)
     for p in range(packs):
-        entry = [meta[p][i // 6][5 - i % 6 : 6 - i % 6] for i in range(9)]
+        kinds = [pltpu.roll(sums[p][b], (LANES - b * APART) % LANES, 1) if b else sums[p][b] for b in range(3)]
+        entry = [kinds[i % 3][4 + i // 3 : 5 + i // 3] for i in range(9)]
         weight = jnp.zeros((32, LANES), F32)
         for i in range(4):
             weight += jnp.where(cells == entry[i], entry[4 + i], 0.0)
@@ -337,25 +348,25 @@
             message[start : start + 16] = jnp.concatenate(near, axis=0).astype(BF16)
 
 
-def adjoint_step(u, cot, gb, gm, flat, d, out, gain, ws, wn, wo, members):
+def adjoint_step(u, cot, gb, flat, products, d, out, gain, weights, wo, members):
     both = 2 * SLIM
+    channels = flat.shape[1]
     gb[...] = cot[...].astype(BF16)
     flat[...] = dot_t(gb[...], wo[...])
     gb[...] = (flat[...] * d[...]).astype(BF16)
-    gm[...] = dot_t(gb[...], wn[...])
-    flat[...] = dot_t(gb[...], ws[...])
+    products[...] = dot_t(gb[...], weights[...])
     for m in range(members):
         base = m * both
         rows = []
         for lat in range(2):
             start = base + lat * SLIM
-            rows.append(gm[start : start + SLIM].astype(BF16).astype(F32))
+            rows.append(products[start : start + SLIM, :channels].astype(BF16).astype(F32))
         around = neighbours(rows)
         for lat in range(2):
             start = base + lat * SLIM
             x = u[start : start + SLIM]
             s = inverse_rms(x)
-            scaled = gain * (flat[start : start + SLIM] + around[lat])
+            scaled = gain * (products[start : start + SLIM, channels:] + around[lat])
             inner = jnp.mean(x * scaled, axis=-1, keepdims=True)
             out(2 * m + lat, cot[start : start + SLIM] + s * scaled - x * (s * s * s * inner))
 
@@ -376,10 +387,11 @@
 
 def pull_kernel(
     wn_hbm, ws_hbm, spread_own, readout, th, tl, scaled, arrived, field,
-    pulled, away, wn, ws,
+    pulled, away, weights,
     ph, plo, spread, near, sems,
 ):
-    pairs = ((wn_hbm, wn), (ws_hbm, ws))
+    channels = wn_hbm.shape[0]
+    pairs = ((wn_hbm, weights.at[pl.ds(0, channels)]), (ws_hbm, weights.at[pl.ds(channels, channels)]))
     copies = [pltpu.make_async_copy(source, to, sems.at[i]) for i, (source, to) in enumerate(pairs)]
     for copy in copies:
         copy.start()
@@ -396,10 +408,10 @@
 
 
 def backward_kernel(
-    pulled, away, wn, ws, gain, control, edge0, message16, f2x, wo, readout, error, message,
+    pulled, away, weights, gain, control, edge0, message16, f2x, wo, readout, error, message,
     u1x, d0x, d1x,
     result,
-    cot2, cot1, gb, gm, flat, mate_pull, edge, u0x, final, nxt,
+    cot2, cot1, gb, flat, both, mate_pull, edge, u0x, final, nxt,
 ):
     size = result.shape[0]
     members = size // 32
@@ -433,8 +445,8 @@
         a, b = r * SLIM, r * SLIM + 16
         result[r * 16 : (r + 1) * 16] = value[0:16] + error[...] * u0x[a:b]
 
-    adjoint_step(u1x, cot2, gb, gm, flat, d1x, keep, gain[...], ws, wn, wo, members)
-    adjoint_step(u0x, cot1, gb, gm, flat, d0x, finish, gain[...], ws, wn, wo, members)
+    adjoint_step(u1x, cot2, gb, flat, both, d1x, keep, gain[...], weights, wo, members)
+    adjoint_step(u0x, cot1, gb, flat, both, d0x, finish, gain[...], weights, wo, members)
 
 
 def last_kernel(base, background, before, error, result):
@@ -516,7 +528,7 @@
     )
     work = [
         pltpu.VMEM((1, steps * rows), jnp.int32),
-        scratch(16, F32, steps * rows),
+        scratch(24, F32, steps * rows),
         scratch(tiles * CHUNK, F32, LANES),
         scratch(tiles * CHUNK, BF16, LANES),
     ]
@@ -563,9 +575,9 @@
         [spec(groups * 8), spec(slim)] + [spec(slim, BF16)] * 3
         + [spec(4 * lats * cols, F32, members * LANES), spec(size, BF16)]
         + [spec(channels, BF16), spec(channels, BF16, LANES), spec(1), spec(1), spec(size, BF16)],
-        [scratch(wide), scratch(wide), scratch(wide, BF16), scratch(wide, BF16), scratch(wide, BF16)]
+        [scratch(wide), scratch(wide), scratch(wide, BF16, 2 * channels), scratch(wide, BF16)]
         + [scratch(wide), scratch(16), scratch(4 * size, BF16)]
-        + [scratch(channels, BF16), scratch(channels, BF16), pltpu.SemaphoreType.DMA((7,))],
+        + [scratch(2 * channels, BF16), pltpu.SemaphoreType.DMA((7,))],
         10**11,
         4000000,
         hbm=7,
@@ -587,7 +599,7 @@
     from_mate = lax.ppermute(near_spread, "tile", mate_of)
     handed = kernel_call(
         pull_kernel,
-        [spec(2 * size), spec(size), spec(channels, BF16), spec(channels, BF16)],
+        [spec(2 * size), spec(size), spec(2 * channels, BF16)],
         tables + [scratch(2 * size, BF16, LANES), scratch(size, BF16, LANES), pltpu.SemaphoreType.DMA((2,))],
         10**9,
         3000000,
@@ -596,7 +608,7 @@
     base = kernel_call(
         backward_kernel,
         spec(size),
-        [scratch(slim), scratch(slim), scratch(slim, BF16), scratch(slim), scratch(slim)]
+        [scratch(slim), scratch(slim), scratch(slim, BF16), scratch(slim), scratch(slim, F32, 2 * channels)]
         + [scratch(size), scratch(16), scratch(slim), scratch(slim), scratch(size + 4 * groups)],
         12 * slim * channels * channels,
         6000000,

time: 23.3 us -> 23.4 us (level)
  transfers between devices with their start and end apart: 6 -> 6, of which waited for: 1 -> 1; matrix products, arithmetic and copies ran while one was open for 0% -> 0% of each run, Pallas kernels for 40% -> 41%
where the time goes in v6:
time: 23.4 us; the launch traced here: 23.1 us
  starting transfers between devices  11.1 us (47%)
  Pallas kernels  10.2 us (44%)
  waiting for transfers between devices  1.76 us (8%)
    pallas_call x9, Pallas kernels, call(): pl.pallas_call(body, out_shape=outs, in_specs=[pl.BlockSpec(memory_space=...  10.2 us
    ppermute x1, starting transfers between devices, per_device(): oth = lax.ppermute(sent, 'tile', other_of)  4.88 us
    all_to_all x1, starting transfers between devices, per_device(): lax.all_to_all(packed, 'tile', split_axis=0, concat_axis=0, tiled=True)  3.52 us
    ppermute x2, starting transfers between devices, across(): return lax.ppermute(block, ('slot', 'tile'), pairs)  2.16 us
    all_to_all x1, waiting for transfers between devices, per_device(): lax.all_to_all(packed, 'tile', split_axis=0, concat_axis=0, tiled=True)  1.74 us
  transfers between devices with their start and end apart: 6, of which 1 were waited for; matrix products, arithmetic and copies ran while one was open for 0% of the time, Pallas kernels for 41%

profile of v6, /device:TPU:0, one launch (start us, length us, event | category | flops | bytes accessed | tf_op | source)
XLA Modules:
  0.0 23.1 jit_solution(4191026659202499333)
XLA Ops:
  0.0 0.5 %collective-permute-start = (f32[128,512]{1,0:T(8,128)}, f32[128,512]{1,0:T(8,128)S(1)}, u32[]{:S(2)}, u32[]{:S(2)}) collective-permute-start(f32[128,512]{1,0:T(8,128)} %bitcast.20), channel_id=1, source_target_pairs={{0,1},{1,0},{2,3},{3,2},{4,5},{5,4},{6,7},{7,6},{8,9},{9,8},{10,11... | collective-permute-start | bytes 786440 | tf_op jit(solution)/shard_map/ppermute | solution.py:521
  0.5 2.2 %shard_map.127 = (f32[128,512]{1,0:T(8,128)S(1)}, bf16[384,128]{1,0:T(8,128)(2,1)}, s32[2,1,32]{2,1,0:T(1,128)S(1)}, s32[2,4,32]{2,1,0:T(4,128)S(1)}, bf16[2,4,3...) custom-call(f32[128,512]{1,0:T(8,128)} %bitcast.21, s32[2,1,32]{2,1,0:T(1,128)} %bitcast.25, ...), custom_call_target="tpu_custom_call" | custom-call | flops 10000000 | bytes 200000 | tf_op jit(solution)/shard_map/pallas_call | solution.py:466
  2.7 0.0 collective-permute-done.mate
  2.7 4.9 %collective-permute-start.1 = (bf16[144,512]{1,0:T(8,128)(2,1)S(1)}, bf16[144,512]{1,0:T(8,128)(2,1)S(1)}, u32[]{:S(2)}, u32[]{:S(2)}) collective-permute-start(bf16[144,512]{1,0:T(8,128)(2,1)S(1)} %shard_map.128.refs_5_), channel_id=1, source_target_pairs={{0,15},{1,2},{2,1},{3,4},{4,3},{5,6},{6,5},{7,8},{8,7},{9,10},{10,... | collective-permute-start | bytes 442376 | tf_op jit(solution)/shard_map/ppermute | solution.py:548
  7.6 3.5 %all-to-all-start = ((bf16[16,24,128]{2,1,0:T(8,128)(2,1)}), bf16[16,24,128]{2,1,0:T(8,128)(2,1)S(1)}, u32[]{:S(2)}, u32[]{:S(2)}) async-start(bf16[16,24,128]{2,1,0:T(8,128)(2,1)} %bitcast.9), calls=%async_computation | async-start | bytes 196608 | tf_op jit(solution)/shard_map/all_to_all | solution.py:559
  11.1 0.0 collective-permute-done.1.oth
  11.2 0.1 shard_map.130
  11.3 1.6 %collective-permute-start.2 = (bf16[160,512]{1,0:T(8,128)(2,1)S(1)}, bf16[160,512]{1,0:T(8,128)(2,1)S(1)}, u32[]{:S(2)}, u32[]{:S(2)}) collective-permute-start(bf16[160,512]{1,0:T(8,128)(2,1)S(1)} %get-tuple-element.53), channel_id=1, source_target_pairs={{16,0},{17,1},{18,2},{19,3},{20,4},{21,5},{22,6},{23,7},{24,8},{25... | collective-permute-start | bytes 491528 | tf_op jit(solution)/shard_map/ppermute | solution.py:519
  12.8 3.3 %shard_map.131 = (f32[64,512]{1,0:T(8,128)S(1)}, f32[192,512]{1,0:T(8,128)S(1)}, bf16[192,512]{1,0:T(8,128)(2,1)S(1)}, bf16[192,512]{1,0:T(8,128)(2,1)S(1)}, bf1...) custom-call(f32[1,512]{1,0:T(1,128)} %bitcast.28, ...), custom_call_target="tpu_custom_call" | custom-call | flops 99999997952 | bytes 4000000 | tf_op jit(solution)/shard_map/pallas_call | solution.py:466
  16.2 0.6 %collective-permute-start.4 = (bf16[128,512]{1,0:T(8,128)(2,1)S(1)}, bf16[128,512]{1,0:T(8,128)(2,1)S(1)}, u32[]{:S(2)}, u32[]{:S(2)}) collective-permute-start(bf16[128,512]{1,0:T(8,128)(2,1)S(1)} %get-tuple-element.62), channel_id=1, source_target_pairs={{16,0},{17,1},{18,2},{19,3},{20,4},{21,5},{22,6},{23,7},{24,8},{25... | collective-permute-start | bytes 393224 | tf_op jit(solution)/shard_map/ppermute | solution.py:519
  16.8 1.7 %all-to-all-done = bf16[16,24,128]{2,1,0:T(8,128)(2,1)S(1)} async-done(((bf16[16,24,128]{2,1,0:T(8,128)(2,1)}), bf16[16,24,128]{2,1,0:T(8,128)(2,1)S(1)}, u32[]{:S(2)}, u32[]{:S(2)}) %all-to-all-start) | async-done | bytes 98336 | tf_op jit(solution)/shard_map/all_to_all | solution.py:559
  18.5 0.5 %shard_map.132 = (bf16[256,128]{1,0:T(8,128)(2,1)S(1)}, bf16[128,128]{1,0:T(8,128)(2,1)S(1)}, bf16[32,384]{1,0:T(8,128)(2,1)S(1)}, bf16[32,384]{1,0:T(8,128)(2,1)S(1)}, f32[32,384]{1,0:T(8,128)S(1)}) custom-call(bf16[384,128]{1,0:T(8,128)(2,1)S(1)} %bitcast.18, f32[128,512]{1,0:T(8,128)S(1)} %get-tuple-element.42.field), custom_call_target="tpu_custom_call" | custom-call | flops 1000000000 | bytes 2000000 | tf_op jit(solution)/shard_map/pallas_call | solution.py:466
  19.1 0.1 collective-permute-start.3
  19.2 1.5 %shard_map.133 = (f32[256,512]{1,0:T(8,128)S(1)}, f32[128,512]{1,0:T(8,128)S(1)}, bf16[1024,512]{1,0:T(8,128)(2,1)S(1)}) custom-call(bf16[512,512]{1,0:T(8,128)(2,1)} %wn_hbm.3, bf16[512,512]{1,0:T(8,128)(2,1)} %ws_hbm.3, bf16[256,128]{1,0:T(8,128)(2,1)S(1)} %get-tuple-element.43.spread_own, bf16[512,128]{1,0:T(8,128)(2,1)S(1)} %get-tuple-element.44.readout, ...), custom_call_target="tpu_custom_call" | custom-call | flops 1000000000 | bytes 3000000 | tf_op jit(solution)/shard_map/pallas_call | solution.py:466
  20.7 0.0 collective-permute-done.3.message
  20.7 0.0 collective-permute-done.2.message16
  20.7 1.7 %shard_map.134.base = f32[128,512]{1,0:T(8,128)S(1)} custom-call(f32[256,512]{1,0:T(8,128)S(1)} %get-tuple-element.48.pulled, f32[128,512]{1,0:T(8,128)S(1)} %get-tuple-element.49.away, bf16[1024,512]{1,0:T(8,128)(2,1)S(1)} %get-tuple-element.50.weights, f32[1,512]{1,0:T(1,128)S(1)} %get-tuple-element.51.gain, f32[128,512]{1,0:T(8,128)S(1)} %get-tuple-element.40.control, ...), custom_call_target="tpu_custom_call" | custom-call | flops 603979776 | bytes 6000000 | tf_op jit(solution)/shard_map/pallas_call | solution.py:466
  22.4 0.0 collective-permute-done.4.before
  22.4 0.8 %shard_map.135 = f32[128,512]{1,0:T(8,128)} custom-call(f32[128,512]{1,0:T(8,128)S(1)} %shard_map.134.base, bf16[128,512]{1,0:T(8,128)(2,1)S(1)} %get-tuple-element.61.background, bf16[128,512]{1,0:T(8,128)(2,1)S(1)} %collective-permute-done.4.before, f32[1,512]{1,0:T(1,128)S(1)} %get-tuple-element.56.error), custom_call_target="tpu_custom_call" | custom-call | flops 1000000 | bytes 900000 | tf_op jit(solution)/shard_map/pallas_call | solution.py:466
  (2 shorter events, 0.1 us)
Async XLA Ops:
  0.0 2.7 %collective-permute-start = (f32[128,512]{1,0:T(8,128)}, f32[128,512]{1,0:T(8,128)S(1)}, u32[]{:S(2)}, u32[]{:S(2)}) collective-permute-start(f32[128,512]{1,0:T(8,128)} %bitcast.20), channel_id=1, source_target_pairs={{0,1},{1,0},{2,3},{3,2},{4,5},{5,4},{6,7},{7,6},{8,9},{9,8},{10,11... | collective-permute-start | bytes 786440 | tf_op jit(solution)/shard_map/ppermute | solution.py:521
  2.7 8.4 %collective-permute-start.1 = (bf16[144,512]{1,0:T(8,128)(2,1)S(1)}, bf16[144,512]{1,0:T(8,128)(2,1)S(1)}, u32[]{:S(2)}, u32[]{:S(2)}) collective-permute-start(bf16[144,512]{1,0:T(8,128)(2,1)S(1)} %shard_map.128.refs_5_), channel_id=1, source_target_pairs={{0,15},{1,2},{2,1},{3,4},{4,3},{5,6},{6,5},{7,8},{8,7},{9,10},{10,... | collective-permute-start | bytes 442376 | tf_op jit(solution)/shard_map/ppermute | solution.py:548
  7.6 10.9 %all-to-all-start = ((bf16[16,24,128]{2,1,0:T(8,128)(2,1)}), bf16[16,24,128]{2,1,0:T(8,128)(2,1)S(1)}, u32[]{:S(2)}, u32[]{:S(2)}) async-start(bf16[16,24,128]{2,1,0:T(8,128)(2,1)} %bitcast.9), calls=%async_computation | async-start | bytes 196608 | tf_op jit(solution)/shard_map/all_to_all | solution.py:559
  11.3 9.4 %collective-permute-start.2 = (bf16[160,512]{1,0:T(8,128)(2,1)S(1)}, bf16[160,512]{1,0:T(8,128)(2,1)S(1)}, u32[]{:S(2)}, u32[]{:S(2)}) collective-permute-start(bf16[160,512]{1,0:T(8,128)(2,1)S(1)} %get-tuple-element.53), channel_id=1, source_target_pairs={{16,0},{17,1},{18,2},{19,3},{20,4},{21,5},{22,6},{23,7},{24,8},{25... | collective-permute-start | bytes 491528 | tf_op jit(solution)/shard_map/ppermute | solution.py:519
  16.2 6.2 %collective-permute-start.4 = (bf16[128,512]{1,0:T(8,128)(2,1)S(1)}, bf16[128,512]{1,0:T(8,128)(2,1)S(1)}, u32[]{:S(2)}, u32[]{:S(2)}) collective-permute-start(bf16[128,512]{1,0:T(8,128)(2,1)S(1)} %get-tuple-element.62), channel_id=1, source_target_pairs={{16,0},{17,1},{18,2},{19,3},{20,4},{21,5},{22,6},{23,7},{24,8},{25... | collective-permute-start | bytes 393224 | tf_op jit(solution)/shard_map/ppermute | solution.py:519
  19.1 1.6 %collective-permute-start.3 = (bf16[128,128]{1,0:T(8,128)(2,1)S(1)}, bf16[128,128]{1,0:T(8,128)(2,1)S(1)}, u32[]{:S(2)}, u32[]{:S(2)}) collective-permute-start(bf16[128,128]{1,0:T(8,128)(2,1)S(1)} %get-tuple-element.57), channel_id=1, source_target_pairs={{0,1},{1,0},{2,3},{3,2},{4,5},{5,4},{6,7},{7,6},{8,9},{9,8},{10,11... | collective-permute-start | bytes 98312 | tf_op jit(solution)/shard_map/ppermute | solution.py:599

commit v7 on v6

--- a/solution.py
+++ b/solution.py
@@ -348,25 +348,25 @@
             message[start : start + 16] = jnp.concatenate(near, axis=0).astype(BF16)
 
 
-def adjoint_step(u, cot, gb, flat, products, d, out, gain, weights, wo, members):
+def adjoint_step(u, cot, gb, gm, flat, d, out, gain, ws, wn, wo, members):
     both = 2 * SLIM
-    channels = flat.shape[1]
     gb[...] = cot[...].astype(BF16)
     flat[...] = dot_t(gb[...], wo[...])
     gb[...] = (flat[...] * d[...]).astype(BF16)
-    products[...] = dot_t(gb[...], weights[...])
+    gm[...] = dot_t(gb[...], wn[...])
+    flat[...] = dot_t(gb[...], ws[...])
     for m in range(members):
         base = m * both
         rows = []
         for lat in range(2):
             start = base + lat * SLIM
-            rows.append(products[start : start + SLIM, :channels].astype(BF16).astype(F32))
+            rows.append(gm[start : start + SLIM].astype(BF16).astype(F32))
         around = neighbours(rows)
         for lat in range(2):
             start = base + lat * SLIM
             x = u[start : start + SLIM]
             s = inverse_rms(x)
-            scaled = gain * (products[start : start + SLIM, channels:] + around[lat])
+            scaled = gain * (flat[start : start + SLIM] + around[lat])
             inner = jnp.mean(x * scaled, axis=-1, keepdims=True)
             out(2 * m + lat, cot[start : start + SLIM] + s * scaled - x * (s * s * s * inner))
 
@@ -387,11 +387,10 @@
 
 def pull_kernel(
     wn_hbm, ws_hbm, spread_own, readout, th, tl, scaled, arrived, field,
-    pulled, away, weights,
+    pulled, away, wn, ws,
     ph, plo, spread, near, sems,
 ):
-    channels = wn_hbm.shape[0]
-    pairs = ((wn_hbm, weights.at[pl.ds(0, channels)]), (ws_hbm, weights.at[pl.ds(channels, channels)]))
+    pairs = ((wn_hbm, wn), (ws_hbm, ws))
     copies = [pltpu.make_async_copy(source, to, sems.at[i]) for i, (source, to) in enumerate(pairs)]
     for copy in copies:
         copy.start()
@@ -408,10 +407,10 @@
 
 
 def backward_kernel(
-    pulled, away, weights, gain, control, edge0, message16, f2x, wo, readout, error, message,
+    pulled, away, wn, ws, gain, control, edge0, message16, f2x, wo, readout, error, message,
     u1x, d0x, d1x,
     result,
-    cot2, cot1, gb, flat, both, mate_pull, edge, u0x, final, nxt,
+    cot2, cot1, gb, gm, flat, mate_pull, edge, u0x, final, nxt,
 ):
     size = result.shape[0]
     members = size // 32
@@ -445,8 +444,8 @@
         a, b = r * SLIM, r * SLIM + 16
         result[r * 16 : (r + 1) * 16] = value[0:16] + error[...] * u0x[a:b]
 
-    adjoint_step(u1x, cot2, gb, flat, both, d1x, keep, gain[...], weights, wo, members)
-    adjoint_step(u0x, cot1, gb, flat, both, d0x, finish, gain[...], weights, wo, members)
+    adjoint_step(u1x, cot2, gb, gm, flat, d1x, keep, gain[...], ws, wn, wo, members)
+    adjoint_step(u0x, cot1, gb, gm, flat, d0x, finish, gain[...], ws, wn, wo, members)
 
 
 def last_kernel(base, background, before, error, result):
@@ -599,7 +598,7 @@
     from_mate = lax.ppermute(near_spread, "tile", mate_of)
     handed = kernel_call(
         pull_kernel,
-        [spec(2 * size), spec(size), spec(2 * channels, BF16)],
+        [spec(2 * size), spec(size), spec(channels, BF16), spec(channels, BF16)],
         tables + [scratch(2 * size, BF16, LANES), scratch(size, BF16, LANES), pltpu.SemaphoreType.DMA((2,))],
         10**9,
         3000000,
@@ -608,7 +607,7 @@
     base = kernel_call(
         backward_kernel,
         spec(size),
-        [scratch(slim), scratch(slim), scratch(slim, BF16), scratch(slim), scratch(slim, F32, 2 * channels)]
+        [scratch(slim), scratch(slim), scratch(slim, BF16), scratch(slim), scratch(slim)]
         + [scratch(size), scratch(16), scratch(slim), scratch(slim), scratch(size + 4 * groups)],
         12 * slim * channels * channels,
         6000000,

time: 23.4 us -> 23.1 us (0.987)
  Pallas kernels: 10.2 us -> 9.91 us
    pallas_call x9, Pallas kernels: 10.2 us -> 9.91 us  [call(): pl.pallas_call(body, out_shape=outs, in_specs=[pl.BlockSpec(memory_space=...]
  transfers between devices with their start and end apart: 6 -> 6, of which waited for: 1 -> 1; matrix products, arithmetic and copies ran while one was open for 0% -> 0% of each run, Pallas kernels for 41% -> 40%
where the time goes in v7:
time: 23.1 us; the launch traced here: 22.9 us
  starting transfers between devices  11.1 us (48%)
  Pallas kernels  9.91 us (43%)
  waiting for transfers between devices  1.76 us (8%)
    pallas_call x9, Pallas kernels, call(): pl.pallas_call(body, out_shape=outs, in_specs=[pl.BlockSpec(memory_space=...  9.91 us
    ppermute x1, starting transfers between devices, per_device(): oth = lax.ppermute(sent, 'tile', other_of)  4.88 us
    all_to_all x1, starting transfers between devices, per_device(): lax.all_to_all(packed, 'tile', split_axis=0, concat_axis=0, tiled=True)  3.52 us
    ppermute x2, starting transfers between devices, across(): return lax.ppermute(block, ('slot', 'tile'), pairs)  2.16 us
    all_to_all x1, waiting for transfers between devices, per_device(): lax.all_to_all(packed, 'tile', split_axis=0, concat_axis=0, tiled=True)  1.74 us
  transfers between devices with their start and end apart: 6, of which 1 were waited for; matrix products, arithmetic and copies ran while one was open for 0% of the time, Pallas kernels for 40%

profile of v7, /device:TPU:0, one launch (start us, length us, event | category | flops | bytes accessed | tf_op | source)
XLA Modules:
  0.0 22.9 jit_solution(5335723290801666908)
XLA Ops:
  0.0 0.5 %collective-permute-start = (f32[128,512]{1,0:T(8,128)}, f32[128,512]{1,0:T(8,128)S(1)}, u32[]{:S(2)}, u32[]{:S(2)}) collective-permute-start(f32[128,512]{1,0:T(8,128)} %bitcast.20), channel_id=1, source_target_pairs={{0,1},{1,0},{2,3},{3,2},{4,5},{5,4},{6,7},{7,6},{8,9},{9,8},{10,11... | collective-permute-start | bytes 786440 | tf_op jit(solution)/shard_map/ppermute | solution.py:520
  0.5 2.2 %shard_map.127 = (f32[128,512]{1,0:T(8,128)S(1)}, bf16[384,128]{1,0:T(8,128)(2,1)}, s32[2,1,32]{2,1,0:T(1,128)S(1)}, s32[2,4,32]{2,1,0:T(4,128)S(1)}, bf16[2,4,3...) custom-call(f32[128,512]{1,0:T(8,128)} %bitcast.21, s32[2,1,32]{2,1,0:T(1,128)} %bitcast.25, ...), custom_call_target="tpu_custom_call" | custom-call | flops 10000000 | bytes 200000 | tf_op jit(solution)/shard_map/pallas_call | solution.py:465
  2.7 0.0 collective-permute-done.mate
  2.7 4.9 %collective-permute-start.1 = (bf16[144,512]{1,0:T(8,128)(2,1)S(1)}, bf16[144,512]{1,0:T(8,128)(2,1)S(1)}, u32[]{:S(2)}, u32[]{:S(2)}) collective-permute-start(bf16[144,512]{1,0:T(8,128)(2,1)S(1)} %shard_map.128.refs_5_), channel_id=1, source_target_pairs={{0,15},{1,2},{2,1},{3,4},{4,3},{5,6},{6,5},{7,8},{8,7},{9,10},{10,... | collective-permute-start | bytes 442376 | tf_op jit(solution)/shard_map/ppermute | solution.py:547
  7.6 3.5 %all-to-all-start = ((bf16[16,24,128]{2,1,0:T(8,128)(2,1)}), bf16[16,24,128]{2,1,0:T(8,128)(2,1)S(1)}, u32[]{:S(2)}, u32[]{:S(2)}) async-start(bf16[16,24,128]{2,1,0:T(8,128)(2,1)} %bitcast.9), calls=%async_computation | async-start | bytes 196608 | tf_op jit(solution)/shard_map/all_to_all | solution.py:558
  11.1 0.0 collective-permute-done.1.oth
  11.2 0.1 shard_map.130
  11.3 1.6 %collective-permute-start.2 = (bf16[160,512]{1,0:T(8,128)(2,1)S(1)}, bf16[160,512]{1,0:T(8,128)(2,1)S(1)}, u32[]{:S(2)}, u32[]{:S(2)}) collective-permute-start(bf16[160,512]{1,0:T(8,128)(2,1)S(1)} %get-tuple-element.55), channel_id=1, source_target_pairs={{16,0},{17,1},{18,2},{19,3},{20,4},{21,5},{22,6},{23,7},{24,8},{25... | collective-permute-start | bytes 491528 | tf_op jit(solution)/shard_map/ppermute | solution.py:518
  12.8 3.3 %shard_map.131 = (f32[64,512]{1,0:T(8,128)S(1)}, f32[192,512]{1,0:T(8,128)S(1)}, bf16[192,512]{1,0:T(8,128)(2,1)S(1)}, bf16[192,512]{1,0:T(8,128)(2,1)S(1)}, bf1...) custom-call(f32[1,512]{1,0:T(1,128)} %bitcast.28, ...), custom_call_target="tpu_custom_call" | custom-call | flops 99999997952 | bytes 4000000 | tf_op jit(solution)/shard_map/pallas_call | solution.py:465
  16.2 0.6 %collective-permute-start.4 = (bf16[128,512]{1,0:T(8,128)(2,1)S(1)}, bf16[128,512]{1,0:T(8,128)(2,1)S(1)}, u32[]{:S(2)}, u32[]{:S(2)}) collective-permute-start(bf16[128,512]{1,0:T(8,128)(2,1)S(1)} %get-tuple-element.64), channel_id=1, source_target_pairs={{16,0},{17,1},{18,2},{19,3},{20,4},{21,5},{22,6},{23,7},{24,8},{25... | collective-permute-start | bytes 393224 | tf_op jit(solution)/shard_map/ppermute | solution.py:518
  16.8 1.7 %all-to-all-done = bf16[16,24,128]{2,1,0:T(8,128)(2,1)S(1)} async-done(((bf16[16,24,128]{2,1,0:T(8,128)(2,1)}), bf16[16,24,128]{2,1,0:T(8,128)(2,1)S(1)}, u32[]{:S(2)}, u32[]{:S(2)}) %all-to-all-start) | async-done | bytes 98336 | tf_op jit(solution)/shard_map/all_to_all | solution.py:558
  18.5 0.5 %shard_map.132 = (bf16[256,128]{1,0:T(8,128)(2,1)S(1)}, bf16[128,128]{1,0:T(8,128)(2,1)S(1)}, bf16[32,384]{1,0:T(8,128)(2,1)S(1)}, bf16[32,384]{1,0:T(8,128)(2,1)S(1)}, f32[32,384]{1,0:T(8,128)S(1)}) custom-call(bf16[384,128]{1,0:T(8,128)(2,1)S(1)} %bitcast.18, f32[128,512]{1,0:T(8,128)S(1)} %get-tuple-element.43.field), custom_call_target="tpu_custom_call" | custom-call | flops 1000000000 | bytes 2000000 | tf_op jit(solution)/shard_map/pallas_call | solution.py:465
  19.1 0.1 collective-permute-start.3
  19.2 1.2 %shard_map.133 = (f32[256,512]{1,0:T(8,128)S(1)}, f32[128,512]{1,0:T(8,128)S(1)}, bf16[512,512]{1,0:T(8,128)(2,1)S(1)}, bf16[512,512]{1,0:T(8,128)(2,1)S(1)}) custom-call(bf16[512,512]{1,0:T(8,128)(2,1)} %wn_hbm.3, bf16[512,512]{1,0:T(8,128)(2,1)} %ws_hbm.3, bf16[256,128]{1,0:T(8,128)(2,1)S(1)} %get-tuple-element.44.spread_own, ...), custom_call_target="tpu_custom_call" | custom-call | flops 1000000000 | bytes 3000000 | tf_op jit(solution)/shard_map/pallas_call | solution.py:465
  20.4 0.0 collective-permute-done.3.message
  20.4 0.0 collective-permute-done.2.message16
  20.4 1.7 %shard_map.134.base = f32[128,512]{1,0:T(8,128)S(1)} custom-call(f32[256,512]{1,0:T(8,128)S(1)} %get-tuple-element.49.pulled, f32[128,512]{1,0:T(8,128)S(1)} %get-tuple-element.50.away, bf16[512,512]{1,0:T(8,128)(2,1)S(1)} %get-tuple-element.51.wn, bf16[512,512]{1,0:T(8,128)(2,1)S(1)} %get-tuple-element.52.ws, f32[1,512]{1,0:T(1,128)S(1)} %get-tuple-element.53.gain, ...), custom_call_target="tpu_custom_call" | custom-call | flops 603979776 | bytes 6000000 | tf_op jit(solution)/shard_map/pallas_call | solution.py:465
  22.1 0.0 collective-permute-done.4.before
  22.1 0.8 %shard_map.135 = f32[128,512]{1,0:T(8,128)} custom-call(f32[128,512]{1,0:T(8,128)S(1)} %shard_map.134.base, bf16[128,512]{1,0:T(8,128)(2,1)S(1)} %get-tuple-element.63.background, bf16[128,512]{1,0:T(8,128)(2,1)S(1)} %collective-permute-done.4.before, f32[1,512]{1,0:T(1,128)S(1)} %get-tuple-element.58.error), custom_call_target="tpu_custom_call" | custom-call | flops 1000000 | bytes 900000 | tf_op jit(solution)/shard_map/pallas_call | solution.py:465
  (2 shorter events, 0.1 us)
Async XLA Ops:
  0.0 2.7 %collective-permute-start = (f32[128,512]{1,0:T(8,128)}, f32[128,512]{1,0:T(8,128)S(1)}, u32[]{:S(2)}, u32[]{:S(2)}) collective-permute-start(f32[128,512]{1,0:T(8,128)} %bitcast.20), channel_id=1, source_target_pairs={{0,1},{1,0},{2,3},{3,2},{4,5},{5,4},{6,7},{7,6},{8,9},{9,8},{10,11... | collective-permute-start | bytes 786440 | tf_op jit(solution)/shard_map/ppermute | solution.py:520
  2.7 8.4 %collective-permute-start.1 = (bf16[144,512]{1,0:T(8,128)(2,1)S(1)}, bf16[144,512]{1,0:T(8,128)(2,1)S(1)}, u32[]{:S(2)}, u32[]{:S(2)}) collective-permute-start(bf16[144,512]{1,0:T(8,128)(2,1)S(1)} %shard_map.128.refs_5_), channel_id=1, source_target_pairs={{0,15},{1,2},{2,1},{3,4},{4,3},{5,6},{6,5},{7,8},{8,7},{9,10},{10,... | collective-permute-start | bytes 442376 | tf_op jit(solution)/shard_map/ppermute | solution.py:547
  7.6 10.9 %all-to-all-start = ((bf16[16,24,128]{2,1,0:T(8,128)(2,1)}), bf16[16,24,128]{2,1,0:T(8,128)(2,1)S(1)}, u32[]{:S(2)}, u32[]{:S(2)}) async-start(bf16[16,24,128]{2,1,0:T(8,128)(2,1)} %bitcast.9), calls=%async_computation | async-start | bytes 196608 | tf_op jit(solution)/shard_map/all_to_all | solution.py:558
  11.3 9.1 %collective-permute-start.2 = (bf16[160,512]{1,0:T(8,128)(2,1)S(1)}, bf16[160,512]{1,0:T(8,128)(2,1)S(1)}, u32[]{:S(2)}, u32[]{:S(2)}) collective-permute-start(bf16[160,512]{1,0:T(8,128)(2,1)S(1)} %get-tuple-element.55), channel_id=1, source_target_pairs={{16,0},{17,1},{18,2},{19,3},{20,4},{21,5},{22,6},{23,7},{24,8},{25... | collective-permute-start | bytes 491528 | tf_op jit(solution)/shard_map/ppermute | solution.py:518
  16.2 5.9 %collective-permute-start.4 = (bf16[128,512]{1,0:T(8,128)(2,1)S(1)}, bf16[128,512]{1,0:T(8,128)(2,1)S(1)}, u32[]{:S(2)}, u32[]{:S(2)}) collective-permute-start(bf16[128,512]{1,0:T(8,128)(2,1)S(1)} %get-tuple-element.64), channel_id=1, source_target_pairs={{16,0},{17,1},{18,2},{19,3},{20,4},{21,5},{22,6},{23,7},{24,8},{25... | collective-permute-start | bytes 393224 | tf_op jit(solution)/shard_map/ppermute | solution.py:518
  19.1 1.3 %collective-permute-start.3 = (bf16[128,128]{1,0:T(8,128)(2,1)S(1)}, bf16[128,128]{1,0:T(8,128)(2,1)S(1)}, u32[]{:S(2)}, u32[]{:S(2)}) collective-permute-start(bf16[128,128]{1,0:T(8,128)(2,1)S(1)} %get-tuple-element.59), channel_id=1, source_target_pairs={{0,1},{1,0},{2,3},{3,2},{4,5},{5,4},{6,7},{7,6},{8,9},{9,8},{10,11... | collective-permute-start | bytes 98312 | tf_op jit(solution)/shard_map/ppermute | solution.py:598

commit v8 on v7

--- a/solution.py
+++ b/solution.py
@@ -211,8 +211,8 @@
 
 def forward_kernel(
     gain_hbm, ws_hbm, wn_hbm, wo_hbm, readout_hbm, error_hbm, background_hbm, control, mate, oth,
-    edge0, u1x, d0x, d1x, f2x, field, final, wo, readout, gain, error, background,
-    ua, ub, n, act, pre, edge, states, weights, sems,
+    edge0, u1x, d0x, d1x, f2x, field, final, wo_turned, readout, gain, error, background, ws_hbm_turned, wn_hbm_turned,
+    ua, ub, n, act, pre, edge, states, weights, wo, turned, sems,
 ):
     channels = wo.shape[0]
     halves = weights.at[pl.ds(0, channels)], weights.at[pl.ds(channels, channels)]
@@ -259,6 +259,12 @@
             states[away + r * 16 : away + (r + 1) * 16] = taken.astype(BF16)
 
     forward_step(ua, n, act, pre, d0x, g, weights, wo, WIDE, members, keep(ub), copies[1:])
+    stores = []
+    for i, place in enumerate((ws_hbm_turned, wn_hbm_turned)):
+        turned[i] = jnp.transpose(halves[i][...])
+        stores.append(pltpu.make_async_copy(turned.at[i], place, sems.at[7 + i]))
+        stores[-1].start()
+    wo_turned[...] = jnp.transpose(wo[...])
     for m in range(members):
         slim_copy(u1x, ub, m)
     keep_states(ub, 0)
@@ -272,6 +278,8 @@
         for m in range(members):
             start = (q * members + m) * 32
             field[q * 32 : (q + 1) * 32, m * LANES : (m + 1) * LANES] = read[start : start + 32]
+    for store in stores:
+        store.wait()
 
 
 def split(x):
@@ -279,7 +287,7 @@
     return high, (x - high.astype(F32)).astype(BF16)
 
 
-def spread_of(first, th, tl, scaled, taken, field, ph, plo, spread):
+def spread_of(first, th, tl, scaled, taken, field, pp, spread):
     lane = lax.broadcasted_iota(jnp.int32, (1, LANES), 1)
     members = field.shape[1] // LANES
     for p in range(th.shape[1] // LANES):
@@ -288,14 +296,17 @@
         table_of = jnp.where(slot < SLOTS, slot // CAP, -1)
         for q in range(2):
             kept = jnp.where(table_of == first + q, scaled[:, at], 0.0)
-            ph[q * 32 : (q + 1) * 32, at], plo[q * 32 : (q + 1) * 32, at] = split(kept)
-    cross = dot_t(ph[...], th[...]) + dot_t(plo[...], th[...]) + dot_t(ph[...], tl[...])
+            pp[q * 32 : (q + 1) * 32, at], pp[64 + q * 32 : 96 + q * 32, at] = split(kept)
+    cross = dot_t(pp[...], th[...])
+    cross = cross[:64] + cross[64:] + dot_t(pp[0:64], tl[...])
     block = jnp.concatenate([cross] * 2, axis=1)
     on_block = sublane(block.shape) // 32 == lax.broadcasted_iota(jnp.int32, block.shape, 1) // 32
-    target = dot(ph[...], taken[...]) + dot(plo[...], taken[...])
+    target = dot(pp[...], taken[...])
+    target = target[:64] + target[64:]
     ch, cl = split(jnp.where(on_block, block, 0.0))
     fh, fl = split(field[first * 32 : (first + 2) * 32])
-    mixed = dot(ch, fh) + dot(cl, fh) + dot(ch, fl)
+    mixed = dot(jnp.concatenate([ch, cl], axis=0), fh)
+    mixed = mixed[:64] + mixed[64:] + dot(ch, fl)
     for q in range(2):
         for m in range(members):
             start = (q * members + m) * 32
@@ -306,7 +317,7 @@
 def observe_kernel(
     tiles, arrived, field,
     spread, message, th, tl, scaled,
-    ph, plo, wide,
+    pp, wide,
 ):
     steps = 2
     members = field.shape[1] // LANES
@@ -337,7 +348,7 @@
         at = slice(p * LANES, (p + 1) * LANES)
         th[:, at], tl[:, at] = split(weight)
         scaled[:, at] = weight * entry[8]
-    spread_of(0, th, tl, scaled, arrived, field, ph, plo, spread)
+    spread_of(0, th, tl, scaled, arrived, field, pp, spread)
     size = members * 32
     for k in range(steps):
         for m in range(members):
@@ -351,10 +362,10 @@
 def adjoint_step(u, cot, gb, gm, flat, d, out, gain, ws, wn, wo, members):
     both = 2 * SLIM
     gb[...] = cot[...].astype(BF16)
-    flat[...] = dot_t(gb[...], wo[...])
+    flat[...] = dot(gb[...], wo[...])
     gb[...] = (flat[...] * d[...]).astype(BF16)
-    gm[...] = dot_t(gb[...], wn[...])
-    flat[...] = dot_t(gb[...], ws[...])
+    gm[...] = dot(gb[...], wn[...])
+    flat[...] = dot(gb[...], ws[...])
     for m in range(members):
         base = m * both
         rows = []
@@ -388,7 +399,7 @@
 def pull_kernel(
     wn_hbm, ws_hbm, spread_own, readout, th, tl, scaled, arrived, field,
     pulled, away, wn, ws,
-    ph, plo, spread, near, sems,
+    pp, spread, near, sems,
 ):
     pairs = ((wn_hbm, wn), (ws_hbm, ws))
     copies = [pltpu.make_async_copy(source, to, sems.at[i]) for i, (source, to) in enumerate(pairs)]
@@ -396,7 +407,7 @@
         copy.start()
     even = lax.rem(lax.axis_index("tile"), 2) == 0
     pulled[...] = dot_t(spread_own[...], readout[...])
-    spread_of(2, th, tl, scaled, arrived, field, ph, plo, spread)
+    spread_of(2, th, tl, scaled, arrived, field, pp, spread)
     for start in range(0, spread.shape[0], 32):
         pair = spread[start : start + 32].astype(F32)
         rows = [jnp.where(even, pair[i + 8 : i + 16], pair[i : i + 8]) for i in (0, 16)]
@@ -569,24 +580,28 @@
     slim = groups * SLIM
     (
         edge0, u1x, d0x, d1x, f2x, field, final, wo, readout_held, gain_held, error_held, background_held,
+        ws_turned, wn_turned,
     ) = kernel_call(
         forward_kernel,
         [spec(groups * 8), spec(slim)] + [spec(slim, BF16)] * 3
         + [spec(4 * lats * cols, F32, members * LANES), spec(size, BF16)]
-        + [spec(channels, BF16), spec(channels, BF16, LANES), spec(1), spec(1), spec(size, BF16)],
+        + [spec(channels, BF16), spec(channels, BF16, LANES), spec(1), spec(1), spec(size, BF16)]
+        + [spec(channels, BF16), spec(channels, BF16)],
         [scratch(wide), scratch(wide), scratch(wide, BF16, 2 * channels), scratch(wide, BF16)]
         + [scratch(wide), scratch(16), scratch(4 * size, BF16)]
-        + [scratch(2 * channels, BF16), pltpu.SemaphoreType.DMA((7,))],
+        + [scratch(2 * channels, BF16), scratch(channels, BF16), pltpu.VMEM((2, channels, channels), BF16)]
+        + [pltpu.SemaphoreType.DMA((9,))],
         10**11,
         4000000,
         hbm=7,
+        out_places=[pltpu.VMEM] * 12 + [pltpu.HBM] * 2,
     )(
         gain, self_weight, neighbour_weight, output_weight, readout, error, background.reshape(size, channels),
         held, near4, oth,
     )
     before = across(final, -1)
     total = tiles * CHUNK
-    tables = [scratch(64, BF16, total), scratch(64, BF16, total)]
+    tables = [scratch(128, BF16, total)]
     spread, near_spread, *reports_held = kernel_call(
         functools.partial(observe_kernel, tiles),
         [spec(2 * size, BF16, LANES), spec(size, BF16, LANES)]
@@ -603,7 +618,7 @@
         10**9,
         3000000,
         hbm=2,
-    )(neighbour_weight, self_weight, spread, readout_held, *reports_held, arrived, field)
+    )(wn_turned, ws_turned, spread, readout_held, *reports_held, arrived, field)
     base = kernel_call(
         backward_kernel,
         spec(size),

time: 23.1 us -> 24.5 us (1.061)
  local copies, waits for them, and re-layouts: 0 us -> 1.58 us
  waiting for transfers between devices: 1.76 us -> 1.37 us
  Pallas kernels: 9.91 us -> 10.2 us
    all_to_all x1, waiting for transfers between devices: 1.74 us -> 0.01 us  [per_device(): lax.all_to_all(packed, 'tile', split_axis=0, concat_axis=0, tiled=True)]
    unnamed x0 -> x4, local copies, waits for them, and re-layouts: none -> 1.58 us
    ppermute x2, waiting for transfers between devices: 0.01 us -> 1.36 us  [across(): return lax.ppermute(block, ('slot', 'tile'), pairs)]
    pallas_call x9, Pallas kernels: 9.91 us -> 10.2 us  [call(): pl.pallas_call(body, out_shape=outs, in_specs=[pl.BlockSpec(memory_space=...]
  transfers between devices with their start and end apart: 6 -> 6, of which waited for: 1 -> 1; matrix products, arithmetic and copies ran while one was open for 0% -> 0% of each run, Pallas kernels for 40% -> 39%
where the time goes in v8:
time: 24.5 us; the launch traced here: 24.3 us
  starting transfers between devices  11 us (45%)
  Pallas kernels  10.2 us (42%)
  local copies, waits for them, and re-layouts  1.58 us (6%)
  waiting for transfers between devices  1.37 us (6%)
    pallas_call x9, Pallas kernels, call(): pl.pallas_call(body, out_shape=outs, in_specs=[pl.BlockSpec(memory_space=...  10.2 us
    ppermute x1, starting transfers between devices, per_device(): oth = lax.ppermute(sent, 'tile', other_of)  4.88 us
    all_to_all x1, starting transfers between devices, per_device(): lax.all_to_all(packed, 'tile', split_axis=0, concat_axis=0, tiled=True)  3.52 us
    ppermute x2, starting transfers between devices, across(): return lax.ppermute(block, ('slot', 'tile'), pairs)  2.1 us
    unnamed x4, local copies, waits for them, and re-layouts  1.58 us
    ppermute x2, waiting for transfers between devices, across(): return lax.ppermute(block, ('slot', 'tile'), pairs)  1.36 us
  transfers between devices with their start and end apart: 6, of which 1 were waited for; matrix products, arithmetic and copies ran while one was open for 0% of the time, Pallas kernels for 39%

profile of v8, /device:TPU:0, one launch (start us, length us, event | category | flops | bytes accessed | tf_op | source)
XLA Modules:
  0.0 24.3 jit_solution(17479278260515955059)
XLA Ops:
  0.0 0.5 %collective-permute-start = (f32[128,512]{1,0:T(8,128)}, f32[128,512]{1,0:T(8,128)S(1)}, u32[]{:S(2)}, u32[]{:S(2)}) collective-permute-start(f32[128,512]{1,0:T(8,128)} %bitcast.20), channel_id=1, source_target_pairs={{0,1},{1,0},{2,3},{3,2},{4,5},{5,4},{6,7},{7,6},{8,9},{9,8},{10,11... | collective-permute-start | bytes 786440 | tf_op jit(solution)/shard_map/ppermute | solution.py:531
  0.5 2.2 %shard_map.127 = (f32[128,512]{1,0:T(8,128)S(1)}, bf16[384,128]{1,0:T(8,128)(2,1)}, s32[2,1,32]{2,1,0:T(1,128)S(1)}, s32[2,4,32]{2,1,0:T(4,128)S(1)}, bf16[2,4,3...) custom-call(f32[128,512]{1,0:T(8,128)} %bitcast.21, s32[2,1,32]{2,1,0:T(1,128)} %bitcast.25, ...), custom_call_target="tpu_custom_call" | custom-call | flops 10000000 | bytes 200000 | tf_op jit(solution)/shard_map/pallas_call | solution.py:476
  2.7 0.0 collective-permute-done.mate
  2.7 4.9 %collective-permute-start.1 = (bf16[144,512]{1,0:T(8,128)(2,1)S(1)}, bf16[144,512]{1,0:T(8,128)(2,1)S(1)}, u32[]{:S(2)}, u32[]{:S(2)}) collective-permute-start(bf16[144,512]{1,0:T(8,128)(2,1)S(1)} %shard_map.128.refs_5_), channel_id=1, source_target_pairs={{0,15},{1,2},{2,1},{3,4},{4,3},{5,6},{6,5},{7,8},{8,7},{9,10},{10,... | collective-permute-start | bytes 442376 | tf_op jit(solution)/shard_map/ppermute | solution.py:558
  7.6 3.5 %all-to-all-start = ((bf16[16,24,128]{2,1,0:T(8,128)(2,1)}), bf16[16,24,128]{2,1,0:T(8,128)(2,1)S(1)}, u32[]{:S(2)}, u32[]{:S(2)}) async-start(bf16[16,24,128]{2,1,0:T(8,128)(2,1)} %bitcast.12), calls=%async_computation | async-start | bytes 196608 | tf_op jit(solution)/shard_map/all_to_all | solution.py:569
  11.1 0.0 collective-permute-done.1.oth
  11.2 0.1 shard_map.129
  11.3 1.6 %collective-permute-start.2 = (bf16[160,512]{1,0:T(8,128)(2,1)S(1)}, bf16[160,512]{1,0:T(8,128)(2,1)S(1)}, u32[]{:S(2)}, u32[]{:S(2)}) collective-permute-start(bf16[160,512]{1,0:T(8,128)(2,1)S(1)} %get-tuple-element.59), channel_id=1, source_target_pairs={{16,0},{17,1},{18,2},{19,3},{20,4},{21,5},{22,6},{23,7},{24,8},{25... | collective-permute-start | bytes 491528 | tf_op jit(solution)/shard_map/ppermute | solution.py:529
  12.8 3.7 %shard_map.130 = (f32[64,512]{1,0:T(8,128)S(1)}, f32[192,512]{1,0:T(8,128)S(1)}, bf16[192,512]{1,0:T(8,128)(2,1)S(1)}, bf16[192,512]{1,0:T(8,128)(2,1)S(1)}, bf1...) custom-call(f32[1,512]{1,0:T(1,128)} %bitcast.28, ...), custom_call_target="tpu_custom_call" | custom-call | flops 99999997952 | bytes 4000000 | tf_op jit(solution)/shard_map/pallas_call | solution.py:476
  16.5 0.0 copy-start
  16.6 0.8 %copy-done = bf16[512,512]{1,0:T(8,128)(2,1)} copy-done((bf16[512,512]{1,0:T(8,128)(2,1)}, bf16[512,512]{1,0:T(8,128)(2,1)S(1)}, u32[]{:S(2)}) %copy-start) | copy-done | bytes 524312
  17.3 0.0 copy-start.1
  17.3 0.8 %copy-done.1 = bf16[512,512]{1,0:T(8,128)(2,1)} copy-done((bf16[512,512]{1,0:T(8,128)(2,1)}, bf16[512,512]{1,0:T(8,128)(2,1)S(1)}, u32[]{:S(2)}) %copy-start.1) | copy-done | bytes 524312
  18.1 0.5 %collective-permute-start.4 = (bf16[128,512]{1,0:T(8,128)(2,1)S(1)}, bf16[128,512]{1,0:T(8,128)(2,1)S(1)}, u32[]{:S(2)}, u32[]{:S(2)}) collective-permute-start(bf16[128,512]{1,0:T(8,128)(2,1)S(1)} %get-tuple-element.68), channel_id=1, source_target_pairs={{16,0},{17,1},{18,2},{19,3},{20,4},{21,5},{22,6},{23,7},{24,8},{25... | collective-permute-start | bytes 393224 | tf_op jit(solution)/shard_map/ppermute | solution.py:529
  18.7 0.0 all-to-all-done
  18.7 0.5 %shard_map.132 = (bf16[256,128]{1,0:T(8,128)(2,1)S(1)}, bf16[128,128]{1,0:T(8,128)(2,1)S(1)}, bf16[32,384]{1,0:T(8,128)(2,1)S(1)}, bf16[32,384]{1,0:T(8,128)(2,1)S(1)}, f32[32,384]{1,0:T(8,128)S(1)}) custom-call(bf16[384,128]{1,0:T(8,128)(2,1)S(1)} %bitcast.18, f32[128,512]{1,0:T(8,128)S(1)} %get-tuple-element.47.field), custom_call_target="tpu_custom_call" | custom-call | flops 1000000000 | bytes 2000000 | tf_op jit(solution)/shard_map/pallas_call | solution.py:476
  19.2 0.1 collective-permute-start.3
  19.3 1.3 %shard_map.133 = (f32[256,512]{1,0:T(8,128)S(1)}, f32[128,512]{1,0:T(8,128)S(1)}, bf16[512,512]{1,0:T(8,128)(2,1)S(1)}, bf16[512,512]{1,0:T(8,128)(2,1)S(1)}) custom-call(bf16[512,512]{1,0:T(8,128)(2,1)} %copy-done.1, bf16[512,512]{1,0:T(8,128)(2,1)} %copy-done, bf16[256,128]{1,0:T(8,128)(2,1)S(1)} %get-tuple-element.48.spread_own, ...), custom_call_target="tpu_custom_call" | custom-call | flops 1000000000 | bytes 3000000 | tf_op jit(solution)/shard_map/pallas_call | solution.py:476
  20.6 0.0 collective-permute-done.3.message
  20.6 0.0 collective-permute-done.2.message16
  20.6 1.5 %shard_map.134.base = f32[128,512]{1,0:T(8,128)S(1)} custom-call(f32[256,512]{1,0:T(8,128)S(1)} %get-tuple-element.53.pulled, f32[128,512]{1,0:T(8,128)S(1)} %get-tuple-element.54.away, bf16[512,512]{1,0:T(8,128)(2,1)S(1)} %get-tuple-element.55.wn, bf16[512,512]{1,0:T(8,128)(2,1)S(1)} %get-tuple-element.56.ws, f32[1,512]{1,0:T(1,128)S(1)} %get-tuple-element.57.gain, ...), custom_call_target="tpu_custom_call" | custom-call | flops 603979776 | bytes 6000000 | tf_op jit(solution)/shard_map/pallas_call | solution.py:476
  22.2 1.4 %collective-permute-done.4.before = bf16[128,512]{1,0:T(8,128)(2,1)S(1)} collective-permute-done((bf16[128,512]{1,0:T(8,128)(2,1)S(1)}, bf16[128,512]{1,0:T(8,128)(2,1)S(1)}, u32[]{:S(2)}, u32[]{:S(2)}) %collective-permute-start.4) | collective-permute-done | bytes 131104 | tf_op jit(solution)/shard_map/ppermute | solution.py:529
  23.5 0.8 %shard_map.135 = f32[128,512]{1,0:T(8,128)} custom-call(f32[128,512]{1,0:T(8,128)S(1)} %shard_map.134.base, bf16[128,512]{1,0:T(8,128)(2,1)S(1)} %get-tuple-element.67.background, bf16[128,512]{1,0:T(8,128)(2,1)S(1)} %collective-permute-done.4.before, f32[1,512]{1,0:T(1,128)S(1)} %get-tuple-element.62.error), custom_call_target="tpu_custom_call" | custom-call | flops 1000000 | bytes 900000 | tf_op jit(solution)/shard_map/pallas_call | solution.py:476
  (2 shorter events, 0.1 us)
Async XLA Ops:
  0.0 2.7 %collective-permute-start = (f32[128,512]{1,0:T(8,128)}, f32[128,512]{1,0:T(8,128)S(1)}, u32[]{:S(2)}, u32[]{:S(2)}) collective-permute-start(f32[128,512]{1,0:T(8,128)} %bitcast.20), channel_id=1, source_target_pairs={{0,1},{1,0},{2,3},{3,2},{4,5},{5,4},{6,7},{7,6},{8,9},{9,8},{10,11... | collective-permute-start | bytes 786440 | tf_op jit(solution)/shard_map/ppermute | solution.py:531
  2.7 8.4 %collective-permute-start.1 = (bf16[144,512]{1,0:T(8,128)(2,1)S(1)}, bf16[144,512]{1,0:T(8,128)(2,1)S(1)}, u32[]{:S(2)}, u32[]{:S(2)}) collective-permute-start(bf16[144,512]{1,0:T(8,128)(2,1)S(1)} %shard_map.128.refs_5_), channel_id=1, source_target_pairs={{0,15},{1,2},{2,1},{3,4},{4,3},{5,6},{6,5},{7,8},{8,7},{9,10},{10,... | collective-permute-start | bytes 442376 | tf_op jit(solution)/shard_map/ppermute | solution.py:558
  7.6 11.1 %all-to-all-start = ((bf16[16,24,128]{2,1,0:T(8,128)(2,1)}), bf16[16,24,128]{2,1,0:T(8,128)(2,1)S(1)}, u32[]{:S(2)}, u32[]{:S(2)}) async-start(bf16[16,24,128]{2,1,0:T(8,128)(2,1)} %bitcast.12), calls=%async_computation | async-start | bytes 196608 | tf_op jit(solution)/shard_map/all_to_all | solution.py:569
  11.3 9.4 %collective-permute-start.2 = (bf16[160,512]{1,0:T(8,128)(2,1)S(1)}, bf16[160,512]{1,0:T(8,128)(2,1)S(1)}, u32[]{:S(2)}, u32[]{:S(2)}) collective-permute-start(bf16[160,512]{1,0:T(8,128)(2,1)S(1)} %get-tuple-element.59), channel_id=1, source_target_pairs={{16,0},{17,1},{18,2},{19,3},{20,4},{21,5},{22,6},{23,7},{24,8},{25... | collective-permute-start | bytes 491528 | tf_op jit(solution)/shard_map/ppermute | solution.py:529
  16.5 0.8 %copy-start = (bf16[512,512]{1,0:T(8,128)(2,1)}, bf16[512,512]{1,0:T(8,128)(2,1)S(1)}, u32[]{:S(2)}) copy-start(bf16[512,512]{1,0:T(8,128)(2,1)S(1)} %get-tuple-element.40.ws_hbm) | copy-start | bytes 1572868
  17.3 0.8 %copy-start.1 = (bf16[512,512]{1,0:T(8,128)(2,1)}, bf16[512,512]{1,0:T(8,128)(2,1)S(1)}, u32[]{:S(2)}) copy-start(bf16[512,512]{1,0:T(8,128)(2,1)S(1)} %get-tuple-element.39.wn_hbm) | copy-start | bytes 1572868
  18.1 5.4 %collective-permute-start.4 = (bf16[128,512]{1,0:T(8,128)(2,1)S(1)}, bf16[128,512]{1,0:T(8,128)(2,1)S(1)}, u32[]{:S(2)}, u32[]{:S(2)}) collective-permute-start(bf16[128,512]{1,0:T(8,128)(2,1)S(1)} %get-tuple-element.68), channel_id=1, source_target_pairs={{16,0},{17,1},{18,2},{19,3},{20,4},{21,5},{22,6},{23,7},{24,8},{25... | collective-permute-start | bytes 393224 | tf_op jit(solution)/shard_map/ppermute | solution.py:529
  19.2 1.4 %collective-permute-start.3 = (bf16[128,128]{1,0:T(8,128)(2,1)S(1)}, bf16[128,128]{1,0:T(8,128)(2,1)S(1)}, u32[]{:S(2)}, u32[]{:S(2)}) collective-permute-start(bf16[128,128]{1,0:T(8,128)(2,1)S(1)} %get-tuple-element.63), channel_id=1, source_target_pairs={{0,1},{1,0},{2,3},{3,2},{4,5},{5,4},{6,7},{7,6},{8,9},{9,8},{10,11... | collective-permute-start | bytes 98312 | tf_op jit(solution)/shard_map/ppermute | solution.py:613

commit v9 on v8

--- a/solution.py
+++ b/solution.py
@@ -211,7 +211,7 @@
 
 def forward_kernel(
     gain_hbm, ws_hbm, wn_hbm, wo_hbm, readout_hbm, error_hbm, background_hbm, control, mate, oth,
-    edge0, u1x, d0x, d1x, f2x, field, final, wo_turned, readout, gain, error, background, ws_hbm_turned, wn_hbm_turned,
+    edge0, u1x, d0x, d1x, f2x, field, final, wo_turned, readout, gain, error, background, both_hbm,
     ua, ub, n, act, pre, edge, states, weights, wo, turned, sems,
 ):
     channels = wo.shape[0]
@@ -259,11 +259,10 @@
             states[away + r * 16 : away + (r + 1) * 16] = taken.astype(BF16)
 
     forward_step(ua, n, act, pre, d0x, g, weights, wo, WIDE, members, keep(ub), copies[1:])
-    stores = []
-    for i, place in enumerate((ws_hbm_turned, wn_hbm_turned)):
-        turned[i] = jnp.transpose(halves[i][...])
-        stores.append(pltpu.make_async_copy(turned.at[i], place, sems.at[7 + i]))
-        stores[-1].start()
+    for i in range(2):
+        turned[i * channels : (i + 1) * channels] = jnp.transpose(halves[i][...])
+    store = pltpu.make_async_copy(turned, both_hbm, sems.at[7])
+    store.start()
     wo_turned[...] = jnp.transpose(wo[...])
     for m in range(members):
         slim_copy(u1x, ub, m)
@@ -278,8 +277,7 @@
         for m in range(members):
             start = (q * members + m) * 32
             field[q * 32 : (q + 1) * 32, m * LANES : (m + 1) * LANES] = read[start : start + 32]
-    for store in stores:
-        store.wait()
+    store.wait()
 
 
 def split(x):
@@ -397,11 +395,12 @@
 
 
 def pull_kernel(
-    wn_hbm, ws_hbm, spread_own, readout, th, tl, scaled, arrived, field,
+    both_hbm, spread_own, readout, th, tl, scaled, arrived, field,
     pulled, away, wn, ws,
     pp, spread, near, sems,
 ):
-    pairs = ((wn_hbm, wn), (ws_hbm, ws))
+    channels = wn.shape[0]
+    pairs = ((both_hbm.at[pl.ds(channels, channels)], wn), (both_hbm.at[pl.ds(0, channels)], ws))
     copies = [pltpu.make_async_copy(source, to, sems.at[i]) for i, (source, to) in enumerate(pairs)]
     for copy in copies:
         copy.start()
@@ -465,11 +464,11 @@
     result[...] = base[...] - error[...] * taken
 
 
-def kernel_call(body, outs, scratch, flops, moved, hbm=0, out_places=None, aliases={}):
+def kernel_call(body, outs, scratch, flops, moved, hbm=0, out_places=None, aliases={}, fixed=True):
     def call(*operands):
-        fixed = [i in range(hbm) and i not in aliases for i in range(len(operands))]
+        there = [fixed and i < hbm and i not in aliases for i in range(len(operands))]
         operands = [
-            pltpu.with_memory_space_constraint(x, pltpu.HBM) if fix else x for x, fix in zip(operands, fixed)
+            pltpu.with_memory_space_constraint(x, pltpu.HBM) if fix else x for x, fix in zip(operands, there)
         ]
         places = [pltpu.HBM] * hbm + [pltpu.VMEM] * (len(operands) - hbm)
         given = {} if out_places is None else {"out_specs": [pl.BlockSpec(memory_space=p) for p in out_places]}
@@ -580,21 +579,21 @@
     slim = groups * SLIM
     (
         edge0, u1x, d0x, d1x, f2x, field, final, wo, readout_held, gain_held, error_held, background_held,
-        ws_turned, wn_turned,
+        both_turned,
     ) = kernel_call(
         forward_kernel,
         [spec(groups * 8), spec(slim)] + [spec(slim, BF16)] * 3
         + [spec(4 * lats * cols, F32, members * LANES), spec(size, BF16)]
         + [spec(channels, BF16), spec(channels, BF16, LANES), spec(1), spec(1), spec(size, BF16)]
-        + [spec(channels, BF16), spec(channels, BF16)],
+        + [spec(2 * channels, BF16)],
         [scratch(wide), scratch(wide), scratch(wide, BF16, 2 * channels), scratch(wide, BF16)]
         + [scratch(wide), scratch(16), scratch(4 * size, BF16)]
-        + [scratch(2 * channels, BF16), scratch(channels, BF16), pltpu.VMEM((2, channels, channels), BF16)]
-        + [pltpu.SemaphoreType.DMA((9,))],
+        + [scratch(2 * channels, BF16), scratch(channels, BF16), scratch(2 * channels, BF16)]
+        + [pltpu.SemaphoreType.DMA((8,))],
         10**11,
         4000000,
         hbm=7,
-        out_places=[pltpu.VMEM] * 12 + [pltpu.HBM] * 2,
+        out_places=[pltpu.VMEM] * 12 + [pltpu.HBM],
     )(
         gain, self_weight, neighbour_weight, output_weight, readout, error, background.reshape(size, channels),
         held, near4, oth,
@@ -617,8 +616,9 @@
         tables + [scratch(2 * size, BF16, LANES), scratch(size, BF16, LANES), pltpu.SemaphoreType.DMA((2,))],
         10**9,
         3000000,
-        hbm=2,
-    )(wn_turned, ws_turned, spread, readout_held, *reports_held, arrived, field)
+        hbm=1,
+        fixed=False,
+    )(both_turned, spread, readout_held, *reports_held, arrived, field)
     base = kernel_call(
         backward_kernel,
         spec(size),

time: 24.5 us -> 23.8 us (0.971)
  Pallas kernels: 10.2 us -> 9.47 us
    pallas_call x9, Pallas kernels: 10.2 us -> 9.47 us  [call(): pl.pallas_call(body, out_shape=outs, in_specs=[pl.BlockSpec(memory_space=...]
    ppermute x2, waiting for transfers between devices: 1.36 us -> 0.7 us  [across(): return lax.ppermute(block, ('slot', 'tile'), pairs)]
    all_to_all x1, waiting for transfers between devices: 0.01 us -> 0.66 us  [per_device(): lax.all_to_all(packed, 'tile', split_axis=0, concat_axis=0, tiled=True)]
  transfers between devices with their start and end apart: 6 -> 6, of which waited for: 1 -> 2; matrix products, arithmetic and copies ran while one was open for 0% -> 0% of each run, Pallas kernels for 39% -> 37%
where the time goes in v9:
time: 23.8 us; the launch traced here: 23.5 us
  starting transfers between devices  11 us (46%)
  Pallas kernels  9.47 us (40%)
  local copies, waits for them, and re-layouts  1.57 us (7%)
  waiting for transfers between devices  1.37 us (6%)
    pallas_call x9, Pallas kernels, call(): pl.pallas_call(body, out_shape=outs, in_specs=[pl.BlockSpec(memory_space=...  9.47 us
    ppermute x1, starting transfers between devices, per_device(): oth = lax.ppermute(sent, 'tile', other_of)  4.88 us
    all_to_all x1, starting transfers between devices, per_device(): lax.all_to_all(packed, 'tile', split_axis=0, concat_axis=0, tiled=True)  3.52 us
    ppermute x2, starting transfers between devices, across(): return lax.ppermute(block, ('slot', 'tile'), pairs)  2.07 us
    unnamed x4, local copies, waits for them, and re-layouts  1.57 us
    ppermute x2, waiting for transfers between devices, across(): return lax.ppermute(block, ('slot', 'tile'), pairs)  0.7 us
    all_to_all x1, waiting for transfers between devices, per_device(): lax.all_to_all(packed, 'tile', split_axis=0, concat_axis=0, tiled=True)  0.66 us
  transfers between devices with their start and end apart: 6, of which 2 were waited for; matrix products, arithmetic and copies ran while one was open for 0% of the time, Pallas kernels for 37%

profile of v9, /device:TPU:0, one launch (start us, length us, event | category | flops | bytes accessed | tf_op | source)
XLA Modules:
  0.0 23.5 jit_solution(10768916804405680449)
XLA Ops:
  0.0 0.5 %collective-permute-start = (f32[128,512]{1,0:T(8,128)}, f32[128,512]{1,0:T(8,128)S(1)}, u32[]{:S(2)}, u32[]{:S(2)}) collective-permute-start(f32[128,512]{1,0:T(8,128)} %bitcast.20), channel_id=1, source_target_pairs={{0,1},{1,0},{2,3},{3,2},{4,5},{5,4},{6,7},{7,6},{8,9},{9,8},{10,11... | collective-permute-start | bytes 786440 | tf_op jit(solution)/shard_map/ppermute | solution.py:530
  0.5 2.2 %shard_map.127 = (f32[128,512]{1,0:T(8,128)S(1)}, bf16[384,128]{1,0:T(8,128)(2,1)}, s32[2,1,32]{2,1,0:T(1,128)S(1)}, s32[2,4,32]{2,1,0:T(4,128)S(1)}, bf16[2,4,3...) custom-call(f32[128,512]{1,0:T(8,128)} %bitcast.21, s32[2,1,32]{2,1,0:T(1,128)} %bitcast.25, ...), custom_call_target="tpu_custom_call" | custom-call | flops 10000000 | bytes 200000 | tf_op jit(solution)/shard_map/pallas_call | solution.py:475
  2.7 0.0 collective-permute-done.mate
  2.7 4.9 %collective-permute-start.1 = (bf16[144,512]{1,0:T(8,128)(2,1)S(1)}, bf16[144,512]{1,0:T(8,128)(2,1)S(1)}, u32[]{:S(2)}, u32[]{:S(2)}) collective-permute-start(bf16[144,512]{1,0:T(8,128)(2,1)S(1)} %shard_map.128.refs_5_), channel_id=1, source_target_pairs={{0,15},{1,2},{2,1},{3,4},{4,3},{5,6},{6,5},{7,8},{8,7},{9,10},{10,... | collective-permute-start | bytes 442376 | tf_op jit(solution)/shard_map/ppermute | solution.py:557
  7.6 3.5 %all-to-all-start = ((bf16[16,24,128]{2,1,0:T(8,128)(2,1)}), bf16[16,24,128]{2,1,0:T(8,128)(2,1)S(1)}, u32[]{:S(2)}, u32[]{:S(2)}) async-start(bf16[16,24,128]{2,1,0:T(8,128)(2,1)} %bitcast.12), calls=%async_computation | async-start | bytes 196608 | tf_op jit(solution)/shard_map/all_to_all | solution.py:568
  11.1 0.0 collective-permute-done.1.oth
  11.2 0.1 shard_map.129
  11.3 1.6 %collective-permute-start.2 = (bf16[160,512]{1,0:T(8,128)(2,1)S(1)}, bf16[160,512]{1,0:T(8,128)(2,1)S(1)}, u32[]{:S(2)}, u32[]{:S(2)}) collective-permute-start(bf16[160,512]{1,0:T(8,128)(2,1)S(1)} %get-tuple-element.57), channel_id=1, source_target_pairs={{16,0},{17,1},{18,2},{19,3},{20,4},{21,5},{22,6},{23,7},{24,8},{25... | collective-permute-start | bytes 491528 | tf_op jit(solution)/shard_map/ppermute | solution.py:528
  12.8 3.5 %shard_map.130 = (f32[64,512]{1,0:T(8,128)S(1)}, f32[192,512]{1,0:T(8,128)S(1)}, bf16[192,512]{1,0:T(8,128)(2,1)S(1)}, bf16[192,512]{1,0:T(8,128)(2,1)S(1)}, bf1...) custom-call(f32[1,512]{1,0:T(1,128)} %bitcast.28, ...), custom_call_target="tpu_custom_call" | custom-call | flops 99999997952 | bytes 4000000 | tf_op jit(solution)/shard_map/pallas_call | solution.py:475
  16.4 0.0 copy-start
  16.4 1.0 %copy-done = bf16[1024,512]{1,0:T(8,128)(2,1)} copy-done((bf16[1024,512]{1,0:T(8,128)(2,1)}, bf16[1024,512]{1,0:T(8,128)(2,1)S(1)}, u32[]{:S(2)}) %copy-start) | copy-done | bytes 1048600
  17.3 0.5 %collective-permute-start.4 = (bf16[128,512]{1,0:T(8,128)(2,1)S(1)}, bf16[128,512]{1,0:T(8,128)(2,1)S(1)}, u32[]{:S(2)}, u32[]{:S(2)}) collective-permute-start(bf16[128,512]{1,0:T(8,128)(2,1)S(1)} %get-tuple-element.66), channel_id=1, source_target_pairs={{16,0},{17,1},{18,2},{19,3},{20,4},{21,5},{22,6},{23,7},{24,8},{25... | collective-permute-start | bytes 393224 | tf_op jit(solution)/shard_map/ppermute | solution.py:528
  17.9 0.7 %all-to-all-done = bf16[16,24,128]{2,1,0:T(8,128)(2,1)S(1)} async-done(((bf16[16,24,128]{2,1,0:T(8,128)(2,1)}), bf16[16,24,128]{2,1,0:T(8,128)(2,1)S(1)}, u32[]{:S(2)}, u32[]{:S(2)}) %all-to-all-start) | async-done | bytes 98336 | tf_op jit(solution)/shard_map/all_to_all | solution.py:568
  18.5 0.0 copy-start.1
  18.5 0.5 %shard_map.132 = (bf16[256,128]{1,0:T(8,128)(2,1)S(1)}, bf16[128,128]{1,0:T(8,128)(2,1)S(1)}, bf16[32,384]{1,0:T(8,128)(2,1)S(1)}, bf16[32,384]{1,0:T(8,128)(2,1)S(1)}, f32[32,384]{1,0:T(8,128)S(1)}) custom-call(bf16[384,128]{1,0:T(8,128)(2,1)S(1)} %bitcast.18, f32[128,512]{1,0:T(8,128)S(1)} %get-tuple-element.45.field), custom_call_target="tpu_custom_call" | custom-call | flops 1000000000 | bytes 2000000 | tf_op jit(solution)/shard_map/pallas_call | solution.py:475
  19.1 0.1 collective-permute-start.3
  19.1 0.6 %copy-done.1 = bf16[1024,512]{1,0:T(8,128)(2,1)S(1)} copy-done((bf16[1024,512]{1,0:T(8,128)(2,1)S(1)}, bf16[1024,512]{1,0:T(8,128)(2,1)}, u32[]{:S(2)}) %copy-start.1) | copy-done | bytes 1048600
  19.7 0.8 %shard_map.133 = (f32[256,512]{1,0:T(8,128)S(1)}, f32[128,512]{1,0:T(8,128)S(1)}, bf16[512,512]{1,0:T(8,128)(2,1)S(1)}, bf16[512,512]{1,0:T(8,128)(2,1)S(1)}) custom-call(bf16[1024,512]{1,0:T(8,128)(2,1)S(1)} %copy-done.1, bf16[256,128]{1,0:T(8,128)(2,1)S(1)} %get-tuple-element.46.spread_own, bf16[512,128]{1,0:T(8,128)(2,1)S(1)} %get-tuple-element.47.readout, ...), custom_call_target="tpu_custom_call" | custom-call | flops 1000000000 | bytes 3000000 | tf_op jit(solution)/shard_map/pallas_call | solution.py:475
  20.5 0.0 collective-permute-done.3.message
  20.5 0.0 collective-permute-done.2.message16
  20.6 1.5 %shard_map.134.base = f32[128,512]{1,0:T(8,128)S(1)} custom-call(f32[256,512]{1,0:T(8,128)S(1)} %get-tuple-element.51.pulled, f32[128,512]{1,0:T(8,128)S(1)} %get-tuple-element.52.away, bf16[512,512]{1,0:T(8,128)(2,1)S(1)} %get-tuple-element.53.wn, bf16[512,512]{1,0:T(8,128)(2,1)S(1)} %get-tuple-element.54.ws, f32[1,512]{1,0:T(1,128)S(1)} %get-tuple-element.55.gain, ...), custom_call_target="tpu_custom_call" | custom-call | flops 603979776 | bytes 6000000 | tf_op jit(solution)/shard_map/pallas_call | solution.py:475
  22.1 0.7 %collective-permute-done.4.before = bf16[128,512]{1,0:T(8,128)(2,1)S(1)} collective-permute-done((bf16[128,512]{1,0:T(8,128)(2,1)S(1)}, bf16[128,512]{1,0:T(8,128)(2,1)S(1)}, u32[]{:S(2)}, u32[]{:S(2)}) %collective-permute-start.4) | collective-permute-done | bytes 131104 | tf_op jit(solution)/shard_map/ppermute | solution.py:528
  22.8 0.8 %shard_map.135 = f32[128,512]{1,0:T(8,128)} custom-call(f32[128,512]{1,0:T(8,128)S(1)} %shard_map.134.base, bf16[128,512]{1,0:T(8,128)(2,1)S(1)} %get-tuple-element.65.background, bf16[128,512]{1,0:T(8,128)(2,1)S(1)} %collective-permute-done.4.before, f32[1,512]{1,0:T(1,128)S(1)} %get-tuple-element.60.error), custom_call_target="tpu_custom_call" | custom-call | flops 1000000 | bytes 900000 | tf_op jit(solution)/shard_map/pallas_call | solution.py:475
  (2 shorter events, 0.1 us)
Async XLA Ops:
  0.0 2.7 %collective-permute-start = (f32[128,512]{1,0:T(8,128)}, f32[128,512]{1,0:T(8,128)S(1)}, u32[]{:S(2)}, u32[]{:S(2)}) collective-permute-start(f32[128,512]{1,0:T(8,128)} %bitcast.20), channel_id=1, source_target_pairs={{0,1},{1,0},{2,3},{3,2},{4,5},{5,4},{6,7},{7,6},{8,9},{9,8},{10,11... | collective-permute-start | bytes 786440 | tf_op jit(solution)/shard_map/ppermute | solution.py:530
  2.7 8.4 %collective-permute-start.1 = (bf16[144,512]{1,0:T(8,128)(2,1)S(1)}, bf16[144,512]{1,0:T(8,128)(2,1)S(1)}, u32[]{:S(2)}, u32[]{:S(2)}) collective-permute-start(bf16[144,512]{1,0:T(8,128)(2,1)S(1)} %shard_map.128.refs_5_), channel_id=1, source_target_pairs={{0,15},{1,2},{2,1},{3,4},{4,3},{5,6},{6,5},{7,8},{8,7},{9,10},{10,... | collective-permute-start | bytes 442376 | tf_op jit(solution)/shard_map/ppermute | solution.py:557
  7.6 10.9 %all-to-all-start = ((bf16[16,24,128]{2,1,0:T(8,128)(2,1)}), bf16[16,24,128]{2,1,0:T(8,128)(2,1)S(1)}, u32[]{:S(2)}, u32[]{:S(2)}) async-start(bf16[16,24,128]{2,1,0:T(8,128)(2,1)} %bitcast.12), calls=%async_computation | async-start | bytes 196608 | tf_op jit(solution)/shard_map/all_to_all | solution.py:568
  11.3 9.3 %collective-permute-start.2 = (bf16[160,512]{1,0:T(8,128)(2,1)S(1)}, bf16[160,512]{1,0:T(8,128)(2,1)S(1)}, u32[]{:S(2)}, u32[]{:S(2)}) collective-permute-start(bf16[160,512]{1,0:T(8,128)(2,1)S(1)} %get-tuple-element.57), channel_id=1, source_target_pairs={{16,0},{17,1},{18,2},{19,3},{20,4},{21,5},{22,6},{23,7},{24,8},{25... | collective-permute-start | bytes 491528 | tf_op jit(solution)/shard_map/ppermute | solution.py:528
  16.4 1.0 %copy-start = (bf16[1024,512]{1,0:T(8,128)(2,1)}, bf16[1024,512]{1,0:T(8,128)(2,1)S(1)}, u32[]{:S(2)}) copy-start(bf16[1024,512]{1,0:T(8,128)(2,1)S(1)} %get-tuple-element.38.both_hbm) | copy-start | bytes 3145732
  17.3 5.4 %collective-permute-start.4 = (bf16[128,512]{1,0:T(8,128)(2,1)S(1)}, bf16[128,512]{1,0:T(8,128)(2,1)S(1)}, u32[]{:S(2)}, u32[]{:S(2)}) collective-permute-start(bf16[128,512]{1,0:T(8,128)(2,1)S(1)} %get-tuple-element.66), channel_id=1, source_target_pairs={{16,0},{17,1},{18,2},{19,3},{20,4},{21,5},{22,6},{23,7},{24,8},{25... | collective-permute-start | bytes 393224 | tf_op jit(solution)/shard_map/ppermute | solution.py:528
  18.5 1.2 %copy-start.1 = (bf16[1024,512]{1,0:T(8,128)(2,1)S(1)}, bf16[1024,512]{1,0:T(8,128)(2,1)}, u32[]{:S(2)}) copy-start(bf16[1024,512]{1,0:T(8,128)(2,1)} %copy-done) | copy-start | bytes 3145732
  19.1 1.5 %collective-permute-start.3 = (bf16[128,128]{1,0:T(8,128)(2,1)S(1)}, bf16[128,128]{1,0:T(8,128)(2,1)S(1)}, u32[]{:S(2)}, u32[]{:S(2)}) collective-permute-start(bf16[128,128]{1,0:T(8,128)(2,1)S(1)} %get-tuple-element.61), channel_id=1, source_target_pairs={{0,1},{1,0},{2,3},{3,2},{4,5},{5,4},{6,7},{7,6},{8,9},{9,8},{10,11... | collective-permute-start | bytes 98312 | tf_op jit(solution)/shard_map/ppermute | solution.py:612

commit v10 on v7

--- a/solution.py
+++ b/solution.py
@@ -211,8 +211,8 @@
 
 def forward_kernel(
     gain_hbm, ws_hbm, wn_hbm, wo_hbm, readout_hbm, error_hbm, background_hbm, control, mate, oth,
-    edge0, u1x, d0x, d1x, f2x, field, final, wo, readout, gain, error, background,
-    ua, ub, n, act, pre, edge, states, weights, sems,
+    edge0, u1x, d0x, d1x, f2x, field, final, wo_turned, readout, gain, error, background,
+    ua, ub, n, act, pre, edge, states, weights, wo, sems,
 ):
     channels = wo.shape[0]
     halves = weights.at[pl.ds(0, channels)], weights.at[pl.ds(channels, channels)]
@@ -259,6 +259,7 @@
             states[away + r * 16 : away + (r + 1) * 16] = taken.astype(BF16)
 
     forward_step(ua, n, act, pre, d0x, g, weights, wo, WIDE, members, keep(ub), copies[1:])
+    wo_turned[...] = jnp.transpose(wo[...])
     for m in range(members):
         slim_copy(u1x, ub, m)
     keep_states(ub, 0)
@@ -279,38 +280,51 @@
     return high, (x - high.astype(F32)).astype(BF16)
 
 
-def spread_of(first, th, tl, scaled, taken, field, ph, plo, spread):
+def near_rows(x):
+    even = lax.rem(lax.axis_index("tile"), 2) == 0
+    return jnp.where(
+        even, jnp.concatenate([x[8:16], x[24:32]], axis=0), jnp.concatenate([x[0:8], x[16:24]], axis=0)
+    )
+
+
+def spread_of(first, near, th, tl, scaled, taken, field, pp, out):
+    count = 16 if near else 32
+    half = 2 * count
     lane = lax.broadcasted_iota(jnp.int32, (1, LANES), 1)
     members = field.shape[1] // LANES
     for p in range(th.shape[1] // LANES):
         at = slice(p * LANES, (p + 1) * LANES)
         slot = (lane + p * LANES) % CHUNK
         table_of = jnp.where(slot < SLOTS, slot // CAP, -1)
+        rows = scaled[:, at]
+        rows = near_rows(rows) if near else rows
         for q in range(2):
-            kept = jnp.where(table_of == first + q, scaled[:, at], 0.0)
-            ph[q * 32 : (q + 1) * 32, at], plo[q * 32 : (q + 1) * 32, at] = split(kept)
-    cross = dot_t(ph[...], th[...]) + dot_t(plo[...], th[...]) + dot_t(ph[...], tl[...])
+            a, b = q * count, (q + 1) * count
+            pp[a:b, at], pp[half + a : half + b, at] = split(jnp.where(table_of == first + q, rows, 0.0))
+    both = pp[0 : 2 * half]
+    cross = dot_t(both, th[...])
+    cross = cross[:half] + cross[half:] + dot_t(pp[0:half], tl[...])
     block = jnp.concatenate([cross] * 2, axis=1)
-    on_block = sublane(block.shape) // 32 == lax.broadcasted_iota(jnp.int32, block.shape, 1) // 32
-    target = dot(ph[...], taken[...]) + dot(plo[...], taken[...])
+    on_block = sublane(block.shape) // count == lax.broadcasted_iota(jnp.int32, block.shape, 1) // 32
+    target = dot(both, taken[...])
+    target = target[:half] + target[half:]
     ch, cl = split(jnp.where(on_block, block, 0.0))
     fh, fl = split(field[first * 32 : (first + 2) * 32])
-    mixed = dot(ch, fh) + dot(cl, fh) + dot(ch, fl)
+    mixed = dot(jnp.concatenate([ch, cl], axis=0), fh)
+    mixed = mixed[:half] + mixed[half:] + dot(ch, fl)
     for q in range(2):
         for m in range(members):
-            start = (q * members + m) * 32
-            value = mixed[q * 32 : (q + 1) * 32, m * LANES : (m + 1) * LANES] - target[q * 32 : (q + 1) * 32]
-            spread[start : start + 32] = value.astype(BF16)
+            start = (q * members + m) * count
+            a, b = q * count, (q + 1) * count
+            value = mixed[a:b, m * LANES : (m + 1) * LANES] - target[a:b]
+            out[start : start + count] = value.astype(BF16)
 
 
 def observe_kernel(
     tiles, arrived, field,
-    spread, message, th, tl, scaled,
-    ph, plo, wide,
+    message, th, tl, scaled,
+    pp, wide,
 ):
-    steps = 2
-    members = field.shape[1] // LANES
-    even = lax.rem(lax.axis_index("tile"), 2) == 0
     cells = sublane((32, LANES)).astype(F32)
     lane = lax.broadcasted_iota(jnp.int32, (8, LANES), 1)
     wide[...] = arrived[...].astype(F32)
@@ -337,21 +351,13 @@
         at = slice(p * LANES, (p + 1) * LANES)
         th[:, at], tl[:, at] = split(weight)
         scaled[:, at] = weight * entry[8]
-    spread_of(0, th, tl, scaled, arrived, field, ph, plo, spread)
-    size = members * 32
-    for k in range(steps):
-        for m in range(members):
-            start = k * size + m * 32
-            pair = spread[start : start + 32].astype(F32)
-            near = [jnp.where(even, pair[i + 8 : i + 16], pair[i : i + 8]) for i in (0, 16)]
-            start = k * size // 2 + m * 16
-            message[start : start + 16] = jnp.concatenate(near, axis=0).astype(BF16)
+    spread_of(0, True, th, tl, scaled, arrived, field, pp, message)
 
 
 def adjoint_step(u, cot, gb, gm, flat, d, out, gain, ws, wn, wo, members):
     both = 2 * SLIM
     gb[...] = cot[...].astype(BF16)
-    flat[...] = dot_t(gb[...], wo[...])
+    flat[...] = dot(gb[...], wo[...])
     gb[...] = (flat[...] * d[...]).astype(BF16)
     gm[...] = dot_t(gb[...], wn[...])
     flat[...] = dot_t(gb[...], ws[...])
@@ -386,21 +392,17 @@
 
 
 def pull_kernel(
-    wn_hbm, ws_hbm, spread_own, readout, th, tl, scaled, arrived, field,
+    wn_hbm, ws_hbm, readout, th, tl, scaled, arrived, field,
     pulled, away, wn, ws,
-    ph, plo, spread, near, sems,
+    pp, spread, near, sems,
 ):
     pairs = ((wn_hbm, wn), (ws_hbm, ws))
     copies = [pltpu.make_async_copy(source, to, sems.at[i]) for i, (source, to) in enumerate(pairs)]
     for copy in copies:
         copy.start()
-    even = lax.rem(lax.axis_index("tile"), 2) == 0
-    pulled[...] = dot_t(spread_own[...], readout[...])
-    spread_of(2, th, tl, scaled, arrived, field, ph, plo, spread)
-    for start in range(0, spread.shape[0], 32):
-        pair = spread[start : start + 32].astype(F32)
-        rows = [jnp.where(even, pair[i + 8 : i + 16], pair[i : i + 8]) for i in (0, 16)]
-        near[start // 2 : start // 2 + 16] = jnp.concatenate(rows, axis=0).astype(BF16)
+    spread_of(0, False, th, tl, scaled, arrived, field, pp, spread)
+    pulled[...] = dot_t(spread[...], readout[...])
+    spread_of(2, True, th, tl, scaled, arrived, field, pp, near)
     away[...] = dot_t(near[...], readout[...])
     for copy in copies:
         copy.wait()
@@ -576,7 +578,7 @@
         + [spec(channels, BF16), spec(channels, BF16, LANES), spec(1), spec(1), spec(size, BF16)],
         [scratch(wide), scratch(wide), scratch(wide, BF16, 2 * channels), scratch(wide, BF16)]
         + [scratch(wide), scratch(16), scratch(4 * size, BF16)]
-        + [scratch(2 * channels, BF16), pltpu.SemaphoreType.DMA((7,))],
+        + [scratch(2 * channels, BF16), scratch(channels, BF16), pltpu.SemaphoreType.DMA((7,))],
         10**11,
         4000000,
         hbm=7,
@@ -586,12 +588,10 @@
     )
     before = across(final, -1)
     total = tiles * CHUNK
-    tables = [scratch(64, BF16, total), scratch(64, BF16, total)]
-    spread, near_spread, *reports_held = kernel_call(
+    near_spread, *reports_held = kernel_call(
         functools.partial(observe_kernel, tiles),
-        [spec(2 * size, BF16, LANES), spec(size, BF16, LANES)]
-        + [spec(32, BF16, total), spec(32, BF16, total), spec(32, F32, total)],
-        tables + [scratch(total, F32, LANES)],
+        [spec(size, BF16, LANES), spec(32, BF16, total), spec(32, BF16, total), spec(32, F32, total)],
+        [scratch(64, BF16, total), scratch(total, F32, LANES)],
         10**9,
         2000000,
     )(arrived, field)
@@ -599,11 +599,12 @@
     handed = kernel_call(
         pull_kernel,
         [spec(2 * size), spec(size), spec(channels, BF16), spec(channels, BF16)],
-        tables + [scratch(2 * size, BF16, LANES), scratch(size, BF16, LANES), pltpu.SemaphoreType.DMA((2,))],
+        [scratch(128, BF16, total), scratch(2 * size, BF16, LANES), scratch(size, BF16, LANES)]
+        + [pltpu.SemaphoreType.DMA((2,))],
         10**9,
         3000000,
         hbm=2,
-    )(neighbour_weight, self_weight, spread, readout_held, *reports_held, arrived, field)
+    )(neighbour_weight, self_weight, readout_held, *reports_held, arrived, field)
     base = kernel_call(
         backward_kernel,
         spec(size),

time: 23.1 us -> 23.5 us (1.017)
  Pallas kernels: 9.91 us -> 10.3 us
    pallas_call x9, Pallas kernels: 9.91 us -> 10.3 us  [call(): pl.pallas_call(body, out_shape=outs, in_specs=[pl.BlockSpec(memory_space=...]
  transfers between devices with their start and end apart: 6 -> 6, of which waited for: 1 -> 1; matrix products, arithmetic and copies ran while one was open for 0% -> 0% of each run, Pallas kernels for 40% -> 41%
where the time goes in v10:
time: 23.5 us; the launch traced here: 23.2 us
  starting transfers between devices  11.1 us (47%)
  Pallas kernels  10.3 us (44%)
  waiting for transfers between devices  1.75 us (7%)
    pallas_call x9, Pallas kernels, call(): pl.pallas_call(body, out_shape=outs, in_specs=[pl.BlockSpec(memory_space=...  10.3 us
    ppermute x1, starting transfers between devices, per_device(): oth = lax.ppermute(sent, 'tile', other_of)  4.88 us
    all_to_all x1, starting transfers between devices, per_device(): lax.all_to_all(packed, 'tile', split_axis=0, concat_axis=0, tiled=True)  3.52 us
    ppermute x2, starting transfers between devices, across(): return lax.ppermute(block, ('slot', 'tile'), pairs)  2.16 us
    all_to_all x1, waiting for transfers between devices, per_device(): lax.all_to_all(packed, 'tile', split_axis=0, concat_axis=0, tiled=True)  1.74 us
  transfers between devices with their start and end apart: 6, of which 1 were waited for; matrix products, arithmetic and copies ran while one was open for 0% of the time, Pallas kernels for 41%

profile of v10, /device:TPU:0, one launch (start us, length us, event | category | flops | bytes accessed | tf_op | source)
XLA Modules:
  0.0 23.2 jit_solution(14487937613816591145)
XLA Ops:
  0.0 0.5 %collective-permute-start = (f32[128,512]{1,0:T(8,128)}, f32[128,512]{1,0:T(8,128)S(1)}, u32[]{:S(2)}, u32[]{:S(2)}) collective-permute-start(f32[128,512]{1,0:T(8,128)} %bitcast.20), channel_id=1, source_target_pairs={{0,1},{1,0},{2,3},{3,2},{4,5},{5,4},{6,7},{7,6},{8,9},{9,8},{10,11... | collective-permute-start | bytes 786440 | tf_op jit(solution)/shard_map/ppermute | solution.py:522
  0.5 2.2 %shard_map.127 = (f32[128,512]{1,0:T(8,128)S(1)}, bf16[384,128]{1,0:T(8,128)(2,1)}, s32[2,1,32]{2,1,0:T(1,128)S(1)}, s32[2,4,32]{2,1,0:T(4,128)S(1)}, bf16[2,4,3...) custom-call(f32[128,512]{1,0:T(8,128)} %bitcast.21, s32[2,1,32]{2,1,0:T(1,128)} %bitcast.25, ...), custom_call_target="tpu_custom_call" | custom-call | flops 10000000 | bytes 200000 | tf_op jit(solution)/shard_map/pallas_call | solution.py:467
  2.7 0.0 collective-permute-done.mate
  2.7 4.9 %collective-permute-start.1 = (bf16[144,512]{1,0:T(8,128)(2,1)S(1)}, bf16[144,512]{1,0:T(8,128)(2,1)S(1)}, u32[]{:S(2)}, u32[]{:S(2)}) collective-permute-start(bf16[144,512]{1,0:T(8,128)(2,1)S(1)} %shard_map.128.refs_5_), channel_id=1, source_target_pairs={{0,15},{1,2},{2,1},{3,4},{4,3},{5,6},{6,5},{7,8},{8,7},{9,10},{10,... | collective-permute-start | bytes 442376 | tf_op jit(solution)/shard_map/ppermute | solution.py:549
  7.6 3.5 %all-to-all-start = ((bf16[16,24,128]{2,1,0:T(8,128)(2,1)}), bf16[16,24,128]{2,1,0:T(8,128)(2,1)S(1)}, u32[]{:S(2)}, u32[]{:S(2)}) async-start(bf16[16,24,128]{2,1,0:T(8,128)(2,1)} %bitcast.12), calls=%async_computation | async-start | bytes 196608 | tf_op jit(solution)/shard_map/all_to_all | solution.py:560
  11.1 0.0 collective-permute-done.1.oth
  11.2 0.1 shard_map.129
  11.3 1.6 %collective-permute-start.2 = (bf16[160,512]{1,0:T(8,128)(2,1)S(1)}, bf16[160,512]{1,0:T(8,128)(2,1)S(1)}, u32[]{:S(2)}, u32[]{:S(2)}) collective-permute-start(bf16[160,512]{1,0:T(8,128)(2,1)S(1)} %get-tuple-element.53), channel_id=1, source_target_pairs={{16,0},{17,1},{18,2},{19,3},{20,4},{21,5},{22,6},{23,7},{24,8},{25... | collective-permute-start | bytes 491528 | tf_op jit(solution)/shard_map/ppermute | solution.py:520
  12.8 3.4 %shard_map.130 = (f32[64,512]{1,0:T(8,128)S(1)}, f32[192,512]{1,0:T(8,128)S(1)}, bf16[192,512]{1,0:T(8,128)(2,1)S(1)}, bf16[192,512]{1,0:T(8,128)(2,1)S(1)}, bf1...) custom-call(f32[1,512]{1,0:T(1,128)} %bitcast.28, ...), custom_call_target="tpu_custom_call" | custom-call | flops 99999997952 | bytes 4000000 | tf_op jit(solution)/shard_map/pallas_call | solution.py:467
  16.2 0.6 %collective-permute-start.4 = (bf16[128,512]{1,0:T(8,128)(2,1)S(1)}, bf16[128,512]{1,0:T(8,128)(2,1)S(1)}, u32[]{:S(2)}, u32[]{:S(2)}) collective-permute-start(bf16[128,512]{1,0:T(8,128)(2,1)S(1)} %get-tuple-element.62), channel_id=1, source_target_pairs={{16,0},{17,1},{18,2},{19,3},{20,4},{21,5},{22,6},{23,7},{24,8},{25... | collective-permute-start | bytes 393224 | tf_op jit(solution)/shard_map/ppermute | solution.py:520
  16.8 1.7 %all-to-all-done = bf16[16,24,128]{2,1,0:T(8,128)(2,1)S(1)} async-done(((bf16[16,24,128]{2,1,0:T(8,128)(2,1)}), bf16[16,24,128]{2,1,0:T(8,128)(2,1)S(1)}, u32[]{:S(2)}, u32[]{:S(2)}) %all-to-all-start) | async-done | bytes 98336 | tf_op jit(solution)/shard_map/all_to_all | solution.py:560
  18.5 0.5 %shard_map.132 = (bf16[128,128]{1,0:T(8,128)(2,1)S(1)}, bf16[32,384]{1,0:T(8,128)(2,1)S(1)}, bf16[32,384]{1,0:T(8,128)(2,1)S(1)}, f32[32,384]{1,0:T(8,128)S(1)}) custom-call(bf16[384,128]{1,0:T(8,128)(2,1)S(1)} %bitcast.18, f32[128,512]{1,0:T(8,128)S(1)} %get-tuple-element.43.field), custom_call_target="tpu_custom_call" | custom-call | flops 1000000000 | bytes 2000000 | tf_op jit(solution)/shard_map/pallas_call | solution.py:467
  19.0 0.1 collective-permute-start.3
  19.0 1.7 %shard_map.133 = (f32[256,512]{1,0:T(8,128)S(1)}, f32[128,512]{1,0:T(8,128)S(1)}, bf16[512,512]{1,0:T(8,128)(2,1)S(1)}, bf16[512,512]{1,0:T(8,128)(2,1)S(1)}) custom-call(bf16[512,512]{1,0:T(8,128)(2,1)} %wn_hbm.3, bf16[512,512]{1,0:T(8,128)(2,1)} %ws_hbm.3, bf16[512,128]{1,0:T(8,128)(2,1)S(1)} %get-tuple-element.36.readout, ...), custom_call_target="tpu_custom_call" | custom-call | flops 1000000000 | bytes 3000000 | tf_op jit(solution)/shard_map/pallas_call | solution.py:467
  20.7 0.0 collective-permute-done.3.message
  20.8 0.0 collective-permute-done.2.message16
  20.8 1.6 %shard_map.134.base = f32[128,512]{1,0:T(8,128)S(1)} custom-call(f32[256,512]{1,0:T(8,128)S(1)} %get-tuple-element.47.pulled, f32[128,512]{1,0:T(8,128)S(1)} %get-tuple-element.48.away, bf16[512,512]{1,0:T(8,128)(2,1)S(1)} %get-tuple-element.49.wn, bf16[512,512]{1,0:T(8,128)(2,1)S(1)} %get-tuple-element.50.ws, f32[1,512]{1,0:T(1,128)S(1)} %get-tuple-element.51.gain, ...), custom_call_target="tpu_custom_call" | custom-call | flops 603979776 | bytes 6000000 | tf_op jit(solution)/shard_map/pallas_call | solution.py:467
  22.4 0.0 collective-permute-done.4.before
  22.4 0.8 %shard_map.135 = f32[128,512]{1,0:T(8,128)} custom-call(f32[128,512]{1,0:T(8,128)S(1)} %shard_map.134.base, bf16[128,512]{1,0:T(8,128)(2,1)S(1)} %get-tuple-element.61.background, bf16[128,512]{1,0:T(8,128)(2,1)S(1)} %collective-permute-done.4.before, f32[1,512]{1,0:T(1,128)S(1)} %get-tuple-element.56.error), custom_call_target="tpu_custom_call" | custom-call | flops 1000000 | bytes 900000 | tf_op jit(solution)/shard_map/pallas_call | solution.py:467
  (2 shorter events, 0.1 us)
Async XLA Ops:
  0.0 2.7 %collective-permute-start = (f32[128,512]{1,0:T(8,128)}, f32[128,512]{1,0:T(8,128)S(1)}, u32[]{:S(2)}, u32[]{:S(2)}) collective-permute-start(f32[128,512]{1,0:T(8,128)} %bitcast.20), channel_id=1, source_target_pairs={{0,1},{1,0},{2,3},{3,2},{4,5},{5,4},{6,7},{7,6},{8,9},{9,8},{10,11... | collective-permute-start | bytes 786440 | tf_op jit(solution)/shard_map/ppermute | solution.py:522
  2.7 8.4 %collective-permute-start.1 = (bf16[144,512]{1,0:T(8,128)(2,1)S(1)}, bf16[144,512]{1,0:T(8,128)(2,1)S(1)}, u32[]{:S(2)}, u32[]{:S(2)}) collective-permute-start(bf16[144,512]{1,0:T(8,128)(2,1)S(1)} %shard_map.128.refs_5_), channel_id=1, source_target_pairs={{0,15},{1,2},{2,1},{3,4},{4,3},{5,6},{6,5},{7,8},{8,7},{9,10},{10,... | collective-permute-start | bytes 442376 | tf_op jit(solution)/shard_map/ppermute | solution.py:549
  7.6 10.9 %all-to-all-start = ((bf16[16,24,128]{2,1,0:T(8,128)(2,1)}), bf16[16,24,128]{2,1,0:T(8,128)(2,1)S(1)}, u32[]{:S(2)}, u32[]{:S(2)}) async-start(bf16[16,24,128]{2,1,0:T(8,128)(2,1)} %bitcast.12), calls=%async_computation | async-start | bytes 196608 | tf_op jit(solution)/shard_map/all_to_all | solution.py:560
  11.3 9.5 %collective-permute-start.2 = (bf16[160,512]{1,0:T(8,128)(2,1)S(1)}, bf16[160,512]{1,0:T(8,128)(2,1)S(1)}, u32[]{:S(2)}, u32[]{:S(2)}) collective-permute-start(bf16[160,512]{1,0:T(8,128)(2,1)S(1)} %get-tuple-element.53), channel_id=1, source_target_pairs={{16,0},{17,1},{18,2},{19,3},{20,4},{21,5},{22,6},{23,7},{24,8},{25... | collective-permute-start | bytes 491528 | tf_op jit(solution)/shard_map/ppermute | solution.py:520
  16.2 6.2 %collective-permute-start.4 = (bf16[128,512]{1,0:T(8,128)(2,1)S(1)}, bf16[128,512]{1,0:T(8,128)(2,1)S(1)}, u32[]{:S(2)}, u32[]{:S(2)}) collective-permute-start(bf16[128,512]{1,0:T(8,128)(2,1)S(1)} %get-tuple-element.62), channel_id=1, source_target_pairs={{16,0},{17,1},{18,2},{19,3},{20,4},{21,5},{22,6},{23,7},{24,8},{25... | collective-permute-start | bytes 393224 | tf_op jit(solution)/shard_map/ppermute | solution.py:520
  19.0 1.8 %collective-permute-start.3 = (bf16[128,128]{1,0:T(8,128)(2,1)S(1)}, bf16[128,128]{1,0:T(8,128)(2,1)S(1)}, u32[]{:S(2)}, u32[]{:S(2)}) collective-permute-start(bf16[128,128]{1,0:T(8,128)(2,1)S(1)} %get-tuple-element.57), channel_id=1, source_target_pairs={{0,1},{1,0},{2,3},{3,2},{4,5},{5,4},{6,7},{7,6},{8,9},{9,8},{10,11... | collective-permute-start | bytes 98312 | tf_op jit(solution)/shard_map/ppermute | solution.py:598

commit v11 on v7

--- a/solution.py
+++ b/solution.py
@@ -271,7 +271,10 @@
     for q in range(4):
         for m in range(members):
             start = (q * members + m) * 32
-            field[q * 32 : (q + 1) * 32, m * LANES : (m + 1) * LANES] = read[start : start + 32]
+            at = slice(m * LANES, (m + 1) * LANES)
+            field[q * 32 : (q + 1) * 32, at], field[LANES + q * 32 : LANES + (q + 1) * 32, at] = split(
+                read[start : start + 32]
+            )
 
 
 def split(x):
@@ -279,7 +282,7 @@
     return high, (x - high.astype(F32)).astype(BF16)
 
 
-def spread_of(first, th, tl, scaled, taken, field, ph, plo, spread):
+def spread_of(first, th, tl, scaled, taken, field, pp, spread):
     lane = lax.broadcasted_iota(jnp.int32, (1, LANES), 1)
     members = field.shape[1] // LANES
     for p in range(th.shape[1] // LANES):
@@ -288,14 +291,18 @@
         table_of = jnp.where(slot < SLOTS, slot // CAP, -1)
         for q in range(2):
             kept = jnp.where(table_of == first + q, scaled[:, at], 0.0)
-            ph[q * 32 : (q + 1) * 32, at], plo[q * 32 : (q + 1) * 32, at] = split(kept)
-    cross = dot_t(ph[...], th[...]) + dot_t(plo[...], th[...]) + dot_t(ph[...], tl[...])
+            pp[q * 32 : (q + 1) * 32, at], pp[64 + q * 32 : 96 + q * 32, at] = split(kept)
+    cross = dot_t(pp[...], th[...])
+    cross = cross[:64] + cross[64:] + dot_t(pp[0:64], tl[...])
     block = jnp.concatenate([cross] * 2, axis=1)
     on_block = sublane(block.shape) // 32 == lax.broadcasted_iota(jnp.int32, block.shape, 1) // 32
-    target = dot(ph[...], taken[...]) + dot(plo[...], taken[...])
+    target = dot(pp[...], taken[...])
+    target = target[:64] + target[64:]
     ch, cl = split(jnp.where(on_block, block, 0.0))
-    fh, fl = split(field[first * 32 : (first + 2) * 32])
-    mixed = dot(ch, fh) + dot(cl, fh) + dot(ch, fl)
+    high = field[first * 32 : (first + 2) * 32]
+    low = field[LANES + first * 32 : LANES + (first + 2) * 32]
+    mixed = dot(jnp.concatenate([ch, cl], axis=0), high)
+    mixed = mixed[:64] + mixed[64:] + dot(ch, low)
     for q in range(2):
         for m in range(members):
             start = (q * members + m) * 32
@@ -306,19 +313,20 @@
 def observe_kernel(
     tiles, arrived, field,
     spread, message, th, tl, scaled,
-    ph, plo, wide,
+    pp,
 ):
     steps = 2
     members = field.shape[1] // LANES
     even = lax.rem(lax.axis_index("tile"), 2) == 0
     cells = sublane((32, LANES)).astype(F32)
     lane = lax.broadcasted_iota(jnp.int32, (8, LANES), 1)
-    wide[...] = arrived[...].astype(F32)
     packs = th.shape[1] // LANES
     sums = [[jnp.zeros((8, LANES), F32)] * 3 for _ in range(packs)]
     for d in range(tiles):
         p, start = divmod(d * CHUNK, LANES)
-        group = wide[d * CHUNK + 16 : (d + 1) * CHUNK]
+        window = (d * CHUNK + 16) // 16 * 16
+        group = arrived[window : window + 16].astype(F32)
+        group = group[8:] if d % 2 else group[:8]
         for b in range(3):
             first = start + b * APART
             place = lane - first % LANES
@@ -337,7 +345,7 @@
         at = slice(p * LANES, (p + 1) * LANES)
         th[:, at], tl[:, at] = split(weight)
         scaled[:, at] = weight * entry[8]
-    spread_of(0, th, tl, scaled, arrived, field, ph, plo, spread)
+    spread_of(0, th, tl, scaled, arrived, field, pp, spread)
     size = members * 32
     for k in range(steps):
         for m in range(members):
@@ -388,7 +396,7 @@
 def pull_kernel(
     wn_hbm, ws_hbm, spread_own, readout, th, tl, scaled, arrived, field,
     pulled, away, wn, ws,
-    ph, plo, spread, near, sems,
+    pp, spread, near, sems,
 ):
     pairs = ((wn_hbm, wn), (ws_hbm, ws))
     copies = [pltpu.make_async_copy(source, to, sems.at[i]) for i, (source, to) in enumerate(pairs)]
@@ -396,7 +404,7 @@
         copy.start()
     even = lax.rem(lax.axis_index("tile"), 2) == 0
     pulled[...] = dot_t(spread_own[...], readout[...])
-    spread_of(2, th, tl, scaled, arrived, field, ph, plo, spread)
+    spread_of(2, th, tl, scaled, arrived, field, pp, spread)
     for start in range(0, spread.shape[0], 32):
         pair = spread[start : start + 32].astype(F32)
         rows = [jnp.where(even, pair[i + 8 : i + 16], pair[i : i + 8]) for i in (0, 16)]
@@ -572,7 +580,7 @@
     ) = kernel_call(
         forward_kernel,
         [spec(groups * 8), spec(slim)] + [spec(slim, BF16)] * 3
-        + [spec(4 * lats * cols, F32, members * LANES), spec(size, BF16)]
+        + [spec(8 * lats * cols, BF16, members * LANES), spec(size, BF16)]
         + [spec(channels, BF16), spec(channels, BF16, LANES), spec(1), spec(1), spec(size, BF16)],
         [scratch(wide), scratch(wide), scratch(wide, BF16, 2 * channels), scratch(wide, BF16)]
         + [scratch(wide), scratch(16), scratch(4 * size, BF16)]
@@ -586,12 +594,12 @@
     )
     before = across(final, -1)
     total = tiles * CHUNK
-    tables = [scratch(64, BF16, total), scratch(64, BF16, total)]
+    tables = [scratch(128, BF16, total)]
     spread, near_spread, *reports_held = kernel_call(
         functools.partial(observe_kernel, tiles),
         [spec(2 * size, BF16, LANES), spec(size, BF16, LANES)]
         + [spec(32, BF16, total), spec(32, BF16, total), spec(32, F32, total)],
-        tables + [scratch(total, F32, LANES)],
+        tables,
         10**9,
         2000000,
     )(arrived, field)

time: 23.1 us -> 23.1 us (level)
  no operation moved by 1% of the time
where the time goes in v11:
time: 23.1 us; the launch traced here: 22.8 us
  starting transfers between devices  11.1 us (48%)
  Pallas kernels  9.9 us (43%)
  waiting for transfers between devices  1.75 us (8%)
    pallas_call x9, Pallas kernels, call(): pl.pallas_call(body, out_shape=outs, in_specs=[pl.BlockSpec(memory_space=...  9.9 us
    ppermute x1, starting transfers between devices, per_device(): oth = lax.ppermute(sent, 'tile', other_of)  4.88 us
    all_to_all x1, starting transfers between devices, per_device(): lax.all_to_all(packed, 'tile', split_axis=0, concat_axis=0, tiled=True)  3.52 us
    ppermute x2, starting transfers between devices, across(): return lax.ppermute(block, ('slot', 'tile'), pairs)  2.16 us
    all_to_all x1, waiting for transfers between devices, per_device(): lax.all_to_all(packed, 'tile', split_axis=0, concat_axis=0, tiled=True)  1.73 us
  transfers between devices with their start and end apart: 6, of which 1 were waited for; matrix products, arithmetic and copies ran while one was open for 0% of the time, Pallas kernels for 40%

profile of v11, /device:TPU:0, one launch (start us, length us, event | category | flops | bytes accessed | tf_op | source)
XLA Modules:
  0.0 22.8 jit_solution(9549735603648977654)
XLA Ops:
  0.0 0.5 %collective-permute-start = (f32[128,512]{1,0:T(8,128)}, f32[128,512]{1,0:T(8,128)S(1)}, u32[]{:S(2)}, u32[]{:S(2)}) collective-permute-start(f32[128,512]{1,0:T(8,128)} %bitcast.20), channel_id=1, source_target_pairs={{0,1},{1,0},{2,3},{3,2},{4,5},{5,4},{6,7},{7,6},{8,9},{9,8},{10,11... | collective-permute-start | bytes 786440 | tf_op jit(solution)/shard_map/ppermute | solution.py:528
  0.5 2.2 %shard_map.127 = (f32[128,512]{1,0:T(8,128)S(1)}, bf16[384,128]{1,0:T(8,128)(2,1)}, s32[2,1,32]{2,1,0:T(1,128)S(1)}, s32[2,4,32]{2,1,0:T(4,128)S(1)}, bf16[2,4,3...) custom-call(f32[128,512]{1,0:T(8,128)} %bitcast.21, s32[2,1,32]{2,1,0:T(1,128)} %bitcast.25, ...), custom_call_target="tpu_custom_call" | custom-call | flops 10000000 | bytes 200000 | tf_op jit(solution)/shard_map/pallas_call | solution.py:473
  2.7 0.0 collective-permute-done.mate
  2.7 4.9 %collective-permute-start.1 = (bf16[144,512]{1,0:T(8,128)(2,1)S(1)}, bf16[144,512]{1,0:T(8,128)(2,1)S(1)}, u32[]{:S(2)}, u32[]{:S(2)}) collective-permute-start(bf16[144,512]{1,0:T(8,128)(2,1)S(1)} %shard_map.128.refs_5_), channel_id=1, source_target_pairs={{0,15},{1,2},{2,1},{3,4},{4,3},{5,6},{6,5},{7,8},{8,7},{9,10},{10,... | collective-permute-start | bytes 442376 | tf_op jit(solution)/shard_map/ppermute | solution.py:555
  7.6 3.5 %all-to-all-start = ((bf16[16,24,128]{2,1,0:T(8,128)(2,1)}), bf16[16,24,128]{2,1,0:T(8,128)(2,1)S(1)}, u32[]{:S(2)}, u32[]{:S(2)}) async-start(bf16[16,24,128]{2,1,0:T(8,128)(2,1)} %bitcast.9), calls=%async_computation | async-start | bytes 196608 | tf_op jit(solution)/shard_map/all_to_all | solution.py:566
  11.1 0.0 collective-permute-done.1.oth
  11.2 0.1 shard_map.130
  11.3 1.6 %collective-permute-start.2 = (bf16[160,512]{1,0:T(8,128)(2,1)S(1)}, bf16[160,512]{1,0:T(8,128)(2,1)S(1)}, u32[]{:S(2)}, u32[]{:S(2)}) collective-permute-start(bf16[160,512]{1,0:T(8,128)(2,1)S(1)} %get-tuple-element.55), channel_id=1, source_target_pairs={{16,0},{17,1},{18,2},{19,3},{20,4},{21,5},{22,6},{23,7},{24,8},{25... | collective-permute-start | bytes 491528 | tf_op jit(solution)/shard_map/ppermute | solution.py:526
  12.8 3.4 %shard_map.131 = (f32[64,512]{1,0:T(8,128)S(1)}, f32[192,512]{1,0:T(8,128)S(1)}, bf16[192,512]{1,0:T(8,128)(2,1)S(1)}, bf16[192,512]{1,0:T(8,128)(2,1)S(1)}, bf1...) custom-call(f32[1,512]{1,0:T(1,128)} %bitcast.28, ...), custom_call_target="tpu_custom_call" | custom-call | flops 99999997952 | bytes 4000000 | tf_op jit(solution)/shard_map/pallas_call | solution.py:473
  16.2 0.6 %collective-permute-start.4 = (bf16[128,512]{1,0:T(8,128)(2,1)S(1)}, bf16[128,512]{1,0:T(8,128)(2,1)S(1)}, u32[]{:S(2)}, u32[]{:S(2)}) collective-permute-start(bf16[128,512]{1,0:T(8,128)(2,1)S(1)} %get-tuple-element.64), channel_id=1, source_target_pairs={{16,0},{17,1},{18,2},{19,3},{20,4},{21,5},{22,6},{23,7},{24,8},{25... | collective-permute-start | bytes 393224 | tf_op jit(solution)/shard_map/ppermute | solution.py:526
  16.8 1.7 %all-to-all-done = bf16[16,24,128]{2,1,0:T(8,128)(2,1)S(1)} async-done(((bf16[16,24,128]{2,1,0:T(8,128)(2,1)}), bf16[16,24,128]{2,1,0:T(8,128)(2,1)S(1)}, u32[]{:S(2)}, u32[]{:S(2)}) %all-to-all-start) | async-done | bytes 98336 | tf_op jit(solution)/shard_map/all_to_all | solution.py:566
  18.5 0.5 %shard_map.132 = (bf16[256,128]{1,0:T(8,128)(2,1)S(1)}, bf16[128,128]{1,0:T(8,128)(2,1)S(1)}, bf16[32,384]{1,0:T(8,128)(2,1)S(1)}, bf16[32,384]{1,0:T(8,128)(2,1)S(1)}, f32[32,384]{1,0:T(8,128)S(1)}) custom-call(bf16[384,128]{1,0:T(8,128)(2,1)S(1)} %bitcast.18, bf16[256,512]{1,0:T(8,128)(2,1)S(1)} %get-tuple-element.43.field), custom_call_target="tpu_custom_call" | custom-call | flops 1000000000 | bytes 2000000 | tf_op jit(solution)/shard_map/pallas_call | solution.py:473
  19.1 0.1 collective-permute-start.3
  19.1 1.2 %shard_map.133 = (f32[256,512]{1,0:T(8,128)S(1)}, f32[128,512]{1,0:T(8,128)S(1)}, bf16[512,512]{1,0:T(8,128)(2,1)S(1)}, bf16[512,512]{1,0:T(8,128)(2,1)S(1)}) custom-call(bf16[512,512]{1,0:T(8,128)(2,1)} %wn_hbm.3, bf16[512,512]{1,0:T(8,128)(2,1)} %ws_hbm.3, bf16[256,128]{1,0:T(8,128)(2,1)S(1)} %get-tuple-element.44.spread_own, ...), custom_call_target="tpu_custom_call" | custom-call | flops 1000000000 | bytes 3000000 | tf_op jit(solution)/shard_map/pallas_call | solution.py:473
  20.4 0.0 collective-permute-done.3.message
  20.4 0.0 collective-permute-done.2.message16
  20.4 1.7 %shard_map.134.base = f32[128,512]{1,0:T(8,128)S(1)} custom-call(f32[256,512]{1,0:T(8,128)S(1)} %get-tuple-element.49.pulled, f32[128,512]{1,0:T(8,128)S(1)} %get-tuple-element.50.away, bf16[512,512]{1,0:T(8,128)(2,1)S(1)} %get-tuple-element.51.wn, bf16[512,512]{1,0:T(8,128)(2,1)S(1)} %get-tuple-element.52.ws, f32[1,512]{1,0:T(1,128)S(1)} %get-tuple-element.53.gain, ...), custom_call_target="tpu_custom_call" | custom-call | flops 603979776 | bytes 6000000 | tf_op jit(solution)/shard_map/pallas_call | solution.py:473
  22.1 0.0 collective-permute-done.4.before
  22.1 0.8 %shard_map.135 = f32[128,512]{1,0:T(8,128)} custom-call(f32[128,512]{1,0:T(8,128)S(1)} %shard_map.134.base, bf16[128,512]{1,0:T(8,128)(2,1)S(1)} %get-tuple-element.63.background, bf16[128,512]{1,0:T(8,128)(2,1)S(1)} %collective-permute-done.4.before, f32[1,512]{1,0:T(1,128)S(1)} %get-tuple-element.58.error), custom_call_target="tpu_custom_call" | custom-call | flops 1000000 | bytes 900000 | tf_op jit(solution)/shard_map/pallas_call | solution.py:473
  (2 shorter events, 0.1 us)
Async XLA Ops:
  0.0 2.7 %collective-permute-start = (f32[128,512]{1,0:T(8,128)}, f32[128,512]{1,0:T(8,128)S(1)}, u32[]{:S(2)}, u32[]{:S(2)}) collective-permute-start(f32[128,512]{1,0:T(8,128)} %bitcast.20), channel_id=1, source_target_pairs={{0,1},{1,0},{2,3},{3,2},{4,5},{5,4},{6,7},{7,6},{8,9},{9,8},{10,11... | collective-permute-start | bytes 786440 | tf_op jit(solution)/shard_map/ppermute | solution.py:528
  2.7 8.4 %collective-permute-start.1 = (bf16[144,512]{1,0:T(8,128)(2,1)S(1)}, bf16[144,512]{1,0:T(8,128)(2,1)S(1)}, u32[]{:S(2)}, u32[]{:S(2)}) collective-permute-start(bf16[144,512]{1,0:T(8,128)(2,1)S(1)} %shard_map.128.refs_5_), channel_id=1, source_target_pairs={{0,15},{1,2},{2,1},{3,4},{4,3},{5,6},{6,5},{7,8},{8,7},{9,10},{10,... | collective-permute-start | bytes 442376 | tf_op jit(solution)/shard_map/ppermute | solution.py:555
  7.6 10.9 %all-to-all-start = ((bf16[16,24,128]{2,1,0:T(8,128)(2,1)}), bf16[16,24,128]{2,1,0:T(8,128)(2,1)S(1)}, u32[]{:S(2)}, u32[]{:S(2)}) async-start(bf16[16,24,128]{2,1,0:T(8,128)(2,1)} %bitcast.9), calls=%async_computation | async-start | bytes 196608 | tf_op jit(solution)/shard_map/all_to_all | solution.py:566
  11.3 9.1 %collective-permute-start.2 = (bf16[160,512]{1,0:T(8,128)(2,1)S(1)}, bf16[160,512]{1,0:T(8,128)(2,1)S(1)}, u32[]{:S(2)}, u32[]{:S(2)}) collective-permute-start(bf16[160,512]{1,0:T(8,128)(2,1)S(1)} %get-tuple-element.55), channel_id=1, source_target_pairs={{16,0},{17,1},{18,2},{19,3},{20,4},{21,5},{22,6},{23,7},{24,8},{25... | collective-permute-start | bytes 491528 | tf_op jit(solution)/shard_map/ppermute | solution.py:526
  16.2 5.9 %collective-permute-start.4 = (bf16[128,512]{1,0:T(8,128)(2,1)S(1)}, bf16[128,512]{1,0:T(8,128)(2,1)S(1)}, u32[]{:S(2)}, u32[]{:S(2)}) collective-permute-start(bf16[128,512]{1,0:T(8,128)(2,1)S(1)} %get-tuple-element.64), channel_id=1, source_target_pairs={{16,0},{17,1},{18,2},{19,3},{20,4},{21,5},{22,6},{23,7},{24,8},{25... | collective-permute-start | bytes 393224 | tf_op jit(solution)/shard_map/ppermute | solution.py:526
  19.1 1.3 %collective-permute-start.3 = (bf16[128,128]{1,0:T(8,128)(2,1)S(1)}, bf16[128,128]{1,0:T(8,128)(2,1)S(1)}, u32[]{:S(2)}, u32[]{:S(2)}) collective-permute-start(bf16[128,128]{1,0:T(8,128)(2,1)S(1)} %get-tuple-element.59), channel_id=1, source_target_pairs={{0,1},{1,0},{2,3},{3,2},{4,5},{5,4},{6,7},{7,6},{8,9},{9,8},{10,11... | collective-permute-start | bytes 98312 | tf_op jit(solution)/shard_map/ppermute | solution.py:606

commit v12 on v11

--- a/solution.py
+++ b/solution.py
@@ -358,25 +358,22 @@
 
 def adjoint_step(u, cot, gb, gm, flat, d, out, gain, ws, wn, wo, members):
     both = 2 * SLIM
-    gb[...] = cot[...].astype(BF16)
-    flat[...] = dot_t(gb[...], wo[...])
-    gb[...] = (flat[...] * d[...]).astype(BF16)
-    gm[...] = dot_t(gb[...], wn[...])
+    gb[...] = (dot_t(gb[...], wo[...]) * d[...]).astype(BF16)
+    gm[...] = dot_t(gb[...], wn[...]).astype(BF16)
     flat[...] = dot_t(gb[...], ws[...])
     for m in range(members):
         base = m * both
-        rows = []
-        for lat in range(2):
-            start = base + lat * SLIM
-            rows.append(gm[start : start + SLIM].astype(BF16).astype(F32))
-        around = neighbours(rows)
+        pair = gm[base : base + both].astype(F32)
+        around = neighbours([pair[:SLIM], pair[SLIM:]])
+        values = []
         for lat in range(2):
             start = base + lat * SLIM
             x = u[start : start + SLIM]
             s = inverse_rms(x)
             scaled = gain * (flat[start : start + SLIM] + around[lat])
             inner = jnp.mean(x * scaled, axis=-1, keepdims=True)
-            out(2 * m + lat, cot[start : start + SLIM] + s * scaled - x * (s * s * s * inner))
+            values.append(cot[start : start + SLIM] + s * scaled - x * (s * s * s * inner))
+        out(m, values)
 
 
 def edges(nxt, size, edge, r):
@@ -418,7 +415,7 @@
     pulled, away, wn, ws, gain, control, edge0, message16, f2x, wo, readout, error, message,
     u1x, d0x, d1x,
     result,
-    cot2, cot1, gb, gm, flat, mate_pull, edge, u0x, final, nxt,
+    cot2, cot1, gb, gb2, gm, flat, mate_pull, edge, u0x, final, nxt,
 ):
     size = result.shape[0]
     members = size // 32
@@ -436,24 +433,32 @@
         group = jnp.where(mate_side, mate_pull[near : near + 8], away[near : near + 8])
         return pulled[own : own + 16], group
 
-    for r in range(2 * members):
-        own, group = pulls(1, r)
-        a, b = r * SLIM, r * SLIM + 16
-        cot2[a:b] = own - weight * (nxt[r * 16 : (r + 1) * 16] - final[a:b])
-        u0x[a:b] = control[r * 16 : (r + 1) * 16]
-        a, b = b, b + 8
-        cot2[a:b] = group - weight * (edges(nxt, size, edge, r) - final[a:b])
-        u0x[a:b] = edge0[r * 8 : (r + 1) * 8]
-
-    def keep(r, value):
-        cot1[r * SLIM : (r + 1) * SLIM] = value + jnp.concatenate(pulls(0, r), axis=0)
-
-    def finish(r, value):
-        a, b = r * SLIM, r * SLIM + 16
-        result[r * 16 : (r + 1) * 16] = value[0:16] + error[...] * u0x[a:b]
+    for m in range(members):
+        pair = []
+        for r in (2 * m, 2 * m + 1):
+            own, group = pulls(1, r)
+            a, b, c = r * SLIM, r * SLIM + 16, (r + 1) * SLIM
+            u0x[a:b] = control[r * 16 : (r + 1) * 16]
+            u0x[b:c] = edge0[r * 8 : (r + 1) * 8]
+            pair.append(own - weight * (nxt[r * 16 : (r + 1) * 16] - final[a:b]))
+            pair.append(group - weight * (edges(nxt, size, edge, r) - final[b:c]))
+        at = slice(2 * m * SLIM, (2 * m + 2) * SLIM)
+        cot2[at] = jnp.concatenate(pair, axis=0)
+        gb[at] = jnp.concatenate(pair, axis=0).astype(BF16)
+
+    def keep(m, values):
+        pair = [value + jnp.concatenate(pulls(0, 2 * m + i), axis=0) for i, value in enumerate(values)]
+        at = slice(2 * m * SLIM, (2 * m + 2) * SLIM)
+        cot1[at] = jnp.concatenate(pair, axis=0)
+        gb2[at] = jnp.concatenate(pair, axis=0).astype(BF16)
+
+    def finish(m, values):
+        for r, value in zip((2 * m, 2 * m + 1), values):
+            a, b = r * SLIM, r * SLIM + 16
+            result[r * 16 : (r + 1) * 16] = value[0:16] + error[...] * u0x[a:b]
 
     adjoint_step(u1x, cot2, gb, gm, flat, d1x, keep, gain[...], ws, wn, wo, members)
-    adjoint_step(u0x, cot1, gb, gm, flat, d0x, finish, gain[...], ws, wn, wo, members)
+    adjoint_step(u0x, cot1, gb2, gm, flat, d0x, finish, gain[...], ws, wn, wo, members)
 
 
 def last_kernel(base, background, before, error, result):
@@ -615,7 +620,7 @@
     base = kernel_call(
         backward_kernel,
         spec(size),
-        [scratch(slim), scratch(slim), scratch(slim, BF16), scratch(slim), scratch(slim)]
+        [scratch(slim), scratch(slim), scratch(slim, BF16), scratch(slim, BF16), scratch(slim, BF16), scratch(slim)]
         + [scratch(size), scratch(16), scratch(slim), scratch(slim), scratch(size + 4 * groups)],
         12 * slim * channels * channels,
         6000000,

time: 23.1 us -> 23.1 us (level)
  no operation moved by 1% of the time
where the time goes in v12:
time: 23.1 us; the launch traced here: 22.8 us
  starting transfers between devices  11.1 us (48%)
  Pallas kernels  9.9 us (43%)
  waiting for transfers between devices  1.75 us (8%)
    pallas_call x9, Pallas kernels, call(): pl.pallas_call(body, out_shape=outs, in_specs=[pl.BlockSpec(memory_space=...  9.9 us
    ppermute x1, starting transfers between devices, per_device(): oth = lax.ppermute(sent, 'tile', other_of)  4.88 us
    all_to_all x1, starting transfers between devices, per_device(): lax.all_to_all(packed, 'tile', split_axis=0, concat_axis=0, tiled=True)  3.52 us
    ppermute x2, starting transfers between devices, across(): return lax.ppermute(block, ('slot', 'tile'), pairs)  2.16 us
    all_to_all x1, waiting for transfers between devices, per_device(): lax.all_to_all(packed, 'tile', split_axis=0, concat_axis=0, tiled=True)  1.73 us
  transfers between devices with their start and end apart: 6, of which 1 were waited for; matrix products, arithmetic and copies ran while one was open for 0% of the time, Pallas kernels for 40%

profile of v12, /device:TPU:0, one launch (start us, length us, event | category | flops | bytes accessed | tf_op | source)
XLA Modules:
  0.0 22.8 jit_solution(18402133874782955446)
XLA Ops:
  0.0 0.5 %collective-permute-start = (f32[128,512]{1,0:T(8,128)}, f32[128,512]{1,0:T(8,128)S(1)}, u32[]{:S(2)}, u32[]{:S(2)}) collective-permute-start(f32[128,512]{1,0:T(8,128)} %bitcast.20), channel_id=1, source_target_pairs={{0,1},{1,0},{2,3},{3,2},{4,5},{5,4},{6,7},{7,6},{8,9},{9,8},{10,11... | collective-permute-start | bytes 786440 | tf_op jit(solution)/shard_map/ppermute | solution.py:533
  0.5 2.2 %shard_map.127 = (f32[128,512]{1,0:T(8,128)S(1)}, bf16[384,128]{1,0:T(8,128)(2,1)}, s32[2,1,32]{2,1,0:T(1,128)S(1)}, s32[2,4,32]{2,1,0:T(4,128)S(1)}, bf16[2,4,3...) custom-call(f32[128,512]{1,0:T(8,128)} %bitcast.21, s32[2,1,32]{2,1,0:T(1,128)} %bitcast.25, ...), custom_call_target="tpu_custom_call" | custom-call | flops 10000000 | bytes 200000 | tf_op jit(solution)/shard_map/pallas_call | solution.py:478
  2.7 0.0 collective-permute-done.mate
  2.7 4.9 %collective-permute-start.1 = (bf16[144,512]{1,0:T(8,128)(2,1)S(1)}, bf16[144,512]{1,0:T(8,128)(2,1)S(1)}, u32[]{:S(2)}, u32[]{:S(2)}) collective-permute-start(bf16[144,512]{1,0:T(8,128)(2,1)S(1)} %shard_map.128.refs_5_), channel_id=1, source_target_pairs={{0,15},{1,2},{2,1},{3,4},{4,3},{5,6},{6,5},{7,8},{8,7},{9,10},{10,... | collective-permute-start | bytes 442376 | tf_op jit(solution)/shard_map/ppermute | solution.py:560
  7.6 3.5 %all-to-all-start = ((bf16[16,24,128]{2,1,0:T(8,128)(2,1)}), bf16[16,24,128]{2,1,0:T(8,128)(2,1)S(1)}, u32[]{:S(2)}, u32[]{:S(2)}) async-start(bf16[16,24,128]{2,1,0:T(8,128)(2,1)} %bitcast.9), calls=%async_computation | async-start | bytes 196608 | tf_op jit(solution)/shard_map/all_to_all | solution.py:571
  11.1 0.0 collective-permute-done.1.oth
  11.2 0.1 shard_map.130
  11.3 1.6 %collective-permute-start.2 = (bf16[160,512]{1,0:T(8,128)(2,1)S(1)}, bf16[160,512]{1,0:T(8,128)(2,1)S(1)}, u32[]{:S(2)}, u32[]{:S(2)}) collective-permute-start(bf16[160,512]{1,0:T(8,128)(2,1)S(1)} %get-tuple-element.55), channel_id=1, source_target_pairs={{16,0},{17,1},{18,2},{19,3},{20,4},{21,5},{22,6},{23,7},{24,8},{25... | collective-permute-start | bytes 491528 | tf_op jit(solution)/shard_map/ppermute | solution.py:531
  12.8 3.4 %shard_map.131 = (f32[64,512]{1,0:T(8,128)S(1)}, f32[192,512]{1,0:T(8,128)S(1)}, bf16[192,512]{1,0:T(8,128)(2,1)S(1)}, bf16[192,512]{1,0:T(8,128)(2,1)S(1)}, bf1...) custom-call(f32[1,512]{1,0:T(1,128)} %bitcast.28, ...), custom_call_target="tpu_custom_call" | custom-call | flops 99999997952 | bytes 4000000 | tf_op jit(solution)/shard_map/pallas_call | solution.py:478
  16.2 0.6 %collective-permute-start.4 = (bf16[128,512]{1,0:T(8,128)(2,1)S(1)}, bf16[128,512]{1,0:T(8,128)(2,1)S(1)}, u32[]{:S(2)}, u32[]{:S(2)}) collective-permute-start(bf16[128,512]{1,0:T(8,128)(2,1)S(1)} %get-tuple-element.64), channel_id=1, source_target_pairs={{16,0},{17,1},{18,2},{19,3},{20,4},{21,5},{22,6},{23,7},{24,8},{25... | collective-permute-start | bytes 393224 | tf_op jit(solution)/shard_map/ppermute | solution.py:531
  16.8 1.7 %all-to-all-done = bf16[16,24,128]{2,1,0:T(8,128)(2,1)S(1)} async-done(((bf16[16,24,128]{2,1,0:T(8,128)(2,1)}), bf16[16,24,128]{2,1,0:T(8,128)(2,1)S(1)}, u32[]{:S(2)}, u32[]{:S(2)}) %all-to-all-start) | async-done | bytes 98336 | tf_op jit(solution)/shard_map/all_to_all | solution.py:571
  18.5 0.5 %shard_map.132 = (bf16[256,128]{1,0:T(8,128)(2,1)S(1)}, bf16[128,128]{1,0:T(8,128)(2,1)S(1)}, bf16[32,384]{1,0:T(8,128)(2,1)S(1)}, bf16[32,384]{1,0:T(8,128)(2,1)S(1)}, f32[32,384]{1,0:T(8,128)S(1)}) custom-call(bf16[384,128]{1,0:T(8,128)(2,1)S(1)} %bitcast.18, bf16[256,512]{1,0:T(8,128)(2,1)S(1)} %get-tuple-element.43.field), custom_call_target="tpu_custom_call" | custom-call | flops 1000000000 | bytes 2000000 | tf_op jit(solution)/shard_map/pallas_call | solution.py:478
  19.1 0.1 collective-permute-start.3
  19.1 1.2 %shard_map.133 = (f32[256,512]{1,0:T(8,128)S(1)}, f32[128,512]{1,0:T(8,128)S(1)}, bf16[512,512]{1,0:T(8,128)(2,1)S(1)}, bf16[512,512]{1,0:T(8,128)(2,1)S(1)}) custom-call(bf16[512,512]{1,0:T(8,128)(2,1)} %wn_hbm.3, bf16[512,512]{1,0:T(8,128)(2,1)} %ws_hbm.3, bf16[256,128]{1,0:T(8,128)(2,1)S(1)} %get-tuple-element.44.spread_own, ...), custom_call_target="tpu_custom_call" | custom-call | flops 1000000000 | bytes 3000000 | tf_op jit(solution)/shard_map/pallas_call | solution.py:478
  20.4 0.0 collective-permute-done.3.message
  20.4 0.0 collective-permute-done.2.message16
  20.4 1.7 %shard_map.134.base = f32[128,512]{1,0:T(8,128)S(1)} custom-call(f32[256,512]{1,0:T(8,128)S(1)} %get-tuple-element.49.pulled, f32[128,512]{1,0:T(8,128)S(1)} %get-tuple-element.50.away, bf16[512,512]{1,0:T(8,128)(2,1)S(1)} %get-tuple-element.51.wn, bf16[512,512]{1,0:T(8,128)(2,1)S(1)} %get-tuple-element.52.ws, f32[1,512]{1,0:T(1,128)S(1)} %get-tuple-element.53.gain, ...), custom_call_target="tpu_custom_call" | custom-call | flops 603979776 | bytes 6000000 | tf_op jit(solution)/shard_map/pallas_call | solution.py:478
  22.1 0.0 collective-permute-done.4.before
  22.1 0.8 %shard_map.135 = f32[128,512]{1,0:T(8,128)} custom-call(f32[128,512]{1,0:T(8,128)S(1)} %shard_map.134.base, bf16[128,512]{1,0:T(8,128)(2,1)S(1)} %get-tuple-element.63.background, bf16[128,512]{1,0:T(8,128)(2,1)S(1)} %collective-permute-done.4.before, f32[1,512]{1,0:T(1,128)S(1)} %get-tuple-element.58.error), custom_call_target="tpu_custom_call" | custom-call | flops 1000000 | bytes 900000 | tf_op jit(solution)/shard_map/pallas_call | solution.py:478
  (2 shorter events, 0.1 us)
Async XLA Ops:
  0.0 2.7 %collective-permute-start = (f32[128,512]{1,0:T(8,128)}, f32[128,512]{1,0:T(8,128)S(1)}, u32[]{:S(2)}, u32[]{:S(2)}) collective-permute-start(f32[128,512]{1,0:T(8,128)} %bitcast.20), channel_id=1, source_target_pairs={{0,1},{1,0},{2,3},{3,2},{4,5},{5,4},{6,7},{7,6},{8,9},{9,8},{10,11... | collective-permute-start | bytes 786440 | tf_op jit(solution)/shard_map/ppermute | solution.py:533
  2.7 8.4 %collective-permute-start.1 = (bf16[144,512]{1,0:T(8,128)(2,1)S(1)}, bf16[144,512]{1,0:T(8,128)(2,1)S(1)}, u32[]{:S(2)}, u32[]{:S(2)}) collective-permute-start(bf16[144,512]{1,0:T(8,128)(2,1)S(1)} %shard_map.128.refs_5_), channel_id=1, source_target_pairs={{0,15},{1,2},{2,1},{3,4},{4,3},{5,6},{6,5},{7,8},{8,7},{9,10},{10,... | collective-permute-start | bytes 442376 | tf_op jit(solution)/shard_map/ppermute | solution.py:560
  7.6 10.9 %all-to-all-start = ((bf16[16,24,128]{2,1,0:T(8,128)(2,1)}), bf16[16,24,128]{2,1,0:T(8,128)(2,1)S(1)}, u32[]{:S(2)}, u32[]{:S(2)}) async-start(bf16[16,24,128]{2,1,0:T(8,128)(2,1)} %bitcast.9), calls=%async_computation | async-start | bytes 196608 | tf_op jit(solution)/shard_map/all_to_all | solution.py:571
  11.3 9.1 %collective-permute-start.2 = (bf16[160,512]{1,0:T(8,128)(2,1)S(1)}, bf16[160,512]{1,0:T(8,128)(2,1)S(1)}, u32[]{:S(2)}, u32[]{:S(2)}) collective-permute-start(bf16[160,512]{1,0:T(8,128)(2,1)S(1)} %get-tuple-element.55), channel_id=1, source_target_pairs={{16,0},{17,1},{18,2},{19,3},{20,4},{21,5},{22,6},{23,7},{24,8},{25... | collective-permute-start | bytes 491528 | tf_op jit(solution)/shard_map/ppermute | solution.py:531
  16.2 5.9 %collective-permute-start.4 = (bf16[128,512]{1,0:T(8,128)(2,1)S(1)}, bf16[128,512]{1,0:T(8,128)(2,1)S(1)}, u32[]{:S(2)}, u32[]{:S(2)}) collective-permute-start(bf16[128,512]{1,0:T(8,128)(2,1)S(1)} %get-tuple-element.64), channel_id=1, source_target_pairs={{16,0},{17,1},{18,2},{19,3},{20,4},{21,5},{22,6},{23,7},{24,8},{25... | collective-permute-start | bytes 393224 | tf_op jit(solution)/shard_map/ppermute | solution.py:531
  19.1 1.3 %collective-permute-start.3 = (bf16[128,128]{1,0:T(8,128)(2,1)S(1)}, bf16[128,128]{1,0:T(8,128)(2,1)S(1)}, u32[]{:S(2)}, u32[]{:S(2)}) collective-permute-start(bf16[128,128]{1,0:T(8,128)(2,1)S(1)} %get-tuple-element.59), channel_id=1, source_target_pairs={{0,1},{1,0},{2,3},{3,2},{4,5},{5,4},{6,7},{7,6},{8,9},{9,8},{10,11... | collective-permute-start | bytes 98312 | tf_op jit(solution)/shard_map/ppermute | solution.py:611

commit v13 on v11

--- a/solution.py
+++ b/solution.py
@@ -101,7 +101,7 @@
 
 
 def early():
-    return lax.axis_index("tile") < lax.axis_size("tile") // 2
+    return lax.axis_index("tile") < lax.axis_size("tile") * 3 // 4
 
 
 def first_kernel(control_hbm, *refs):

time: 23.1 us -> 23.7 us (1.026)
  starting transfers between devices: 11.1 us -> 11.6 us
    all_to_all x1, starting transfers between devices: 3.52 us -> 4.06 us  [per_device(): lax.all_to_all(packed, 'tile', split_axis=0, concat_axis=0, tiled=True)]
  transfers between devices with their start and end apart: 6 -> 6, of which waited for: 1 -> 1; matrix products, arithmetic and copies ran while one was open for 0% -> 0% of each run, Pallas kernels for 40% -> 39%
where the time goes in v13:
time: 23.7 us; the launch traced here: 23.4 us
  starting transfers between devices  11.6 us (49%)
  Pallas kernels  9.9 us (42%)
  waiting for transfers between devices  1.78 us (8%)
    pallas_call x9, Pallas kernels, call(): pl.pallas_call(body, out_shape=outs, in_specs=[pl.BlockSpec(memory_space=...  9.9 us
    ppermute x1, starting transfers between devices, per_device(): oth = lax.ppermute(sent, 'tile', other_of)  4.88 us
    all_to_all x1, starting transfers between devices, per_device(): lax.all_to_all(packed, 'tile', split_axis=0, concat_axis=0, tiled=True)  4.06 us
    ppermute x2, starting transfers between devices, across(): return lax.ppermute(block, ('slot', 'tile'), pairs)  2.16 us
    all_to_all x1, waiting for transfers between devices, per_device(): lax.all_to_all(packed, 'tile', split_axis=0, concat_axis=0, tiled=True)  1.77 us
  transfers between devices with their start and end apart: 6, of which 1 were waited for; matrix products, arithmetic and copies ran while one was open for 0% of the time, Pallas kernels for 39%

profile of v13, /device:TPU:0, one launch (start us, length us, event | category | flops | bytes accessed | tf_op | source)
XLA Modules:
  0.0 23.4 jit_solution(13153429633610060607)
XLA Ops:
  0.0 0.5 %collective-permute-start = (f32[128,512]{1,0:T(8,128)}, f32[128,512]{1,0:T(8,128)S(1)}, u32[]{:S(2)}, u32[]{:S(2)}) collective-permute-start(f32[128,512]{1,0:T(8,128)} %bitcast.20), channel_id=1, source_target_pairs={{0,1},{1,0},{2,3},{3,2},{4,5},{5,4},{6,7},{7,6},{8,9},{9,8},{10,11... | collective-permute-start | bytes 786440 | tf_op jit(solution)/shard_map/ppermute | solution.py:528
  0.5 2.2 %shard_map.127 = (f32[128,512]{1,0:T(8,128)S(1)}, bf16[384,128]{1,0:T(8,128)(2,1)}, s32[2,1,32]{2,1,0:T(1,128)S(1)}, s32[2,4,32]{2,1,0:T(4,128)S(1)}, bf16[2,4,3...) custom-call(f32[128,512]{1,0:T(8,128)} %bitcast.21, s32[2,1,32]{2,1,0:T(1,128)} %bitcast.25, ...), custom_call_target="tpu_custom_call" | custom-call | flops 10000000 | bytes 200000 | tf_op jit(solution)/shard_map/pallas_call | solution.py:473
  2.7 0.0 collective-permute-done.mate
  2.7 4.9 %collective-permute-start.1 = (bf16[144,512]{1,0:T(8,128)(2,1)S(1)}, bf16[144,512]{1,0:T(8,128)(2,1)S(1)}, u32[]{:S(2)}, u32[]{:S(2)}) collective-permute-start(bf16[144,512]{1,0:T(8,128)(2,1)S(1)} %shard_map.128.refs_5_), channel_id=1, source_target_pairs={{0,15},{1,2},{2,1},{3,4},{4,3},{5,6},{6,5},{7,8},{8,7},{9,10},{10,... | collective-permute-start | bytes 442376 | tf_op jit(solution)/shard_map/ppermute | solution.py:555
  7.6 4.1 %all-to-all-start = ((bf16[16,24,128]{2,1,0:T(8,128)(2,1)}), bf16[16,24,128]{2,1,0:T(8,128)(2,1)S(1)}, u32[]{:S(2)}, u32[]{:S(2)}) async-start(bf16[16,24,128]{2,1,0:T(8,128)(2,1)} %bitcast.9), calls=%async_computation | async-start | bytes 196608 | tf_op jit(solution)/shard_map/all_to_all | solution.py:566
  11.7 0.0 collective-permute-done.1.oth
  11.7 0.1 shard_map.130
  11.8 1.6 %collective-permute-start.2 = (bf16[160,512]{1,0:T(8,128)(2,1)S(1)}, bf16[160,512]{1,0:T(8,128)(2,1)S(1)}, u32[]{:S(2)}, u32[]{:S(2)}) collective-permute-start(bf16[160,512]{1,0:T(8,128)(2,1)S(1)} %get-tuple-element.55), channel_id=1, source_target_pairs={{16,0},{17,1},{18,2},{19,3},{20,4},{21,5},{22,6},{23,7},{24,8},{25... | collective-permute-start | bytes 491528 | tf_op jit(solution)/shard_map/ppermute | solution.py:526
  13.4 3.4 %shard_map.131 = (f32[64,512]{1,0:T(8,128)S(1)}, f32[192,512]{1,0:T(8,128)S(1)}, bf16[192,512]{1,0:T(8,128)(2,1)S(1)}, bf16[192,512]{1,0:T(8,128)(2,1)S(1)}, bf1...) custom-call(f32[1,512]{1,0:T(1,128)} %bitcast.28, ...), custom_call_target="tpu_custom_call" | custom-call | flops 99999997952 | bytes 4000000 | tf_op jit(solution)/shard_map/pallas_call | solution.py:473
  16.7 0.6 %collective-permute-start.4 = (bf16[128,512]{1,0:T(8,128)(2,1)S(1)}, bf16[128,512]{1,0:T(8,128)(2,1)S(1)}, u32[]{:S(2)}, u32[]{:S(2)}) collective-permute-start(bf16[128,512]{1,0:T(8,128)(2,1)S(1)} %get-tuple-element.64), channel_id=1, source_target_pairs={{16,0},{17,1},{18,2},{19,3},{20,4},{21,5},{22,6},{23,7},{24,8},{25... | collective-permute-start | bytes 393224 | tf_op jit(solution)/shard_map/ppermute | solution.py:526
  17.3 1.8 %all-to-all-done = bf16[16,24,128]{2,1,0:T(8,128)(2,1)S(1)} async-done(((bf16[16,24,128]{2,1,0:T(8,128)(2,1)}), bf16[16,24,128]{2,1,0:T(8,128)(2,1)S(1)}, u32[]{:S(2)}, u32[]{:S(2)}) %all-to-all-start) | async-done | bytes 98336 | tf_op jit(solution)/shard_map/all_to_all | solution.py:566
  19.1 0.5 %shard_map.132 = (bf16[256,128]{1,0:T(8,128)(2,1)S(1)}, bf16[128,128]{1,0:T(8,128)(2,1)S(1)}, bf16[32,384]{1,0:T(8,128)(2,1)S(1)}, bf16[32,384]{1,0:T(8,128)(2,1)S(1)}, f32[32,384]{1,0:T(8,128)S(1)}) custom-call(bf16[384,128]{1,0:T(8,128)(2,1)S(1)} %bitcast.18, bf16[256,512]{1,0:T(8,128)(2,1)S(1)} %get-tuple-element.43.field), custom_call_target="tpu_custom_call" | custom-call | flops 1000000000 | bytes 2000000 | tf_op jit(solution)/shard_map/pallas_call | solution.py:473
  19.6 0.1 collective-permute-start.3
  19.7 1.2 %shard_map.133 = (f32[256,512]{1,0:T(8,128)S(1)}, f32[128,512]{1,0:T(8,128)S(1)}, bf16[512,512]{1,0:T(8,128)(2,1)S(1)}, bf16[512,512]{1,0:T(8,128)(2,1)S(1)}) custom-call(bf16[512,512]{1,0:T(8,128)(2,1)} %wn_hbm.3, bf16[512,512]{1,0:T(8,128)(2,1)} %ws_hbm.3, bf16[256,128]{1,0:T(8,128)(2,1)S(1)} %get-tuple-element.44.spread_own, ...), custom_call_target="tpu_custom_call" | custom-call | flops 1000000000 | bytes 3000000 | tf_op jit(solution)/shard_map/pallas_call | solution.py:473
  20.9 0.0 collective-permute-done.3.message
  21.0 0.0 collective-permute-done.2.message16
  21.0 1.7 %shard_map.134.base = f32[128,512]{1,0:T(8,128)S(1)} custom-call(f32[256,512]{1,0:T(8,128)S(1)} %get-tuple-element.49.pulled, f32[128,512]{1,0:T(8,128)S(1)} %get-tuple-element.50.away, bf16[512,512]{1,0:T(8,128)(2,1)S(1)} %get-tuple-element.51.wn, bf16[512,512]{1,0:T(8,128)(2,1)S(1)} %get-tuple-element.52.ws, f32[1,512]{1,0:T(1,128)S(1)} %get-tuple-element.53.gain, ...), custom_call_target="tpu_custom_call" | custom-call | flops 603979776 | bytes 6000000 | tf_op jit(solution)/shard_map/pallas_call | solution.py:473
  22.6 0.0 collective-permute-done.4.before
  22.6 0.8 %shard_map.135 = f32[128,512]{1,0:T(8,128)} custom-call(f32[128,512]{1,0:T(8,128)S(1)} %shard_map.134.base, bf16[128,512]{1,0:T(8,128)(2,1)S(1)} %get-tuple-element.63.background, bf16[128,512]{1,0:T(8,128)(2,1)S(1)} %collective-permute-done.4.before, f32[1,512]{1,0:T(1,128)S(1)} %get-tuple-element.58.error), custom_call_target="tpu_custom_call" | custom-call | flops 1000000 | bytes 900000 | tf_op jit(solution)/shard_map/pallas_call | solution.py:473
  (2 shorter events, 0.1 us)
Async XLA Ops:
  0.0 2.7 %collective-permute-start = (f32[128,512]{1,0:T(8,128)}, f32[128,512]{1,0:T(8,128)S(1)}, u32[]{:S(2)}, u32[]{:S(2)}) collective-permute-start(f32[128,512]{1,0:T(8,128)} %bitcast.20), channel_id=1, source_target_pairs={{0,1},{1,0},{2,3},{3,2},{4,5},{5,4},{6,7},{7,6},{8,9},{9,8},{10,11... | collective-permute-start | bytes 786440 | tf_op jit(solution)/shard_map/ppermute | solution.py:528
  2.7 9.0 %collective-permute-start.1 = (bf16[144,512]{1,0:T(8,128)(2,1)S(1)}, bf16[144,512]{1,0:T(8,128)(2,1)S(1)}, u32[]{:S(2)}, u32[]{:S(2)}) collective-permute-start(bf16[144,512]{1,0:T(8,128)(2,1)S(1)} %shard_map.128.refs_5_), channel_id=1, source_target_pairs={{0,15},{1,2},{2,1},{3,4},{4,3},{5,6},{6,5},{7,8},{8,7},{9,10},{10,... | collective-permute-start | bytes 442376 | tf_op jit(solution)/shard_map/ppermute | solution.py:555
  7.6 11.5 %all-to-all-start = ((bf16[16,24,128]{2,1,0:T(8,128)(2,1)}), bf16[16,24,128]{2,1,0:T(8,128)(2,1)S(1)}, u32[]{:S(2)}, u32[]{:S(2)}) async-start(bf16[16,24,128]{2,1,0:T(8,128)(2,1)} %bitcast.9), calls=%async_computation | async-start | bytes 196608 | tf_op jit(solution)/shard_map/all_to_all | solution.py:566
  11.8 9.2 %collective-permute-start.2 = (bf16[160,512]{1,0:T(8,128)(2,1)S(1)}, bf16[160,512]{1,0:T(8,128)(2,1)S(1)}, u32[]{:S(2)}, u32[]{:S(2)}) collective-permute-start(bf16[160,512]{1,0:T(8,128)(2,1)S(1)} %get-tuple-element.55), channel_id=1, source_target_pairs={{16,0},{17,1},{18,2},{19,3},{20,4},{21,5},{22,6},{23,7},{24,8},{25... | collective-permute-start | bytes 491528 | tf_op jit(solution)/shard_map/ppermute | solution.py:526
  16.7 5.9 %collective-permute-start.4 = (bf16[128,512]{1,0:T(8,128)(2,1)S(1)}, bf16[128,512]{1,0:T(8,128)(2,1)S(1)}, u32[]{:S(2)}, u32[]{:S(2)}) collective-permute-start(bf16[128,512]{1,0:T(8,128)(2,1)S(1)} %get-tuple-element.64), channel_id=1, source_target_pairs={{16,0},{17,1},{18,2},{19,3},{20,4},{21,5},{22,6},{23,7},{24,8},{25... | collective-permute-start | bytes 393224 | tf_op jit(solution)/shard_map/ppermute | solution.py:526
  19.6 1.3 %collective-permute-start.3 = (bf16[128,128]{1,0:T(8,128)(2,1)S(1)}, bf16[128,128]{1,0:T(8,128)(2,1)S(1)}, u32[]{:S(2)}, u32[]{:S(2)}) collective-permute-start(bf16[128,128]{1,0:T(8,128)(2,1)S(1)} %get-tuple-element.59), channel_id=1, source_target_pairs={{0,1},{1,0},{2,3},{3,2},{4,5},{5,4},{6,7},{7,6},{8,9},{9,8},{10,11... | collective-permute-start | bytes 98312 | tf_op jit(solution)/shard_map/ppermute | solution.py:606

commit v14 on v13

--- a/solution.py
+++ b/solution.py
@@ -101,7 +101,7 @@
 
 
 def early():
-    return lax.axis_index("tile") < lax.axis_size("tile") * 3 // 4
+    return lax.axis_index("tile") < lax.axis_size("tile") // 4
 
 
 def first_kernel(control_hbm, *refs):

time: 23.7 us -> 23.1 us (0.975)
  starting transfers between devices: 11.6 us -> 11.1 us
    all_to_all x1, starting transfers between devices: 4.06 us -> 3.52 us  [per_device(): lax.all_to_all(packed, 'tile', split_axis=0, concat_axis=0, tiled=True)]
  transfers between devices with their start and end apart: 6 -> 6, of which waited for: 1 -> 1; matrix products, arithmetic and copies ran while one was open for 0% -> 0% of each run, Pallas kernels for 39% -> 40%
where the time goes in v14:
time: 23.1 us; the launch traced here: 22.8 us
  starting transfers between devices  11.1 us (48%)
  Pallas kernels  9.9 us (43%)
  waiting for transfers between devices  1.75 us (8%)
    pallas_call x9, Pallas kernels, call(): pl.pallas_call(body, out_shape=outs, in_specs=[pl.BlockSpec(memory_space=...  9.9 us
    ppermute x1, starting transfers between devices, per_device(): oth = lax.ppermute(sent, 'tile', other_of)  4.88 us
    all_to_all x1, starting transfers between devices, per_device(): lax.all_to_all(packed, 'tile', split_axis=0, concat_axis=0, tiled=True)  3.52 us
    ppermute x2, starting transfers between devices, across(): return lax.ppermute(block, ('slot', 'tile'), pairs)  2.16 us
    all_to_all x1, waiting for transfers between devices, per_device(): lax.all_to_all(packed, 'tile', split_axis=0, concat_axis=0, tiled=True)  1.73 us
  transfers between devices with their start and end apart: 6, of which 1 were waited for; matrix products, arithmetic and copies ran while one was open for 0% of the time, Pallas kernels for 40%

profile of v14, /device:TPU:0, one launch (start us, length us, event | category | flops | bytes accessed | tf_op | source)
XLA Modules:
  0.0 22.8 jit_solution(5097340096621309430)
XLA Ops:
  0.0 0.5 %collective-permute-start = (f32[128,512]{1,0:T(8,128)}, f32[128,512]{1,0:T(8,128)S(1)}, u32[]{:S(2)}, u32[]{:S(2)}) collective-permute-start(f32[128,512]{1,0:T(8,128)} %bitcast.20), channel_id=1, source_target_pairs={{0,1},{1,0},{2,3},{3,2},{4,5},{5,4},{6,7},{7,6},{8,9},{9,8},{10,11... | collective-permute-start | bytes 786440 | tf_op jit(solution)/shard_map/ppermute | solution.py:528
  0.5 2.2 %shard_map.127 = (f32[128,512]{1,0:T(8,128)S(1)}, bf16[384,128]{1,0:T(8,128)(2,1)}, s32[2,1,32]{2,1,0:T(1,128)S(1)}, s32[2,4,32]{2,1,0:T(4,128)S(1)}, bf16[2,4,3...) custom-call(f32[128,512]{1,0:T(8,128)} %bitcast.21, s32[2,1,32]{2,1,0:T(1,128)} %bitcast.25, ...), custom_call_target="tpu_custom_call" | custom-call | flops 10000000 | bytes 200000 | tf_op jit(solution)/shard_map/pallas_call | solution.py:473
  2.7 0.0 collective-permute-done.mate
  2.7 4.9 %collective-permute-start.1 = (bf16[144,512]{1,0:T(8,128)(2,1)S(1)}, bf16[144,512]{1,0:T(8,128)(2,1)S(1)}, u32[]{:S(2)}, u32[]{:S(2)}) collective-permute-start(bf16[144,512]{1,0:T(8,128)(2,1)S(1)} %shard_map.128.refs_5_), channel_id=1, source_target_pairs={{0,15},{1,2},{2,1},{3,4},{4,3},{5,6},{6,5},{7,8},{8,7},{9,10},{10,... | collective-permute-start | bytes 442376 | tf_op jit(solution)/shard_map/ppermute | solution.py:555
  7.6 3.5 %all-to-all-start = ((bf16[16,24,128]{2,1,0:T(8,128)(2,1)}), bf16[16,24,128]{2,1,0:T(8,128)(2,1)S(1)}, u32[]{:S(2)}, u32[]{:S(2)}) async-start(bf16[16,24,128]{2,1,0:T(8,128)(2,1)} %bitcast.9), calls=%async_computation | async-start | bytes 196608 | tf_op jit(solution)/shard_map/all_to_all | solution.py:566
  11.1 0.0 collective-permute-done.1.oth
  11.2 0.1 shard_map.130
  11.3 1.6 %collective-permute-start.2 = (bf16[160,512]{1,0:T(8,128)(2,1)S(1)}, bf16[160,512]{1,0:T(8,128)(2,1)S(1)}, u32[]{:S(2)}, u32[]{:S(2)}) collective-permute-start(bf16[160,512]{1,0:T(8,128)(2,1)S(1)} %get-tuple-element.55), channel_id=1, source_target_pairs={{16,0},{17,1},{18,2},{19,3},{20,4},{21,5},{22,6},{23,7},{24,8},{25... | collective-permute-start | bytes 491528 | tf_op jit(solution)/shard_map/ppermute | solution.py:526
  12.8 3.4 %shard_map.131 = (f32[64,512]{1,0:T(8,128)S(1)}, f32[192,512]{1,0:T(8,128)S(1)}, bf16[192,512]{1,0:T(8,128)(2,1)S(1)}, bf16[192,512]{1,0:T(8,128)(2,1)S(1)}, bf1...) custom-call(f32[1,512]{1,0:T(1,128)} %bitcast.28, ...), custom_call_target="tpu_custom_call" | custom-call | flops 99999997952 | bytes 4000000 | tf_op jit(solution)/shard_map/pallas_call | solution.py:473
  16.2 0.6 %collective-permute-start.4 = (bf16[128,512]{1,0:T(8,128)(2,1)S(1)}, bf16[128,512]{1,0:T(8,128)(2,1)S(1)}, u32[]{:S(2)}, u32[]{:S(2)}) collective-permute-start(bf16[128,512]{1,0:T(8,128)(2,1)S(1)} %get-tuple-element.64), channel_id=1, source_target_pairs={{16,0},{17,1},{18,2},{19,3},{20,4},{21,5},{22,6},{23,7},{24,8},{25... | collective-permute-start | bytes 393224 | tf_op jit(solution)/shard_map/ppermute | solution.py:526
  16.8 1.7 %all-to-all-done = bf16[16,24,128]{2,1,0:T(8,128)(2,1)S(1)} async-done(((bf16[16,24,128]{2,1,0:T(8,128)(2,1)}), bf16[16,24,128]{2,1,0:T(8,128)(2,1)S(1)}, u32[]{:S(2)}, u32[]{:S(2)}) %all-to-all-start) | async-done | bytes 98336 | tf_op jit(solution)/shard_map/all_to_all | solution.py:566
  18.5 0.5 %shard_map.132 = (bf16[256,128]{1,0:T(8,128)(2,1)S(1)}, bf16[128,128]{1,0:T(8,128)(2,1)S(1)}, bf16[32,384]{1,0:T(8,128)(2,1)S(1)}, bf16[32,384]{1,0:T(8,128)(2,1)S(1)}, f32[32,384]{1,0:T(8,128)S(1)}) custom-call(bf16[384,128]{1,0:T(8,128)(2,1)S(1)} %bitcast.18, bf16[256,512]{1,0:T(8,128)(2,1)S(1)} %get-tuple-element.43.field), custom_call_target="tpu_custom_call" | custom-call | flops 1000000000 | bytes 2000000 | tf_op jit(solution)/shard_map/pallas_call | solution.py:473
  19.1 0.1 collective-permute-start.3
  19.1 1.2 %shard_map.133 = (f32[256,512]{1,0:T(8,128)S(1)}, f32[128,512]{1,0:T(8,128)S(1)}, bf16[512,512]{1,0:T(8,128)(2,1)S(1)}, bf16[512,512]{1,0:T(8,128)(2,1)S(1)}) custom-call(bf16[512,512]{1,0:T(8,128)(2,1)} %wn_hbm.3, bf16[512,512]{1,0:T(8,128)(2,1)} %ws_hbm.3, bf16[256,128]{1,0:T(8,128)(2,1)S(1)} %get-tuple-element.44.spread_own, ...), custom_call_target="tpu_custom_call" | custom-call | flops 1000000000 | bytes 3000000 | tf_op jit(solution)/shard_map/pallas_call | solution.py:473
  20.4 0.0 collective-permute-done.3.message
  20.4 0.0 collective-permute-done.2.message16
  20.4 1.7 %shard_map.134.base = f32[128,512]{1,0:T(8,128)S(1)} custom-call(f32[256,512]{1,0:T(8,128)S(1)} %get-tuple-element.49.pulled, f32[128,512]{1,0:T(8,128)S(1)} %get-tuple-element.50.away, bf16[512,512]{1,0:T(8,128)(2,1)S(1)} %get-tuple-element.51.wn, bf16[512,512]{1,0:T(8,128)(2,1)S(1)} %get-tuple-element.52.ws, f32[1,512]{1,0:T(1,128)S(1)} %get-tuple-element.53.gain, ...), custom_call_target="tpu_custom_call" | custom-call | flops 603979776 | bytes 6000000 | tf_op jit(solution)/shard_map/pallas_call | solution.py:473
  22.1 0.0 collective-permute-done.4.before
  22.1 0.8 %shard_map.135 = f32[128,512]{1,0:T(8,128)} custom-call(f32[128,512]{1,0:T(8,128)S(1)} %shard_map.134.base, bf16[128,512]{1,0:T(8,128)(2,1)S(1)} %get-tuple-element.63.background, bf16[128,512]{1,0:T(8,128)(2,1)S(1)} %collective-permute-done.4.before, f32[1,512]{1,0:T(1,128)S(1)} %get-tuple-element.58.error), custom_call_target="tpu_custom_call" | custom-call | flops 1000000 | bytes 900000 | tf_op jit(solution)/shard_map/pallas_call | solution.py:473
  (2 shorter events, 0.1 us)
Async XLA Ops:
  0.0 2.7 %collective-permute-start = (f32[128,512]{1,0:T(8,128)}, f32[128,512]{1,0:T(8,128)S(1)}, u32[]{:S(2)}, u32[]{:S(2)}) collective-permute-start(f32[128,512]{1,0:T(8,128)} %bitcast.20), channel_id=1, source_target_pairs={{0,1},{1,0},{2,3},{3,2},{4,5},{5,4},{6,7},{7,6},{8,9},{9,8},{10,11... | collective-permute-start | bytes 786440 | tf_op jit(solution)/shard_map/ppermute | solution.py:528
  2.7 8.4 %collective-permute-start.1 = (bf16[144,512]{1,0:T(8,128)(2,1)S(1)}, bf16[144,512]{1,0:T(8,128)(2,1)S(1)}, u32[]{:S(2)}, u32[]{:S(2)}) collective-permute-start(bf16[144,512]{1,0:T(8,128)(2,1)S(1)} %shard_map.128.refs_5_), channel_id=1, source_target_pairs={{0,15},{1,2},{2,1},{3,4},{4,3},{5,6},{6,5},{7,8},{8,7},{9,10},{10,... | collective-permute-start | bytes 442376 | tf_op jit(solution)/shard_map/ppermute | solution.py:555
  7.6 10.9 %all-to-all-start = ((bf16[16,24,128]{2,1,0:T(8,128)(2,1)}), bf16[16,24,128]{2,1,0:T(8,128)(2,1)S(1)}, u32[]{:S(2)}, u32[]{:S(2)}) async-start(bf16[16,24,128]{2,1,0:T(8,128)(2,1)} %bitcast.9), calls=%async_computation | async-start | bytes 196608 | tf_op jit(solution)/shard_map/all_to_all | solution.py:566
  11.3 9.1 %collective-permute-start.2 = (bf16[160,512]{1,0:T(8,128)(2,1)S(1)}, bf16[160,512]{1,0:T(8,128)(2,1)S(1)}, u32[]{:S(2)}, u32[]{:S(2)}) collective-permute-start(bf16[160,512]{1,0:T(8,128)(2,1)S(1)} %get-tuple-element.55), channel_id=1, source_target_pairs={{16,0},{17,1},{18,2},{19,3},{20,4},{21,5},{22,6},{23,7},{24,8},{25... | collective-permute-start | bytes 491528 | tf_op jit(solution)/shard_map/ppermute | solution.py:526
  16.2 5.9 %collective-permute-start.4 = (bf16[128,512]{1,0:T(8,128)(2,1)S(1)}, bf16[128,512]{1,0:T(8,128)(2,1)S(1)}, u32[]{:S(2)}, u32[]{:S(2)}) collective-permute-start(bf16[128,512]{1,0:T(8,128)(2,1)S(1)} %get-tuple-element.64), channel_id=1, source_target_pairs={{16,0},{17,1},{18,2},{19,3},{20,4},{21,5},{22,6},{23,7},{24,8},{25... | collective-permute-start | bytes 393224 | tf_op jit(solution)/shard_map/ppermute | solution.py:526
  19.1 1.3 %collective-permute-start.3 = (bf16[128,128]{1,0:T(8,128)(2,1)S(1)}, bf16[128,128]{1,0:T(8,128)(2,1)S(1)}, u32[]{:S(2)}, u32[]{:S(2)}) collective-permute-start(bf16[128,128]{1,0:T(8,128)(2,1)S(1)} %get-tuple-element.59), channel_id=1, source_target_pairs={{0,1},{1,0},{2,3},{3,2},{4,5},{5,4},{6,7},{7,6},{8,9},{9,8},{10,11... | collective-permute-start | bytes 98312 | tf_op jit(solution)/shard_map/ppermute | solution.py:606

commit v15 on v11

--- a/solution.py
+++ b/solution.py
@@ -456,10 +456,19 @@
     adjoint_step(u0x, cot1, gb, gm, flat, d0x, finish, gain[...], ws, wn, wo, members)
 
 
-def last_kernel(base, background, before, error, result):
+def last_kernel(base, background, before, error, result, held, sems):
     first = lax.axis_index("slot") == 0
-    taken = jnp.where(first, background[...].astype(F32), before[...].astype(F32))
-    result[...] = base[...] - error[...] * taken
+    count = base.shape[0] // sems.shape[0]
+    copies = []
+    for i in range(sems.shape[0]):
+        at = slice(i * count, (i + 1) * count)
+        taken = jnp.where(first, background[at].astype(F32), before[at].astype(F32))
+        held[at] = base[at] - error[...] * taken
+        rows = pl.ds(i * count, count)
+        copies.append(pltpu.make_async_copy(held.at[rows], result.at[rows], sems.at[i]))
+        copies[-1].start()
+    for copy in copies:
+        copy.wait()
 
 
 def kernel_call(body, outs, scratch, flops, moved, hbm=0, out_places=None, aliases={}):
@@ -623,7 +632,14 @@
         *handed, gain_held, held, edge0, nxt, f2x, wo, readout_held, error_held, from_mate,
         u1x, d0x, d1x,
     )
-    result = kernel_call(last_kernel, spec(size), [], 10**6, 900000)(base, background_held, before, error_held)
+    (result,) = kernel_call(
+        last_kernel,
+        [spec(size)],
+        [scratch(size), pltpu.SemaphoreType.DMA((4,))],
+        10**6,
+        900000,
+        out_places=[pltpu.HBM],
+    )(base, background_held, before, error_held)
     return result.reshape(control.shape)
 
 

time: 23.1 us -> 23.1 us (level)
  no operation moved by 1% of the time
where the time goes in v15:
time: 23.1 us; the launch traced here: 22.8 us
  starting transfers between devices  11.1 us (48%)
  Pallas kernels  9.89 us (43%)
  waiting for transfers between devices  1.75 us (8%)
    pallas_call x9, Pallas kernels, call(): pl.pallas_call(body, out_shape=outs, in_specs=[pl.BlockSpec(memory_space=...  9.89 us
    ppermute x1, starting transfers between devices, per_device(): oth = lax.ppermute(sent, 'tile', other_of)  4.88 us
    all_to_all x1, starting transfers between devices, per_device(): lax.all_to_all(packed, 'tile', split_axis=0, concat_axis=0, tiled=True)  3.52 us
    ppermute x2, starting transfers between devices, across(): return lax.ppermute(block, ('slot', 'tile'), pairs)  2.16 us
    all_to_all x1, waiting for transfers between devices, per_device(): lax.all_to_all(packed, 'tile', split_axis=0, concat_axis=0, tiled=True)  1.73 us
  transfers between devices with their start and end apart: 6, of which 1 were waited for; matrix products, arithmetic and copies ran while one was open for 0% of the time, Pallas kernels for 40%

profile of v15, /device:TPU:0, one launch (start us, length us, event | category | flops | bytes accessed | tf_op | source)
XLA Modules:
  0.0 22.8 jit_solution(8156446382783441012)
XLA Ops:
  0.0 0.5 %collective-permute-start = (f32[128,512]{1,0:T(8,128)}, f32[128,512]{1,0:T(8,128)S(1)}, u32[]{:S(2)}, u32[]{:S(2)}) collective-permute-start(f32[128,512]{1,0:T(8,128)} %bitcast.20), channel_id=1, source_target_pairs={{0,1},{1,0},{2,3},{3,2},{4,5},{5,4},{6,7},{7,6},{8,9},{9,8},{10,11... | collective-permute-start | bytes 786440 | tf_op jit(solution)/shard_map/ppermute | solution.py:537
  0.5 2.2 %shard_map.127 = (f32[128,512]{1,0:T(8,128)S(1)}, bf16[384,128]{1,0:T(8,128)(2,1)}, s32[2,1,32]{2,1,0:T(1,128)S(1)}, s32[2,4,32]{2,1,0:T(4,128)S(1)}, bf16[2,4,3...) custom-call(f32[128,512]{1,0:T(8,128)} %bitcast.21, s32[2,1,32]{2,1,0:T(1,128)} %bitcast.25, ...), custom_call_target="tpu_custom_call" | custom-call | flops 10000000 | bytes 200000 | tf_op jit(solution)/shard_map/pallas_call | solution.py:482
  2.7 0.0 collective-permute-done.mate
  2.7 4.9 %collective-permute-start.1 = (bf16[144,512]{1,0:T(8,128)(2,1)S(1)}, bf16[144,512]{1,0:T(8,128)(2,1)S(1)}, u32[]{:S(2)}, u32[]{:S(2)}) collective-permute-start(bf16[144,512]{1,0:T(8,128)(2,1)S(1)} %shard_map.128.refs_5_), channel_id=1, source_target_pairs={{0,15},{1,2},{2,1},{3,4},{4,3},{5,6},{6,5},{7,8},{8,7},{9,10},{10,... | collective-permute-start | bytes 442376 | tf_op jit(solution)/shard_map/ppermute | solution.py:564
  7.6 3.5 %all-to-all-start = ((bf16[16,24,128]{2,1,0:T(8,128)(2,1)}), bf16[16,24,128]{2,1,0:T(8,128)(2,1)S(1)}, u32[]{:S(2)}, u32[]{:S(2)}) async-start(bf16[16,24,128]{2,1,0:T(8,128)(2,1)} %bitcast.9), calls=%async_computation | async-start | bytes 196608 | tf_op jit(solution)/shard_map/all_to_all | solution.py:575
  11.1 0.0 collective-permute-done.1.oth
  11.2 0.1 shard_map.130
  11.3 1.6 %collective-permute-start.2 = (bf16[160,512]{1,0:T(8,128)(2,1)S(1)}, bf16[160,512]{1,0:T(8,128)(2,1)S(1)}, u32[]{:S(2)}, u32[]{:S(2)}) collective-permute-start(bf16[160,512]{1,0:T(8,128)(2,1)S(1)} %get-tuple-element.55), channel_id=1, source_target_pairs={{16,0},{17,1},{18,2},{19,3},{20,4},{21,5},{22,6},{23,7},{24,8},{25... | collective-permute-start | bytes 491528 | tf_op jit(solution)/shard_map/ppermute | solution.py:535
  12.8 3.4 %shard_map.131 = (f32[64,512]{1,0:T(8,128)S(1)}, f32[192,512]{1,0:T(8,128)S(1)}, bf16[192,512]{1,0:T(8,128)(2,1)S(1)}, bf16[192,512]{1,0:T(8,128)(2,1)S(1)}, bf1...) custom-call(f32[1,512]{1,0:T(1,128)} %bitcast.28, ...), custom_call_target="tpu_custom_call" | custom-call | flops 99999997952 | bytes 4000000 | tf_op jit(solution)/shard_map/pallas_call | solution.py:482
  16.2 0.6 %collective-permute-start.4 = (bf16[128,512]{1,0:T(8,128)(2,1)S(1)}, bf16[128,512]{1,0:T(8,128)(2,1)S(1)}, u32[]{:S(2)}, u32[]{:S(2)}) collective-permute-start(bf16[128,512]{1,0:T(8,128)(2,1)S(1)} %get-tuple-element.64), channel_id=1, source_target_pairs={{16,0},{17,1},{18,2},{19,3},{20,4},{21,5},{22,6},{23,7},{24,8},{25... | collective-permute-start | bytes 393224 | tf_op jit(solution)/shard_map/ppermute | solution.py:535
  16.8 1.7 %all-to-all-done = bf16[16,24,128]{2,1,0:T(8,128)(2,1)S(1)} async-done(((bf16[16,24,128]{2,1,0:T(8,128)(2,1)}), bf16[16,24,128]{2,1,0:T(8,128)(2,1)S(1)}, u32[]{:S(2)}, u32[]{:S(2)}) %all-to-all-start) | async-done | bytes 98336 | tf_op jit(solution)/shard_map/all_to_all | solution.py:575
  18.5 0.5 %shard_map.132 = (bf16[256,128]{1,0:T(8,128)(2,1)S(1)}, bf16[128,128]{1,0:T(8,128)(2,1)S(1)}, bf16[32,384]{1,0:T(8,128)(2,1)S(1)}, bf16[32,384]{1,0:T(8,128)(2,1)S(1)}, f32[32,384]{1,0:T(8,128)S(1)}) custom-call(bf16[384,128]{1,0:T(8,128)(2,1)S(1)} %bitcast.18, bf16[256,512]{1,0:T(8,128)(2,1)S(1)} %get-tuple-element.43.field), custom_call_target="tpu_custom_call" | custom-call | flops 1000000000 | bytes 2000000 | tf_op jit(solution)/shard_map/pallas_call | solution.py:482
  19.1 0.1 collective-permute-start.3
  19.1 1.2 %shard_map.133 = (f32[256,512]{1,0:T(8,128)S(1)}, f32[128,512]{1,0:T(8,128)S(1)}, bf16[512,512]{1,0:T(8,128)(2,1)S(1)}, bf16[512,512]{1,0:T(8,128)(2,1)S(1)}) custom-call(bf16[512,512]{1,0:T(8,128)(2,1)} %wn_hbm.3, bf16[512,512]{1,0:T(8,128)(2,1)} %ws_hbm.3, bf16[256,128]{1,0:T(8,128)(2,1)S(1)} %get-tuple-element.44.spread_own, ...), custom_call_target="tpu_custom_call" | custom-call | flops 1000000000 | bytes 3000000 | tf_op jit(solution)/shard_map/pallas_call | solution.py:482
  20.4 0.0 collective-permute-done.3.message
  20.4 0.0 collective-permute-done.2.message16
  20.4 1.7 %shard_map.134.base = f32[128,512]{1,0:T(8,128)S(1)} custom-call(f32[256,512]{1,0:T(8,128)S(1)} %get-tuple-element.49.pulled, f32[128,512]{1,0:T(8,128)S(1)} %get-tuple-element.50.away, bf16[512,512]{1,0:T(8,128)(2,1)S(1)} %get-tuple-element.51.wn, bf16[512,512]{1,0:T(8,128)(2,1)S(1)} %get-tuple-element.52.ws, f32[1,512]{1,0:T(1,128)S(1)} %get-tuple-element.53.gain, ...), custom_call_target="tpu_custom_call" | custom-call | flops 603979776 | bytes 6000000 | tf_op jit(solution)/shard_map/pallas_call | solution.py:482
  22.1 0.0 collective-permute-done.4.before
  22.1 0.8 %shard_map.135 = f32[128,512]{1,0:T(8,128)} custom-call(f32[128,512]{1,0:T(8,128)S(1)} %shard_map.134.base, bf16[128,512]{1,0:T(8,128)(2,1)S(1)} %get-tuple-element.63.background, bf16[128,512]{1,0:T(8,128)(2,1)S(1)} %collective-permute-done.4.before, f32[1,512]{1,0:T(1,128)S(1)} %get-tuple-element.58.error), custom_call_target="tpu_custom_call" | custom-call | flops 1000000 | bytes 900000 | tf_op jit(solution)/shard_map/pallas_call | solution.py:482
  (2 shorter events, 0.1 us)
Async XLA Ops:
  0.0 2.7 %collective-permute-start = (f32[128,512]{1,0:T(8,128)}, f32[128,512]{1,0:T(8,128)S(1)}, u32[]{:S(2)}, u32[]{:S(2)}) collective-permute-start(f32[128,512]{1,0:T(8,128)} %bitcast.20), channel_id=1, source_target_pairs={{0,1},{1,0},{2,3},{3,2},{4,5},{5,4},{6,7},{7,6},{8,9},{9,8},{10,11... | collective-permute-start | bytes 786440 | tf_op jit(solution)/shard_map/ppermute | solution.py:537
  2.7 8.4 %collective-permute-start.1 = (bf16[144,512]{1,0:T(8,128)(2,1)S(1)}, bf16[144,512]{1,0:T(8,128)(2,1)S(1)}, u32[]{:S(2)}, u32[]{:S(2)}) collective-permute-start(bf16[144,512]{1,0:T(8,128)(2,1)S(1)} %shard_map.128.refs_5_), channel_id=1, source_target_pairs={{0,15},{1,2},{2,1},{3,4},{4,3},{5,6},{6,5},{7,8},{8,7},{9,10},{10,... | collective-permute-start | bytes 442376 | tf_op jit(solution)/shard_map/ppermute | solution.py:564
  7.6 10.9 %all-to-all-start = ((bf16[16,24,128]{2,1,0:T(8,128)(2,1)}), bf16[16,24,128]{2,1,0:T(8,128)(2,1)S(1)}, u32[]{:S(2)}, u32[]{:S(2)}) async-start(bf16[16,24,128]{2,1,0:T(8,128)(2,1)} %bitcast.9), calls=%async_computation | async-start | bytes 196608 | tf_op jit(solution)/shard_map/all_to_all | solution.py:575
  11.3 9.1 %collective-permute-start.2 = (bf16[160,512]{1,0:T(8,128)(2,1)S(1)}, bf16[160,512]{1,0:T(8,128)(2,1)S(1)}, u32[]{:S(2)}, u32[]{:S(2)}) collective-permute-start(bf16[160,512]{1,0:T(8,128)(2,1)S(1)} %get-tuple-element.55), channel_id=1, source_target_pairs={{16,0},{17,1},{18,2},{19,3},{20,4},{21,5},{22,6},{23,7},{24,8},{25... | collective-permute-start | bytes 491528 | tf_op jit(solution)/shard_map/ppermute | solution.py:535
  16.2 5.9 %collective-permute-start.4 = (bf16[128,512]{1,0:T(8,128)(2,1)S(1)}, bf16[128,512]{1,0:T(8,128)(2,1)S(1)}, u32[]{:S(2)}, u32[]{:S(2)}) collective-permute-start(bf16[128,512]{1,0:T(8,128)(2,1)S(1)} %get-tuple-element.64), channel_id=1, source_target_pairs={{16,0},{17,1},{18,2},{19,3},{20,4},{21,5},{22,6},{23,7},{24,8},{25... | collective-permute-start | bytes 393224 | tf_op jit(solution)/shard_map/ppermute | solution.py:535
  19.1 1.3 %collective-permute-start.3 = (bf16[128,128]{1,0:T(8,128)(2,1)S(1)}, bf16[128,128]{1,0:T(8,128)(2,1)S(1)}, u32[]{:S(2)}, u32[]{:S(2)}) collective-permute-start(bf16[128,128]{1,0:T(8,128)(2,1)S(1)} %get-tuple-element.59), channel_id=1, source_target_pairs={{0,1},{1,0},{2,3},{3,2},{4,5},{5,4},{6,7},{7,6},{8,9},{9,8},{10,11... | collective-permute-start | bytes 98312 | tf_op jit(solution)/shard_map/ppermute | solution.py:615
